TPU v7x, 256 devices: a whole 4x4x8 slice. The times are simulated.
256 devices in a mesh: row: 4 (over y), col: 16 (over z, core), aux: 4 (over x).
Axes of the slice: x: 4, y: 4, z: 8, core: 2. Of those that a mesh axis runs over, the one named last changes fastest.
Arguments:
- half_transformed: bfloat16 [64, 2048, 4096], P('aux', 'row', 'col'), may hold values from -0.26367188 to 0.26367188
- screen: int32 [64, 16], replicated, may hold values 0 or 1
Outputs:
- exchange_matrix: float32 [2048, 2048], P(('row', 'col', 'aux'))
All inputs are finite; a program needn't handle non-finite values.
Results may differ from a plain program's by a relative error of at most 0.0003.
Values may be sent and summed in bfloat16 or wider, within the bound.
No kernel may reach another device: no remote copies, remote signals or barrier semaphores. Data moves between devices by JAX's collectives and lax.ppermute only.
A program may use at most 128 MiB of HBM per device.

v0:
```python
import jax
import jax.numpy as jnp
from jax import lax
from jax.sharding import PartitionSpec as P

TILE = 128


def contract(left, right):
    return lax.dot_general(
        left, right, (((0, 2), (0, 2)), ((), ())), preferred_element_type=jnp.float32
    )


def body(half_transformed, screen):
    qrows, mrows, icols = half_transformed.shape
    row_index = lax.axis_index("row")
    aux_index = lax.axis_index("aux")
    tiles = mrows // TILE
    local = lax.dynamic_slice(screen, (aux_index * qrows, row_index * tiles), (qrows, tiles))
    keep = jnp.repeat(local, TILE, axis=1).astype(jnp.bfloat16)
    screened = half_transformed * keep[:, :, None]
    partial_k = contract(screened, lax.all_gather(screened, "row", axis=1, tiled=True))
    return lax.psum_scatter(partial_k, ("col", "aux"), scatter_dimension=0, tiled=True)


def solution(mesh):
    in_specs = (P("aux", "row", "col"), P())
    out_specs = P(("row", "col", "aux"), None)
    return jax.shard_map(body, mesh=mesh, in_specs=in_specs, out_specs=out_specs, check_vma=False)
```

profile of v0, /device:TPU:1, one launch (start us, length us, event | category | flops | bytes accessed | tf_op | source)
XLA Modules:
  0.0 333.9 jit_solution(5357252154829380010)
XLA Ops:
  6.5 0.0 all-gather.2.cloned.1.call-start
  6.5 0.8 dynamic-slice_convert_fusion
  7.3 0.1 copy.3
  7.4 0.1 broadcast_in_dim.4
  7.5 4.1 %broadcast_multiply_fusion = bf16[16,512,256]{2,1,0:T(8,128)(2,1)} fusion(bf16[16,512,256]{2,1,0:T(8,128)(2,1)} %param.2, bf16[16,512]{1,0:T(8,128)(2,1)S(1)} %bitcast.8), kind=kLoop, calls=%fused_computation.1 | loop fusion | flops 2097152 | bytes 8404992 | tf_op jit(solution)/shard_map/mul | solution.py:22
  11.7 0.0 all-gather.2.cloned.1.call-update
  11.7 0.0 reduce-scatter.2.cloned.1.call-start
  11.7 160.5 %all-gather.2.cloned.1.call-done = bf16[16,2048,256]{2,1,0:T(8,128)(2,1)} async-done(((bf16[16,512,256]{2,1,0:T(8,128)(2,1)}), bf16[16,2048,256]{2,1,0:T(8,128)(2,1)}) %all-gather.2.cloned.1.call-update) | async-done | bytes 16777232 | tf_op jit(solution)/shard_map/all_gather | solution.py:23
  172.2 15.0 %convolution_bitcast_fusion = f32[512,2048]{1,0:T(8,128)} fusion(bf16[16,512,256]{2,1,0:T(8,128)(2,1)} %broadcast_multiply_fusion, bf16[16,2048,256]{2,1,0:T(8,128)(2,1)} %all-gather.2.cloned.1.call-done), kind=kOutput, calls=%fused_computation | convolution fusion | flops 8589934592 | bytes 25165824 | tf_op jit(solution)/shard_map/dot_general | solution.py:10
  187.2 0.0 reduce-scatter.2.cloned.1.call-update
  187.2 139.9 %reduce-scatter.2.cloned.1.call-done = f32[8,2048]{1,0:T(8,128)} async-done(((f32[512,2048]{1,0:T(8,128)}), f32[8,2048]{1,0:T(8,128)}) %reduce-scatter.2.cloned.1.call-update) | async-done | bytes 65552 | tf_op jit(solution)/shard_map/reduce_scatter | solution.py:24
  (1 shorter events, 0.0 us)
Async XLA Ops:
  6.5 165.7 %all-gather.2.cloned.1.call-start = ((), (), s32[]{:S(2)}) async-start(), calls=%async_computation.1 | async-start | bytes 20971520 | tf_op jit(solution)/shard_map/all_gather | solution.py:23
  11.7 315.4 %reduce-scatter.2.cloned.1.call-start = ((), (), s32[]{:S(2)}) async-start(), calls=%async_computation.2 | async-start | bytes 4259840 | tf_op jit(solution)/shard_map/reduce_scatter | solution.py:24
Sparse Core Ops, SparseCore 0:
  11.8 160.4 all-gather.1
  187.3 139.7 reduce-scatter.1
where the time goes:
time: 338 us; the launch traced here: 334 us
  waiting for transfers between devices  300 us (89%)
  matrix products  15 us (4%)
  between operations  13.4 us (4%)
  other arithmetic  4.91 us (1%)
    all_gather x1, waiting for transfers between devices, body(): lax.all_gather(screened, 'row', axis=1, tiled=True)  161 us
    reduce_scatter x1, waiting for transfers between devices, body(): lax.psum_scatter(partial_k, ('col', 'aux'), scatter_dimension=0, tiled=True)  140 us
    dot_general x1, matrix products, contract(): lax.dot_general(left, right, (((0, 2), (0, 2)), ((), ())), preferred_elem...  15 us
  transfers between devices with their start and end apart: 2, of which 2 were waited for; matrix products, arithmetic and copies ran while one was open for 0% of the time, Pallas kernels for 0%

commit v1 on v0

v1 whole, which is shorter than its diff:
```python
import functools

import jax
import jax.numpy as jnp
from jax import lax
from jax.experimental import pallas as pl
from jax.experimental.pallas import tpu as pltpu
from jax.sharding import Mesh, PartitionSpec as P

TILE = 128
VMEM_LIMIT = 48 * 1024 * 1024


def shift(value, axis, step, size):
    return lax.ppermute(value, axis, [(i, (i + step) % size) for i in range(size)])


def times_transposed(left, right):
    return lax.dot_general(left, right, (((1,), (1,)), ((), ())), preferred_element_type=jnp.float32)


def diagonal_kernel(place, screen, slab, keep, give, total):
    step = pl.program_id(0)
    core, row, aux = place[0], place[1], place[2]
    rows = slab[0]
    depth = pl.num_programs(0)
    tiles = rows.shape[0] // TILE
    masked = jnp.concatenate(
        [
            rows[t * TILE : (t + 1) * TILE] * screen[aux * depth + step, row * tiles + t].astype(jnp.bfloat16)
            for t in range(tiles)
        ],
        axis=0,
    )
    product = times_transposed(masked, masked)

    @pl.when(step == 0)
    def _():
        total[...] = product.reshape(total.shape)

    @pl.when(step > 0)
    def _():
        total[...] += product.reshape(total.shape)

    @pl.when(step == depth - 1)
    def _():
        keep[...] = total[:, core].reshape(keep.shape)
        give[...] = total[:, 1 - core].reshape(give.shape)


def diagonal(place, screen, block, zs):
    depth, rows, width = block.shape
    half = jax.ShapeDtypeStruct((rows // 2, rows), jnp.float32)
    whole = pl.BlockSpec((rows // 2, rows), lambda q, *_: (0, 0))
    return pl.pallas_call(
        diagonal_kernel,
        grid_spec=pltpu.PrefetchScalarGridSpec(
            num_scalar_prefetch=2,
            grid=(depth,),
            in_specs=[pl.BlockSpec((1, rows, width), lambda q, *_: (q, 0, 0))],
            out_specs=[whole, whole],
            scratch_shapes=[pltpu.VMEM((zs, 2, rows // zs // 2, rows), jnp.float32)],
        ),
        out_shape=[half, half],
        compiler_params=pltpu.CompilerParams(vmem_limit_bytes=VMEM_LIMIT),
        cost_estimate=pl.CostEstimate(
            flops=2 * depth * rows * rows * width, bytes_accessed=2 * depth * rows * width, transcendentals=0
        ),
        name="diagonal",
    )(place, screen, block)


def pairs_kernel(products, extra, blocks, place, *refs):
    step = pl.program_id(0)
    core, aux = place[0], place[2]
    slabs, refs = refs[: 2 * blocks], refs[2 * blocks :]
    added, refs = refs[:extra], refs[extra:]
    outs, total = refs[:-1], refs[-1]
    xs = len(outs)
    cols = slabs[0].shape[1] * slabs[0].shape[2] * slabs[0].shape[3]
    size = cols // 2

    @pl.when(step == 0)
    def _():
        total[...] = jnp.zeros_like(total)

    for at, (left, right) in enumerate(products):
        product = None
        for part in range(2):
            lhs = slabs[2 * left + part][0, :, core].reshape(size, -1)
            rhs = slabs[2 * right + part][0].reshape(cols, -1)
            term = times_transposed(lhs, rhs)
            product = term if product is None else product + term
        total[:, at * cols : (at + 1) * cols] += product

    @pl.when(step == pl.num_programs(0) - 1)
    def _():
        begin = 0
        if extra:
            begin = cols
            diag = (added[0][...] + added[1][...]).reshape(-1, xs, 8, cols)
        grouped = total[...].reshape(-1, xs, 8, total.shape[1])
        zs = grouped.shape[0]
        for there in range(xs):
            piece = grouped[:, there].reshape(zs * 8, -1)
            dpiece = diag[:, there].reshape(zs * 8, -1) if extra else None
            for d in range(xs):
                @pl.when(lax.rem(aux + d, xs) == there)
                def _():
                    outs[d][:, begin:] = piece
                    if extra:
                        outs[d][:, :cols] = dpiece


def pairs(place, slabs, products, added, zs, xs):
    depth, rows, width = slabs[0][0].shape
    flat = [s.reshape(depth, zs, 2, rows // zs // 2, width) for pair in slabs for s in pair]
    spec = pl.BlockSpec((1, zs, 2, rows // zs // 2, width), lambda q, *_: (q, 0, 0, 0, 0))
    aspec = pl.BlockSpec((rows // 2, rows), lambda q, *_: (0, 0))
    cols = rows * (len(products) + (1 if added else 0))
    out = jax.ShapeDtypeStruct((rows // 2 // xs, cols), jnp.float32)
    ospec = pl.BlockSpec(out.shape, lambda q, *_: (0, 0))
    return pl.pallas_call(
        functools.partial(pairs_kernel, products, len(added), len(slabs)),
        grid_spec=pltpu.PrefetchScalarGridSpec(
            num_scalar_prefetch=1,
            grid=(depth,),
            in_specs=[spec] * len(flat) + [aspec] * len(added),
            out_specs=[ospec] * xs,
            scratch_shapes=[pltpu.VMEM((rows // 2, rows * len(products)), jnp.float32)],
        ),
        out_shape=[out] * xs,
        compiler_params=pltpu.CompilerParams(vmem_limit_bytes=VMEM_LIMIT),
        cost_estimate=pl.CostEstimate(
            flops=2 * depth * rows * rows * width * len(products),
            bytes_accessed=2 * depth * rows * width * len(flat),
            transcendentals=0,
        ),
        name="pairs",
    )(place, *flat, *added)


def reduce_aux(parts, xs):
    there = [shift(parts[d], "aux", d, xs) for d in range(1, xs)]
    return parts[0] + there[0] + there[1] + there[2]


def body(half_transformed, screen):
    qrows, mrows, icols = half_transformed.shape
    ys, zs, xs = 4, 8, 4
    quarter = qrows // ys
    row, core, aux = lax.axis_index("row"), lax.axis_index("core"), lax.axis_index("aux")
    place = jnp.stack([core, row, aux]).astype(jnp.int32)
    tiles = mrows // TILE

    local = lax.dynamic_slice(screen, (aux * qrows, row * tiles), (qrows, tiles))
    keep = jnp.repeat(local, TILE, axis=1).astype(jnp.bfloat16)

    def slab(step):
        first = lax.rem(row + step, ys) * quarter
        part = lax.dynamic_slice(half_transformed, (first, 0, 0), (quarter, mrows, icols))
        return part * lax.dynamic_slice(keep, (first, 0), (quarter, mrows))[:, :, None]

    def sibling(value):
        return lax.ppermute(value, "core", [(0, 1), (1, 0)])

    below = shift(slab(1), "row", 1, ys)
    above = shift(slab(3), "row", -1, ys)
    mine = slab(0)
    kept, given = diagonal(place, screen, half_transformed, zs)
    got = sibling(given)
    mine2 = sibling(mine)
    far, below, above = lax.optimization_barrier((slab(2), below, above))
    across = shift(far, "row", 2, ys)
    below2, above2 = sibling(below), sibling(above)

    early = pairs(
        place, [(mine, mine2), (above, above2), (below, below2)], ((0, 1), (1, 2), (0, 2)), (kept, got), zs, xs
    )
    early = reduce_aux(early, xs)
    across2 = sibling(across)
    late = pairs(
        place,
        [(across, across2), (below, below2), (mine, mine2), (above, above2)],
        ((0, 1), (0, 2), (0, 3)),
        (),
        zs,
        xs,
    )
    late = reduce_aux(late, xs)

    n = mrows
    early_up = shift(early[:, n : 3 * n], "row", 1, ys)
    early_down = shift(early[:, 2 * n :], "row", -1, ys)
    late_up = shift(late[:, 2 * n :], "row", 1, ys)
    late_down = shift(late[:, :n], "row", -1, ys)
    late_far = shift(late, "row", 2, ys)
    plus = early[:, n : 2 * n] + late_far[:, :n]
    minus = early[:, 3 * n :] + late_far[:, 2 * n :]
    twice = early_up[:, n:] + late_far[:, n : 2 * n]
    turned_minus = early_up[:, :n] + late_down
    turned_plus = early_down[:, n:] + late_up
    turned_twice = early_down[:, :n] + late[:, n : 2 * n]

    plain = jnp.concatenate([early[:, :n], plus, twice, minus], axis=1).reshape(zs, 8, 4 * n)
    turned = jnp.stack([turned_plus, turned_twice, turned_minus])
    turned = turned.reshape(3, zs * 8, zs, 2 * xs, 8).transpose(2, 4, 3, 0, 1).reshape(zs, 8, 2 * xs * 3 * zs * 8)
    both = lax.all_to_all(jnp.concatenate([plain, turned], axis=2), "z", 0, 0, tiled=True)
    both = jnp.sum(both, axis=0)
    plain, turned = both[:, : 4 * n], both[:, 4 * n :]

    turned = turned.reshape(8, 2, xs * 3 * zs * 8)
    own = lax.dynamic_index_in_dim(turned, core, 1, keepdims=False)
    other = sibling(lax.dynamic_index_in_dim(turned, 1 - core, 1, keepdims=False))
    pieces = jnp.stack([jnp.where(core == 0, own, other), jnp.where(core == 0, other, own)])
    pieces = pieces.reshape(2, 8, xs, 3 * zs * 8).transpose(2, 0, 1, 3)
    pieces = lax.all_to_all(pieces, "aux", 0, 0, tiled=True)
    pieces = pieces.reshape(xs, 2, 8, 3, zs, 8).transpose(2, 3, 4, 1, 0, 5).reshape(8, 3 * n)
    out = plain + jnp.concatenate([jnp.zeros((8, n), jnp.float32), pieces], axis=1)
    return lax.dynamic_slice(jnp.concatenate([out, out], axis=1), (0, lax.rem(ys - row, ys) * n), (8, 4 * n))


def solution(mesh):
    rows, cols, aux = mesh.devices.shape
    split = Mesh(mesh.devices.reshape(rows, cols // 2, 2, aux), ("row", "z", "core", "aux"))
    in_specs = (P("aux", "row", ("z", "core")), P())
    out_specs = P(("row", "z", "core", "aux"), None)
    return jax.shard_map(body, mesh=split, in_specs=in_specs, out_specs=out_specs, check_vma=False)
```

time: 338 us -> 182 us (0.54)
  waiting for transfers between devices: 300 us -> 105 us
  starting transfers between devices: 0.04 us -> 40.7 us
  Pallas kernels: 0 us -> 19.4 us
  matrix products: 15 us -> 0 us
  between operations: 13.4 us -> 0.29 us
  local copies, waits for them, and re-layouts: 0.19 us -> 7.75 us
    all_gather x1 -> x0, waiting for transfers between devices: 161 us -> none  [body(): lax.all_gather(screened, 'row', axis=1, tiled=True)]
    reduce_scatter x1 -> x0, waiting for transfers between devices: 140 us -> none  [body(): lax.psum_scatter(partial_k, ('col', 'aux'), scatter_dimension=0, tiled=True)]
    ppermute x0 -> x20, waiting for transfers between devices: none -> 74.6 us  [the longest x14 73.8 us: shift(): lax.ppermute(value, axis, [(i, (i + step) % size) for i in range(size)])]
    all_to_all x0 -> x2, waiting for transfers between devices: none -> 30.8 us  [the longest x1 26.4 us: body(): lax.all_to_all(jnp.concatenate([plain, turned], axis=2), 'z', 0, 0, tiled...]
    ppermute x0 -> x20, starting transfers between devices: none -> 29.2 us  [the longest x14 22.9 us: shift(): lax.ppermute(value, axis, [(i, (i + step) % size) for i in range(size)])]
    pallas_call x0 -> x3, Pallas kernels: none -> 19.4 us  [the longest x2 11 us: pairs(): pl.pallas_call(functools.partial(pairs_kernel, products, len(added), len(...]
    dot_general x1 -> x0, matrix products: 15 us -> none  [contract(): lax.dot_general(left, right, (((0, 2), (0, 2)), ((), ())), preferred_elem...]
    all_to_all x0 -> x2, starting transfers between devices: none -> 11.5 us  [the longest x1 8.19 us: body(): lax.all_to_all(jnp.concatenate([plain, turned], axis=2), 'z', 0, 0, tiled...]
  transfers between devices with their start and end apart: 2 -> 22, of which waited for: 2 -> 12; matrix products, arithmetic and copies ran while one was open for 0% -> 0% of each run, Pallas kernels for 0% -> 11%
where the time goes in v1:
time: 182 us; the launch traced here: 181 us
  waiting for transfers between devices  105 us (58%)
  starting transfers between devices  40.7 us (22%)
  Pallas kernels  19.4 us (11%)
  local copies, waits for them, and re-layouts  7.75 us (4%)
  other arithmetic  7.6 us (4%)
    ppermute x14, waiting for transfers between devices, shift(): lax.ppermute(value, axis, [(i, (i + step) % size) for i in range(size)])  73.8 us
    all_to_all x1, waiting for transfers between devices, body(): lax.all_to_all(jnp.concatenate([plain, turned], axis=2), 'z', 0, 0, tiled...  26.4 us
    ppermute x14, starting transfers between devices, shift(): lax.ppermute(value, axis, [(i, (i + step) % size) for i in range(size)])  22.9 us
    pallas_call x2, Pallas kernels, pairs(): pl.pallas_call(functools.partial(pairs_kernel, products, len(added), len(...  11 us
    pallas_call x1, Pallas kernels, diagonal(): pl.pallas_call(diagonal_kernel, grid_spec=pltpu.PrefetchScalarGridSpec(nu...  8.38 us
    all_to_all x1, starting transfers between devices, body(): lax.all_to_all(jnp.concatenate([plain, turned], axis=2), 'z', 0, 0, tiled...  8.19 us
    ppermute x6, starting transfers between devices, sibling(): return lax.ppermute(value, 'core', [(0, 1), (1, 0)])  6.38 us
    mul x1, other arithmetic, slab(): part * lax.dynamic_slice(keep, (first, 0), (quarter, mrows))[:, :, None]  4.52 us
  transfers between devices with their start and end apart: 22, of which 12 were waited for; matrix products, arithmetic and copies ran while one was open for 0% of the time, Pallas kernels for 11%

profile of v1, /device:TPU:1, one launch (start us, length us, event | category | flops | bytes accessed | tf_op | source)
XLA Modules:
  0.0 181.2 jit_solution(4101553848715011938)
XLA Ops:
  0.0 0.8 dynamic-slice_convert_fusion
  0.8 0.1 copy.19
  0.9 0.1 broadcast_in_dim.2
  1.0 0.0 copy-start.5
  1.0 4.5 %dynamic-slice_multiply_fusion.3 = (bf16[4,512,256]{2,1,0:T(8,128)(2,1)S(1)}, bf16[4,512,256]{2,1,0:T(8,128)(2,1)S(1)}, bf16[4,512,256]{2,1,0:T(8,128)(2,1)}, bf16[4,512,256]{2,1,0:T(8,128)(2,1)S(1)}) fusion(bf16[16,512,256]{2,1,0:T(8,128)(2,1)} %slab.1, s32[]{:T(128)S(6)} %select_n.44, bf16[4,512]{1,0:T(4,128)(2,1)S(1)} %get-tuple-element.47, ...), kind=kLoop, calls=%fused_computation.3 | loop fusion | flops 2097152 | bytes 8405008 | tf_op jit(solution)/shard_map/mul | solution.py:162
  5.6 2.1 %collective-permute-start.1 = (bf16[4,512,256]{2,1,0:T(8,128)(2,1)S(1)}, bf16[4,512,256]{2,1,0:T(8,128)(2,1)S(1)}, u32[]{:S(2)}, u32[]{:S(2)}) collective-permute-start(bf16[4,512,256]{2,1,0:T(8,128)(2,1)S(1)} %get-tuple-element.32), channel_id=1, source_target_pairs={{0,64},{64,128},{128,192},{192,0},{1,65},{65,129},{129,193},{193,1... | collective-permute-start | bytes 3145736 | tf_op jit(solution)/shard_map/ppermute | solution.py:15
  7.7 1.5 collective-permute-start.2
  9.2 20.8 %collective-permute-done.1 = bf16[4,512,256]{2,1,0:T(8,128)(2,1)S(1)} collective-permute-done((bf16[4,512,256]{2,1,0:T(8,128)(2,1)S(1)}, bf16[4,512,256]{2,1,0:T(8,128)(2,1)S(1)}, u32[]{:S(2)}, u32[]{:S(2)}) %collective-permute-start.1) | collective-permute-done | bytes 1048608 | tf_op jit(solution)/shard_map/ppermute | solution.py:15
  30.0 1.3 collective-permute-done.2
  31.2 2.9 %collective-permute-start.9 = (bf16[4,512,256]{2,1,0:T(8,128)(2,1)}, bf16[4,512,256]{2,1,0:T(8,128)(2,1)}, u32[]{:S(2)}, u32[]{:S(2)}) collective-permute-start(bf16[4,512,256]{2,1,0:T(8,128)(2,1)} %get-tuple-element.26), channel_id=1, source_target_pairs={{0,128},{64,192},{128,0},{192,64},{1,129},{65,193},{129,1},{193,65... | collective-permute-start | bytes 3145736 | tf_op jit(solution)/shard_map/ppermute | solution.py:15
  34.1 2.1 %collective-permute-start = (bf16[4,512,256]{2,1,0:T(8,128)(2,1)S(1)}, bf16[4,512,256]{2,1,0:T(8,128)(2,1)S(1)}, u32[]{:S(2)}, u32[]{:S(2)}) collective-permute-start(bf16[4,512,256]{2,1,0:T(8,128)(2,1)S(1)} %get-tuple-element.31), channel_id=1, source_target_pairs={{0,4},{4,0},{1,5},{5,1},{2,6},{6,2},{3,7},{7,3},{8,12},{12,8},{9,1... | collective-permute-start | bytes 3145736 | tf_op jit(solution)/shard_map/ppermute | solution.py:165
  36.3 0.0 collective-permute-start.4
  36.3 0.5 collective-permute-start.3
  36.8 0.1 copy.20.screen
  36.9 0.1 pad_add_fusion.place
  36.9 2.2 %copy-done.1 = bf16[16,512,256]{2,1,0:T(8,128)(2,1)S(1)} copy-done((bf16[16,512,256]{2,1,0:T(8,128)(2,1)S(1)}, bf16[16,512,256]{2,1,0:T(8,128)(2,1)}, u32[]{:S(2)}) %copy-start.1) | copy-done | bytes 4194328
  39.1 8.4 %diagonal.1 = (f32[256,512]{1,0:T(8,128)S(1)}, f32[256,512]{1,0:T(8,128)S(1)}) custom-call(s32[3]{0:T(128)S(1)} %pad_add_fusion.place, s32[64,16]{1,0:T(8,128)S(1)} %copy.20.screen, bf16[16,512,256]{2,1,0:T(8,128)(2,1)S(1)} %copy-done.1), custom_call_target="tpu_custom_call" | custom-call | flops 2147483648 | bytes 4194304 | tf_op jit(solution)/shard_map/diagonal/pallas_call | solution.py:55
  47.5 0.1 collective-permute-start.5
  47.6 8.0 %collective-permute-done.9 = bf16[4,512,256]{2,1,0:T(8,128)(2,1)} collective-permute-done((bf16[4,512,256]{2,1,0:T(8,128)(2,1)}, bf16[4,512,256]{2,1,0:T(8,128)(2,1)}, u32[]{:S(2)}, u32[]{:S(2)}) %collective-permute-start.9) | collective-permute-done | bytes 1048608 | tf_op jit(solution)/shard_map/ppermute | solution.py:15
  55.6 3.0 %collective-permute-start.10 = (bf16[4,512,256]{2,1,0:T(8,128)(2,1)}, bf16[4,512,256]{2,1,0:T(8,128)(2,1)S(1)}, u32[]{:S(2)}, u32[]{:S(2)}) collective-permute-start(bf16[4,512,256]{2,1,0:T(8,128)(2,1)} %collective-permute-done.9), channel_id=1, source_target_pairs={{0,4},{4,0},{1,5},{5,1},{2,6},{6,2},{3,7},{7,3},{8,12},{12,8},{9,1... | collective-permute-start | bytes 3145736 | tf_op jit(solution)/shard_map/ppermute | solution.py:165
  58.6 0.0 collective-permute-done.5.refs_7_
  58.7 5.4 %pairs.2 = (f32[64,2048]{1,0:T(8,128)S(1)}, f32[64,2048]{1,0:T(8,128)S(1)}, f32[64,2048]{1,0:T(8,128)S(1)}, f32[64,2048]{1,0:T(8,128)S(1)}) custom-call(s32[3]{0:T(128)S(1)} %pad_add_fusion.place, bf16[4,8,2,32,256]{4,3,2,1,0:T(8,128)(2,1)S(1)} %bitcast.33, bf16[4,8,2,32,256]{4,3,2,1,0:T(8,128)(2,1)S(1)} %bitcast.37, ...), custom_call_target="tpu_custom_call" | custom-call | flops 1610612736 | bytes 6291456 | tf_op jit(solution)/shard_map/pairs/pallas_call | solution.py:123
  64.1 3.1 %collective-permute-start.8 = (f32[64,2048]{1,0:T(8,128)S(1)}, f32[64,2048]{1,0:T(8,128)S(1)}, u32[]{:S(2)}, u32[]{:S(2)}) collective-permute-start(f32[64,2048]{1,0:T(8,128)S(1)} %get-tuple-element.25), channel_id=1, source_target_pairs={{0,3},{1,0},{2,1},{3,2},{4,7},{5,4},{6,5},{7,6},{8,11},{9,8},{10,9... | collective-permute-start | bytes 1572872 | tf_op jit(solution)/shard_map/ppermute | solution.py:15
  67.1 0.5 collective-permute-start.7
  67.7 0.6 collective-permute-start.6
  68.3 1.2 copy-done.3
  69.5 5.7 %pairs.3 = (f32[64,1536]{1,0:T(8,128)S(1)}, f32[64,1536]{1,0:T(8,128)S(1)}, f32[64,1536]{1,0:T(8,128)S(1)}, f32[64,1536]{1,0:T(8,128)S(1)}) custom-call(s32[3]{0:T(128)S(1)} %pad_add_fusion.place, bf16[4,8,2,32,256]{4,3,2,1,0:T(8,128)(2,1)} %bitcast.9.refs_0_, bf16[4,8,2,32,256]{4,3,2,1,0:T(8,128)(2,1)S(1)} %bitcast.39, ...), custom_call_target="tpu_custom_call" | custom-call | flops 1610612736 | bytes 8388608 | tf_op jit(solution)/shard_map/pairs/pallas_call | solution.py:123
  75.2 2.1 %collective-permute-start.13 = (f32[64,1536]{1,0:T(8,128)S(1)}, f32[64,1536]{1,0:T(8,128)S(1)}, u32[]{:S(2)}, u32[]{:S(2)}) collective-permute-start(f32[64,1536]{1,0:T(8,128)S(1)} %get-tuple-element.30), channel_id=1, source_target_pairs={{0,3},{1,0},{2,1},{3,2},{4,7},{5,4},{6,5},{7,6},{8,11},{9,8},{10,9... | collective-permute-start | bytes 1179656 | tf_op jit(solution)/shard_map/ppermute | solution.py:15
  77.3 1.2 collective-permute-start.12
  78.6 11.0 %collective-permute-done.8 = f32[64,2048]{1,0:T(8,128)S(1)} collective-permute-done((f32[64,2048]{1,0:T(8,128)S(1)}, f32[64,2048]{1,0:T(8,128)S(1)}, u32[]{:S(2)}, u32[]{:S(2)}) %collective-permute-start.8) | collective-permute-done | bytes 524320 | tf_op jit(solution)/shard_map/ppermute | solution.py:15
  89.6 0.0 collective-permute-start.11
  89.6 4.7 %collective-permute-done.6 = f32[64,2048]{1,0:T(8,128)S(1)} collective-permute-done((f32[64,2048]{1,0:T(8,128)S(1)}, f32[64,2048]{1,0:T(8,128)S(1)}, u32[]{:S(2)}, u32[]{:S(2)}) %collective-permute-start.6) | collective-permute-done | bytes 524320 | tf_op jit(solution)/shard_map/ppermute | solution.py:15
  94.3 0.2 add_add_fusion
  94.5 2.7 %collective-permute-start.16 = (f32[64,1024]{1,0:T(8,128)S(1)}, f32[64,1024]{1,0:T(8,128)S(1)}, u32[]{:S(2)}, u32[]{:S(2)}) collective-permute-start(f32[64,1024]{1,0:T(8,128)S(1)} %get-tuple-element.38), channel_id=1, source_target_pairs={{0,192},{64,0},{128,64},{192,128},{1,193},{65,1},{129,65},{193,129... | collective-permute-start | bytes 786440 | tf_op jit(solution)/shard_map/ppermute | solution.py:15
  97.2 9.2 %collective-permute-done.13 = f32[64,1536]{1,0:T(8,128)S(1)} collective-permute-done((f32[64,1536]{1,0:T(8,128)S(1)}, f32[64,1536]{1,0:T(8,128)S(1)}, u32[]{:S(2)}, u32[]{:S(2)}) %collective-permute-start.13) | collective-permute-done | bytes 393248 | tf_op jit(solution)/shard_map/ppermute | solution.py:15
  106.4 4.1 %collective-permute-done.11 = f32[64,1536]{1,0:T(8,128)S(1)} collective-permute-done((f32[64,1536]{1,0:T(8,128)S(1)}, f32[64,1536]{1,0:T(8,128)S(1)}, u32[]{:S(2)}, u32[]{:S(2)}) %collective-permute-start.11) | collective-permute-done | bytes 393248 | tf_op jit(solution)/shard_map/ppermute | solution.py:15
  110.5 0.1 add_add_fusion.1
  110.6 2.4 %collective-permute-start.14 = (f32[64,1536]{1,0:T(8,128)S(1)}, f32[64,1536]{1,0:T(8,128)S(1)}, u32[]{:S(2)}, u32[]{:S(2)}) collective-permute-start(f32[64,1536]{1,0:T(8,128)S(1)} %add_add_fusion.1), channel_id=1, source_target_pairs={{0,128},{64,192},{128,0},{192,64},{1,129},{65,193},{129,1},{193,65... | collective-permute-start | bytes 1179656 | tf_op jit(solution)/shard_map/ppermute | solution.py:15
  113.1 0.9 collective-permute-start.17
  114.0 0.1 collective-permute-start.15
  114.1 2.6 %collective-permute-start.18 = (f32[64,512]{1,0:T(8,128)S(1)}, f32[64,512]{1,0:T(8,128)S(1)}, u32[]{:S(2)}, u32[]{:S(2)}) collective-permute-start(f32[64,512]{1,0:T(8,128)S(1)} %get-tuple-element.42), channel_id=1, source_target_pairs={{0,192},{64,0},{128,64},{192,128},{1,193},{65,1},{129,65},{193,129... | collective-permute-start | bytes 393224 | tf_op jit(solution)/shard_map/ppermute | solution.py:15
  116.7 0.1 copy.22
  116.8 9.2 %collective-permute-done.17 = f32[64,512]{1,0:T(8,128)S(1)} collective-permute-done((f32[64,512]{1,0:T(8,128)S(1)}, f32[64,512]{1,0:T(8,128)S(1)}, u32[]{:S(2)}, u32[]{:S(2)}) %collective-permute-start.17) | collective-permute-done | bytes 131104 | tf_op jit(solution)/shard_map/ppermute | solution.py:15
  126.1 0.1 copy.21
  126.2 5.5 %collective-permute-done.15 = f32[64,1024]{1,0:T(8,128)S(1)} collective-permute-done((f32[64,1024]{1,0:T(8,128)S(1)}, f32[64,1024]{1,0:T(8,128)S(1)}, u32[]{:S(2)}, u32[]{:S(2)}) %collective-permute-start.15) | collective-permute-done | bytes 262176 | tf_op jit(solution)/shard_map/ppermute | solution.py:15
  131.7 0.1 slice_add_fusion.5
  131.8 0.1 copy.23
  131.9 0.1 maximum_bitcast_fusion
  132.0 0.5 copy.24
  132.5 0.6 reshape.72
  133.2 1.0 pad_maximum_fusion
  134.2 8.2 %all-to-all-start = ((f32[8,8,3584]{2,1,0:T(8,128)}), f32[8,8,3584]{2,1,0:T(8,128)S(1)}, u32[]{:S(2)}, u32[]{:S(2)}) async-start(f32[8,8,3584]{2,1,0:T(8,128)} %pad_maximum_fusion), calls=%async_computation | async-start | bytes 1835008 | tf_op jit(solution)/shard_map/all_to_all | solution.py:208
  142.4 26.4 %all-to-all-done = f32[8,8,3584]{2,1,0:T(8,128)S(1)} async-done(((f32[8,8,3584]{2,1,0:T(8,128)}), f32[8,8,3584]{2,1,0:T(8,128)S(1)}, u32[]{:S(2)}, u32[]{:S(2)}) %all-to-all-start) | async-done | bytes 917536 | tf_op jit(solution)/shard_map/all_to_all | solution.py:208
  168.9 0.6 collective-permute-start.19
  169.4 0.8 collective-permute-done.19
  170.3 0.1 stack.42
  170.4 0.1 stack.41
  170.5 0.6 copy.25
  171.1 3.3 %all-to-all-start.1 = ((f32[4,2,8,192]{3,2,1,0:T(8,128)}), f32[4,2,8,192]{3,2,1,0:T(8,128)S(1)}, u32[]{:S(2)}, u32[]{:S(2)}) async-start(f32[4,2,8,192]{3,2,1,0:T(8,128)} %copy.25), calls=%async_computation.1 | async-start | bytes 131072 | tf_op jit(solution)/shard_map/all_to_all | solution.py:217
  174.4 4.4 %all-to-all-done.1 = f32[4,2,8,192]{3,2,1,0:T(8,128)S(1)} async-done(((f32[4,2,8,192]{3,2,1,0:T(8,128)}), f32[4,2,8,192]{3,2,1,0:T(8,128)S(1)}, u32[]{:S(2)}, u32[]{:S(2)}) %all-to-all-start.1) | async-done | bytes 49184 | tf_op jit(solution)/shard_map/all_to_all | solution.py:217
  178.9 0.3 reshape.74
  179.2 0.5 copy.26
  179.7 0.8 reshape.75
  180.5 0.7 fusion
  (30 shorter events, 0.3 us)
Async XLA Ops:
  1.0 35.8 %copy-start.5 = (s32[64,16]{0,1:T(8,128)S(1)}, s32[64,16]{0,1:T(8,128)}, u32[]{:S(2)}) copy-start(s32[64,16]{0,1:T(8,128)} %param.3) | copy-start | bytes 12292
  5.5 58.5 %copy-start = (bf16[4,512,256]{2,1,0:T(8,128)(2,1)}, bf16[4,512,256]{2,1,0:T(8,128)(2,1)S(1)}, u32[]{:S(2)}) copy-start(bf16[4,512,256]{2,1,0:T(8,128)(2,1)S(1)} %get-tuple-element.31) | copy-start | bytes 3145732
  5.6 24.4 %collective-permute-start.1 = (bf16[4,512,256]{2,1,0:T(8,128)(2,1)S(1)}, bf16[4,512,256]{2,1,0:T(8,128)(2,1)S(1)}, u32[]{:S(2)}, u32[]{:S(2)}) collective-permute-start(bf16[4,512,256]{2,1,0:T(8,128)(2,1)S(1)} %get-tuple-element.32), channel_id=1, source_target_pairs={{0,64},{64,128},{128,192},{192,0},{1,65},{65,129},{129,193},{193,1... | collective-permute-start | bytes 3145736 | tf_op jit(solution)/shard_map/ppermute | solution.py:15
  7.7 23.6 %collective-permute-start.2 = (bf16[4,512,256]{2,1,0:T(8,128)(2,1)S(1)}, bf16[4,512,256]{2,1,0:T(8,128)(2,1)}, u32[]{:S(2)}, u32[]{:S(2)}) collective-permute-start(bf16[4,512,256]{2,1,0:T(8,128)(2,1)S(1)} %get-tuple-element.34), channel_id=1, source_target_pairs={{0,192},{64,0},{128,64},{192,128},{1,193},{65,1},{129,65},{193,129... | collective-permute-start | bytes 3145736 | tf_op jit(solution)/shard_map/ppermute | solution.py:15
  30.0 28.7 %copy-start.2 = (bf16[4,512,256]{2,1,0:T(8,128)(2,1)}, bf16[4,512,256]{2,1,0:T(8,128)(2,1)S(1)}, u32[]{:S(2)}) copy-start(bf16[4,512,256]{2,1,0:T(8,128)(2,1)S(1)} %collective-permute-done.1) | copy-start | bytes 3145732
  31.2 24.3 %collective-permute-start.9 = (bf16[4,512,256]{2,1,0:T(8,128)(2,1)}, bf16[4,512,256]{2,1,0:T(8,128)(2,1)}, u32[]{:S(2)}, u32[]{:S(2)}) collective-permute-start(bf16[4,512,256]{2,1,0:T(8,128)(2,1)} %get-tuple-element.26), channel_id=1, source_target_pairs={{0,128},{64,192},{128,0},{192,64},{1,129},{65,193},{129,1},{193,65... | collective-permute-start | bytes 3145736 | tf_op jit(solution)/shard_map/ppermute | solution.py:15
  34.1 24.5 %collective-permute-start = (bf16[4,512,256]{2,1,0:T(8,128)(2,1)S(1)}, bf16[4,512,256]{2,1,0:T(8,128)(2,1)S(1)}, u32[]{:S(2)}, u32[]{:S(2)}) collective-permute-start(bf16[4,512,256]{2,1,0:T(8,128)(2,1)S(1)} %get-tuple-element.31), channel_id=1, source_target_pairs={{0,4},{4,0},{1,5},{5,1},{2,6},{6,2},{3,7},{7,3},{8,12},{12,8},{9,1... | collective-permute-start | bytes 3145736 | tf_op jit(solution)/shard_map/ppermute | solution.py:165
  36.3 22.4 %collective-permute-start.4 = (bf16[4,512,256]{2,1,0:T(8,128)(2,1)S(1)}, bf16[4,512,256]{2,1,0:T(8,128)(2,1)}, u32[]{:S(2)}, u32[]{:S(2)}) collective-permute-start(bf16[4,512,256]{2,1,0:T(8,128)(2,1)S(1)} %collective-permute-done.1), channel_id=1, source_target_pairs={{0,4},{4,0},{1,5},{5,1},{2,6},{6,2},{3,7},{7,3},{8,12},{12,8},{9,1... | collective-permute-start | bytes 3145736 | tf_op jit(solution)/shard_map/ppermute | solution.py:165
  36.3 22.4 %collective-permute-start.3 = (bf16[4,512,256]{2,1,0:T(8,128)(2,1)}, bf16[4,512,256]{2,1,0:T(8,128)(2,1)}, u32[]{:S(2)}, u32[]{:S(2)}) collective-permute-start(bf16[4,512,256]{2,1,0:T(8,128)(2,1)} %collective-permute-done.2), channel_id=1, source_target_pairs={{0,4},{4,0},{1,5},{5,1},{2,6},{6,2},{3,7},{7,3},{8,12},{12,8},{9,1... | collective-permute-start | bytes 3145736 | tf_op jit(solution)/shard_map/ppermute | solution.py:165
  36.9 2.2 %copy-start.1 = (bf16[16,512,256]{2,1,0:T(8,128)(2,1)S(1)}, bf16[16,512,256]{2,1,0:T(8,128)(2,1)}, u32[]{:S(2)}) copy-start(bf16[16,512,256]{2,1,0:T(8,128)(2,1)} %slab.1) | copy-start | bytes 12582916
  47.5 11.1 %collective-permute-start.5 = (f32[256,512]{1,0:T(8,128)S(1)}, f32[256,512]{1,0:T(8,128)S(1)}, u32[]{:S(2)}, u32[]{:S(2)}) collective-permute-start(f32[256,512]{1,0:T(8,128)S(1)} %get-tuple-element.21), channel_id=1, source_target_pairs={{0,4},{4,0},{1,5},{5,1},{2,6},{6,2},{3,7},{7,3},{8,12},{12,8},{9,1... | collective-permute-start | bytes 1572872 | tf_op jit(solution)/shard_map/ppermute | solution.py:165
  55.6 12.7 %collective-permute-start.10 = (bf16[4,512,256]{2,1,0:T(8,128)(2,1)}, bf16[4,512,256]{2,1,0:T(8,128)(2,1)S(1)}, u32[]{:S(2)}, u32[]{:S(2)}) collective-permute-start(bf16[4,512,256]{2,1,0:T(8,128)(2,1)} %collective-permute-done.9), channel_id=1, source_target_pairs={{0,4},{4,0},{1,5},{5,1},{2,6},{6,2},{3,7},{7,3},{8,12},{12,8},{9,1... | collective-permute-start | bytes 3145736 | tf_op jit(solution)/shard_map/ppermute | solution.py:165
  58.6 9.6 %copy-start.4 = (bf16[4,512,256]{2,1,0:T(8,128)(2,1)}, bf16[4,512,256]{2,1,0:T(8,128)(2,1)S(1)}, u32[]{:S(2)}) copy-start(bf16[4,512,256]{2,1,0:T(8,128)(2,1)S(1)} %collective-permute-done) | copy-start | bytes 3145732
  64.1 25.5 %collective-permute-start.8 = (f32[64,2048]{1,0:T(8,128)S(1)}, f32[64,2048]{1,0:T(8,128)S(1)}, u32[]{:S(2)}, u32[]{:S(2)}) collective-permute-start(f32[64,2048]{1,0:T(8,128)S(1)} %get-tuple-element.25), channel_id=1, source_target_pairs={{0,3},{1,0},{2,1},{3,2},{4,7},{5,4},{6,5},{7,6},{8,11},{9,8},{10,9... | collective-permute-start | bytes 1572872 | tf_op jit(solution)/shard_map/ppermute | solution.py:15
  67.1 22.4 %collective-permute-start.7 = (f32[64,2048]{1,0:T(8,128)S(1)}, f32[64,2048]{1,0:T(8,128)S(1)}, u32[]{:S(2)}, u32[]{:S(2)}) collective-permute-start(f32[64,2048]{1,0:T(8,128)S(1)} %get-tuple-element.24), channel_id=1, source_target_pairs={{0,2},{1,3},{2,0},{3,1},{4,6},{5,7},{6,4},{7,5},{8,10},{9,11},{10,... | collective-permute-start | bytes 1572872 | tf_op jit(solution)/shard_map/ppermute | solution.py:15
  67.7 26.6 %collective-permute-start.6 = (f32[64,2048]{1,0:T(8,128)S(1)}, f32[64,2048]{1,0:T(8,128)S(1)}, u32[]{:S(2)}, u32[]{:S(2)}) collective-permute-start(f32[64,2048]{1,0:T(8,128)S(1)} %get-tuple-element.23), channel_id=1, source_target_pairs={{0,1},{1,2},{2,3},{3,0},{4,5},{5,6},{6,7},{7,4},{8,9},{9,10},{10,1... | collective-permute-start | bytes 1572872 | tf_op jit(solution)/shard_map/ppermute | solution.py:15
  68.3 1.2 copy-start.3
  75.2 31.3 %collective-permute-start.13 = (f32[64,1536]{1,0:T(8,128)S(1)}, f32[64,1536]{1,0:T(8,128)S(1)}, u32[]{:S(2)}, u32[]{:S(2)}) collective-permute-start(f32[64,1536]{1,0:T(8,128)S(1)} %get-tuple-element.30), channel_id=1, source_target_pairs={{0,3},{1,0},{2,1},{3,2},{4,7},{5,4},{6,5},{7,6},{8,11},{9,8},{10,9... | collective-permute-start | bytes 1179656 | tf_op jit(solution)/shard_map/ppermute | solution.py:15
  77.3 29.1 %collective-permute-start.12 = (f32[64,1536]{1,0:T(8,128)S(1)}, f32[64,1536]{1,0:T(8,128)S(1)}, u32[]{:S(2)}, u32[]{:S(2)}) collective-permute-start(f32[64,1536]{1,0:T(8,128)S(1)} %get-tuple-element.29), channel_id=1, source_target_pairs={{0,2},{1,3},{2,0},{3,1},{4,6},{5,7},{6,4},{7,5},{8,10},{9,11},{10,... | collective-permute-start | bytes 1179656 | tf_op jit(solution)/shard_map/ppermute | solution.py:15
  89.6 21.0 %collective-permute-start.11 = (f32[64,1536]{1,0:T(8,128)S(1)}, f32[64,1536]{1,0:T(8,128)S(1)}, u32[]{:S(2)}, u32[]{:S(2)}) collective-permute-start(f32[64,1536]{1,0:T(8,128)S(1)} %get-tuple-element.28), channel_id=1, source_target_pairs={{0,1},{1,2},{2,3},{3,0},{4,5},{5,6},{6,7},{7,4},{8,9},{9,10},{10,1... | collective-permute-start | bytes 1179656 | tf_op jit(solution)/shard_map/ppermute | solution.py:15
  94.5 18.6 %collective-permute-start.16 = (f32[64,1024]{1,0:T(8,128)S(1)}, f32[64,1024]{1,0:T(8,128)S(1)}, u32[]{:S(2)}, u32[]{:S(2)}) collective-permute-start(f32[64,1024]{1,0:T(8,128)S(1)} %get-tuple-element.38), channel_id=1, source_target_pairs={{0,192},{64,0},{128,64},{192,128},{1,193},{65,1},{129,65},{193,129... | collective-permute-start | bytes 786440 | tf_op jit(solution)/shard_map/ppermute | solution.py:15
  110.6 21.1 %collective-permute-start.14 = (f32[64,1536]{1,0:T(8,128)S(1)}, f32[64,1536]{1,0:T(8,128)S(1)}, u32[]{:S(2)}, u32[]{:S(2)}) collective-permute-start(f32[64,1536]{1,0:T(8,128)S(1)} %add_add_fusion.1), channel_id=1, source_target_pairs={{0,128},{64,192},{128,0},{192,64},{1,129},{65,193},{129,1},{193,65... | collective-permute-start | bytes 1179656 | tf_op jit(solution)/shard_map/ppermute | solution.py:15
  113.1 12.9 %collective-permute-start.17 = (f32[64,512]{1,0:T(8,128)S(1)}, f32[64,512]{1,0:T(8,128)S(1)}, u32[]{:S(2)}, u32[]{:S(2)}) collective-permute-start(f32[64,512]{1,0:T(8,128)S(1)} %get-tuple-element.41), channel_id=1, source_target_pairs={{0,64},{64,128},{128,192},{192,0},{1,65},{65,129},{129,193},{193,1... | collective-permute-start | bytes 393224 | tf_op jit(solution)/shard_map/ppermute | solution.py:15
  114.0 17.6 %collective-permute-start.15 = (f32[64,1024]{1,0:T(8,128)S(1)}, f32[64,1024]{1,0:T(8,128)S(1)}, u32[]{:S(2)}, u32[]{:S(2)}) collective-permute-start(f32[64,1024]{1,0:T(8,128)S(1)} %get-tuple-element.39), channel_id=1, source_target_pairs={{0,64},{64,128},{128,192},{192,0},{1,65},{65,129},{129,193},{193,1... | collective-permute-start | bytes 786440 | tf_op jit(solution)/shard_map/ppermute | solution.py:15
  114.1 17.6 %collective-permute-start.18 = (f32[64,512]{1,0:T(8,128)S(1)}, f32[64,512]{1,0:T(8,128)S(1)}, u32[]{:S(2)}, u32[]{:S(2)}) collective-permute-start(f32[64,512]{1,0:T(8,128)S(1)} %get-tuple-element.42), channel_id=1, source_target_pairs={{0,192},{64,0},{128,64},{192,128},{1,193},{65,1},{129,65},{193,129... | collective-permute-start | bytes 393224 | tf_op jit(solution)/shard_map/ppermute | solution.py:15
  134.2 34.6 %all-to-all-start = ((f32[8,8,3584]{2,1,0:T(8,128)}), f32[8,8,3584]{2,1,0:T(8,128)S(1)}, u32[]{:S(2)}, u32[]{:S(2)}) async-start(f32[8,8,3584]{2,1,0:T(8,128)} %pad_maximum_fusion), calls=%async_computation | async-start | bytes 1835008 | tf_op jit(solution)/shard_map/all_to_all | solution.py:208
  168.9 1.4 collective-permute-start.19
  171.1 7.7 %all-to-all-start.1 = ((f32[4,2,8,192]{3,2,1,0:T(8,128)}), f32[4,2,8,192]{3,2,1,0:T(8,128)S(1)}, u32[]{:S(2)}, u32[]{:S(2)}) async-start(f32[4,2,8,192]{3,2,1,0:T(8,128)} %copy.25), calls=%async_computation.1 | async-start | bytes 131072 | tf_op jit(solution)/shard_map/all_to_all | solution.py:217

commit v2 on v0

v2 whole, which is shorter than its diff:
```python
import functools

import jax
import jax.numpy as jnp
from jax import lax
from jax.experimental import pallas as pl
from jax.experimental.pallas import tpu as pltpu
from jax.sharding import Mesh, PartitionSpec as P

TILE = 128
VMEM_LIMIT = 32 * 1024 * 1024
ANYWHERE = pl.BlockSpec(memory_space=pltpu.VMEM)
SOME = 6_000_000_000
AFTER = pl.BlockSpec(memory_space=pl.ANY)
SCALARS = pl.BlockSpec(memory_space=pltpu.SMEM)


def shift(value, axis, step, size):
    return lax.ppermute(value, axis, [(i, (i + step) % size) for i in range(size)])


def sibling(value):
    return lax.ppermute(value, "core", [(0, 1), (1, 0)])


def times_transposed(left, right):
    return lax.dot_general(left, right, (((1,), (1,)), ((), ())), preferred_element_type=jnp.float32)


def diagonal_kernel(place, screen, slab, keep, give, total):
    step = pl.program_id(0)
    core, row, aux = place[0], place[1], place[2]
    group, mrows, _ = slab.shape
    depth = pl.num_programs(0) * group
    tiles = mrows // TILE

    def masked(q):
        at = aux * depth + step * group + q
        parts = [
            slab[q, t * TILE : (t + 1) * TILE, :] * screen[at, row * tiles + t].astype(jnp.bfloat16)
            for t in range(tiles)
        ]
        return jnp.concatenate(parts, axis=0)

    rows = jnp.concatenate([masked(q) for q in range(group)], axis=1)
    product = times_transposed(rows, rows)

    @pl.when(step == 0)
    def _():
        total[...] = product.reshape(total.shape)

    @pl.when(step > 0)
    def _():
        total[...] += product.reshape(total.shape)

    @pl.when(step == pl.num_programs(0) - 1)
    def _():
        keep[...] = total[:, core].reshape(keep.shape)
        give[...] = total[:, 1 - core].reshape(give.shape)


def diagonal(place, screen, block, zs, group=4):
    depth, rows, width = block.shape
    half = jax.ShapeDtypeStruct((rows // 2, rows), jnp.float32)
    whole = pl.BlockSpec((rows // 2, rows), lambda q: (0, 0))
    return pl.pallas_call(
        diagonal_kernel,
        grid=(depth // group,),
        in_specs=[SCALARS, SCALARS, pl.BlockSpec((group, rows, width), lambda q: (q, 0, 0))],
        out_specs=[whole, whole],
        scratch_shapes=[pltpu.VMEM((zs, 2, rows // zs // 2, rows), jnp.float32)],
        out_shape=[half, half],
        compiler_params=pltpu.CompilerParams(vmem_limit_bytes=VMEM_LIMIT),
        cost_estimate=pl.CostEstimate(flops=1, bytes_accessed=1, transcendentals=0),
        name="diagonal",
    )(place, screen, block)


def store_by_aux(aux, product, outs, row, col):
    xs = len(outs)
    grouped = product.reshape(-1, xs, 8, product.shape[1])
    size = grouped.shape[0] * 8
    for there in range(xs):
        piece = grouped[:, there].reshape(size, -1)
        for d in range(xs):
            @pl.when(lax.rem(aux + d, xs) == there)
            def _():
                outs[d][row : row + size, col : col + piece.shape[1]] = piece


def wide(refs, core=None):
    parts = []
    for ref in refs:
        for q in range(ref.shape[0]):
            part = ref[q] if core is None else ref[q, :, core]
            parts.append(part.reshape(-1, part.shape[-1]))
    return jnp.concatenate(parts, axis=1)


def split_kernel(place, kept, got, *outs):
    store_by_aux(place[2], kept[...] + got[...], outs, 0, 0)


def pick_kernel(place, across, _, out):
    out[:, :, 0] = across[:, :, 1 - place[0]]


def early_kernel(place, mine, mine2, above, above2, below, below2, *outs):
    core, aux = place[0], place[2]
    n = above.shape[1] * above.shape[2] * above.shape[3]
    own, up = wide((mine, mine2), core), wide((above, above2), core)
    right, left = wide((above, above2)), wide((below, below2))
    store_by_aux(aux, times_transposed(own, right), outs, 0, 0)
    store_by_aux(aux, times_transposed(up, left), outs, 0, n)
    store_by_aux(aux, times_transposed(own, left), outs, 0, 2 * n)


def late_kernel(place, below, below2, mine, mine2, above, above2, across, across2, _, *outs):
    core, aux = place[0], place[2]
    left = jnp.concatenate([wide((across,), core), wide((across2,), 0)], axis=1)
    n = outs[0].shape[1] // 3
    for at, pair in enumerate(((below, below2), (mine, mine2), (above, above2))):
        store_by_aux(aux, times_transposed(left, wide(pair)), outs, 0, at * n)


def pairs(kernel, place, operands, shape, xs, after=(), flops=1):
    out = jax.ShapeDtypeStruct(shape, jnp.float32)
    return pl.pallas_call(
        kernel,
        in_specs=[SCALARS] + [ANYWHERE] * len(operands) + [AFTER] * len(after),
        out_specs=[ANYWHERE] * xs,
        out_shape=[out] * xs,
        compiler_params=pltpu.CompilerParams(vmem_limit_bytes=VMEM_LIMIT),
        cost_estimate=pl.CostEstimate(flops=flops, bytes_accessed=1, transcendentals=0),
        name=kernel.__name__,
    )(place, *operands, *after)


def pick(place, across, after):
    shape = (*across.shape[:2], 1, *across.shape[3:])
    return pl.pallas_call(
        pick_kernel,
        in_specs=[SCALARS, ANYWHERE, AFTER],
        out_specs=ANYWHERE,
        out_shape=jax.ShapeDtypeStruct(shape, across.dtype),
        compiler_params=pltpu.CompilerParams(vmem_limit_bytes=VMEM_LIMIT),
        cost_estimate=pl.CostEstimate(flops=1, bytes_accessed=1, transcendentals=0),
        name="pick",
    )(place, across, after)


def over_aux(parts, xs):
    return [shift(parts[d], "aux", d, xs) if d else parts[0] for d in range(xs)]


SLOTS = ((0,), (3,), (5,), (1, 6), (7, 4, 2))


def turn(block, zs):
    rows, cols = block.shape
    turned = block.T.reshape(zs, cols // zs // 8, 8, rows)
    return [[turned[at, k] for k in range(turned.shape[1])] for at in range(zs)]


def send_out(place, buffer, outs):
    zs = buffer.shape[0]
    for out, steps in zip(outs, SLOTS):
        for at, step in enumerate(steps):
            out[at] = buffer[lax.rem(place[3] + step, zs)]


def pack_kernel(diagonals, place, *refs):
    parts, diags, outs, buffer = refs[:4], refs[4 : 4 + diagonals], refs[4 + diagonals : -1], refs[-1]
    zs = buffer.shape[0]
    n = parts[0].shape[1] // 3
    begin = 0
    if diags:
        begin = n
        buffer[:, :, :n] = (diags[0][...] + diags[1][...] + diags[2][...] + diags[3][...]).reshape(zs, 8, n)
    for pair in range(3):
        cut = slice(pair * n, (pair + 1) * n)
        block = parts[0][:, cut] + parts[1][:, cut] + parts[2][:, cut] + parts[3][:, cut]
        buffer[:, :, begin + pair * n : begin + (pair + 1) * n] = block.reshape(zs, 8, n)
        size = block.shape[0]
        for at, pieces in enumerate(turn(block, zs)):
            for k, piece in enumerate(pieces):
                lane = begin + (3 + pair) * n + k * size
                buffer[at, :, lane : lane + size] = piece
    send_out(place, buffer, outs)


def pack(place, parts, diags=(), flops=1):
    zs = 8
    n = parts[0].shape[1] // 3
    width = (7 if diags else 6) * n
    operands = (*parts, *diags)
    shapes = [(len(steps), 8, width) for steps in SLOTS]
    return pl.pallas_call(
        functools.partial(pack_kernel, len(diags)),
        in_specs=[SCALARS] + [ANYWHERE] * len(operands),
        out_specs=[ANYWHERE] * len(shapes),
        out_shape=[jax.ShapeDtypeStruct(s, jnp.float32) for s in shapes],
        scratch_shapes=[pltpu.VMEM((zs, 8, width), jnp.float32)],
        compiler_params=pltpu.CompilerParams(vmem_limit_bytes=VMEM_LIMIT),
        cost_estimate=pl.CostEstimate(flops=flops, bytes_accessed=1, transcendentals=0),
        name="pack",
    )(place, *operands)


def reduce_z(packed):
    zs = 8
    here, forward, backward, up, down = packed
    up, down = shift(up, "z", 1, zs), shift(down, "z", -1, zs)
    forward = forward[0] + down[2]
    backward = backward[0] + up[1] + down[1]
    here = here[0] + up[0] + down[0]
    return here + shift(forward, "z", 3, zs) + shift(backward, "z", -3, zs)


def body(half_transformed, screen):
    qrows, mrows, icols = half_transformed.shape
    ys, zs, xs = 4, 8, 4
    quarter = qrows // ys
    row, z = lax.axis_index("row"), lax.axis_index("z")
    core, aux = lax.axis_index("core"), lax.axis_index("aux")
    place = jnp.stack([core, row, aux, z]).astype(jnp.int32)
    tiles = mrows // TILE
    n = mrows
    grouped = (quarter, zs, 2, n // zs // 2, icols)

    local = lax.dynamic_slice(screen, (aux * qrows, row * tiles), (qrows, tiles))
    keep = jnp.repeat(local, TILE, axis=1).astype(jnp.bfloat16)

    def slab(block, step):
        first = lax.rem(row + step, ys) * quarter
        part = lax.dynamic_slice(block, (first, 0, 0), (quarter, mrows, icols))
        return part * lax.dynamic_slice(keep, (first, 0), (quarter, mrows))[:, :, None]

    to_up, to_down = slab(half_transformed, 1), slab(half_transformed, 3)
    block, to_up, to_down = lax.optimization_barrier((half_transformed, to_up, to_down))
    below = shift(to_up, "row", 1, ys)
    above = shift(to_down, "row", -1, ys)
    mine = slab(block, 0)
    mine2 = sibling(mine)
    kept, given = diagonal(place, screen, block, zs)
    diag = pairs(split_kernel, place, (kept, sibling(given)), (zs * 8, n), xs)
    diag = over_aux(diag, xs)
    below, above, far, diag = lax.optimization_barrier((below, above, slab(block, 2), diag))
    across = shift(far, "row", 2, ys)
    below2, above2 = sibling(below), sibling(above)
    mine, mine2, above, above2, below, below2 = (
        s.reshape(grouped) for s in (mine, mine2, above, above2, below, below2)
    )
    early_parts = pairs(
        early_kernel, place, (mine, mine2, above, above2, below, below2), (zs * 8, 3 * n), xs
    )
    computed = early_parts[0]
    early_parts = over_aux(early_parts, xs)
    early = pack(place, early_parts, diag, SOME)
    across2 = sibling(pick(place, across.reshape(grouped), computed))
    late_parts = pairs(
        late_kernel,
        place,
        (below, below2, mine, mine2, above, above2, across.reshape(grouped), across2),
        (zs * 8, 3 * n),
        xs,
        (early[0],),
    )
    early, late_parts = lax.optimization_barrier((early, late_parts))
    early = reduce_z(early)
    late = reduce_z(pack(place, over_aux(late_parts, xs)))
    late_plain, late_turned = late[:, : 3 * n], late[:, 3 * n :]

    def cut(value, at):
        return value[:, at * n : (at + 1) * n]

    up = shift(jnp.concatenate([cut(early, 4), cut(early, 2), cut(late_turned, 2)], axis=1), "row", 1, ys)
    down = shift(jnp.concatenate([cut(early, 6), cut(early, 5), cut(late_turned, 0)], axis=1), "row", -1, ys)
    over = shift(late_plain, "row", 2, ys)
    plus = cut(early, 1) + cut(over, 0)
    twice = cut(up, 1) + cut(over, 1)
    minus = cut(early, 3) + cut(over, 2)
    turned_plus = cut(down, 0) + cut(up, 2)
    turned_twice = cut(down, 1) + cut(late_turned, 1)
    turned_minus = cut(up, 0) + cut(down, 2)

    turned = jnp.stack([turned_plus, turned_twice, turned_minus], axis=1)
    turned = turned.reshape(8, 3, 2, xs * zs * 8)
    own = lax.dynamic_index_in_dim(turned, core, 2, keepdims=False)
    other = sibling(lax.dynamic_index_in_dim(turned, 1 - core, 2, keepdims=False))
    pieces = jnp.stack([jnp.where(core == 0, own, other), jnp.where(core == 0, other, own)])
    pieces = pieces.reshape(2, 8, 3, xs, zs * 8).transpose(3, 0, 1, 2, 4).reshape(xs, 2, 8, 3 * zs * 8)
    pieces = lax.dynamic_slice(jnp.concatenate([pieces, pieces]), (aux, 0, 0, 0), pieces.shape)
    came = [shift(pieces[d], "aux", d, xs) if d else pieces[0] for d in range(xs)]
    came = jnp.stack([came[-e % xs] for e in range(xs)] * 2)
    came = lax.dynamic_slice(came, (lax.rem(xs - aux, xs), 0, 0, 0), pieces.shape)
    came = came.reshape(xs, 2, 8, 3, zs, 8).transpose(2, 3, 4, 1, 0, 5).reshape(8, 3 * n)
    out = jnp.concatenate(
        [cut(early, 0), plus + cut(came, 0), twice + cut(came, 1), minus + cut(came, 2)], axis=1
    )
    return lax.dynamic_slice(jnp.concatenate([out, out], axis=1), (0, lax.rem(ys - row, ys) * n), (8, 4 * n))


def solution(mesh):
    rows, cols, aux = mesh.devices.shape
    split = Mesh(mesh.devices.reshape(rows, cols // 2, 2, aux), ("row", "z", "core", "aux"))
    in_specs = (P("aux", "row", ("z", "core")), P())
    out_specs = P(("row", "z", "core", "aux"), None)
    return jax.shard_map(body, mesh=split, in_specs=in_specs, out_specs=out_specs, check_vma=False)
```

time: 338 us -> 138 us (0.41)
  waiting for transfers between devices: 300 us -> 52.3 us
  starting transfers between devices: 0.04 us -> 59.4 us
  matrix products: 15 us -> 0 us
  Pallas kernels: 0 us -> 14 us
  between operations: 13.4 us -> 0.36 us
  local copies, waits for them, and re-layouts: 0.19 us -> 5.19 us
    all_gather x1 -> x0, waiting for transfers between devices: 161 us -> none  [body(): lax.all_gather(screened, 'row', axis=1, tiled=True)]
    reduce_scatter x1 -> x0, waiting for transfers between devices: 140 us -> none  [body(): lax.psum_scatter(partial_k, ('col', 'aux'), scatter_dimension=0, tiled=True)]
    ppermute x0 -> x32, starting transfers between devices: none -> 59.4 us  [the longest x26 43.4 us: shift(): lax.ppermute(value, axis, [(i, (i + step) % size) for i in range(size)])]
    ppermute x0 -> x32, waiting for transfers between devices: none -> 52.3 us  [the longest x26 48.3 us: shift(): lax.ppermute(value, axis, [(i, (i + step) % size) for i in range(size)])]
    dot_general x1 -> x0, matrix products: 15 us -> none  [contract(): lax.dot_general(left, right, (((0, 2), (0, 2)), ((), ())), preferred_elem...]
    pallas_call x0 -> x7, Pallas kernels: none -> 14 us  [the longest x3 6.82 us: pairs(): pl.pallas_call(kernel, in_specs=[SCALARS] + [ANYWHERE] * len(operands) +...]
  transfers between devices with their start and end apart: 2 -> 32, of which waited for: 2 -> 16; matrix products, arithmetic and copies ran while one was open for 0% -> 2% of each run, Pallas kernels for 0% -> 8%
where the time goes in v2:
time: 138 us; the launch traced here: 136 us
  starting transfers between devices  59.4 us (43%)
  waiting for transfers between devices  52.3 us (38%)
  Pallas kernels  14 us (10%)
  local copies, waits for them, and re-layouts  5.19 us (4%)
  other arithmetic  4.59 us (3%)
    ppermute x26, waiting for transfers between devices, shift(): lax.ppermute(value, axis, [(i, (i + step) % size) for i in range(size)])  48.3 us
    ppermute x26, starting transfers between devices, shift(): lax.ppermute(value, axis, [(i, (i + step) % size) for i in range(size)])  43.4 us
    ppermute x6, starting transfers between devices, sibling(): return lax.ppermute(value, 'core', [(0, 1), (1, 0)])  16.1 us
    pallas_call x3, Pallas kernels, pairs(): pl.pallas_call(kernel, in_specs=[SCALARS] + [ANYWHERE] * len(operands) +...  6.82 us
    pallas_call x1, Pallas kernels, diagonal(): pl.pallas_call(diagonal_kernel, grid=(depth // group,), in_specs=[SCALARS...  4.62 us
    ppermute x6, waiting for transfers between devices, sibling(): return lax.ppermute(value, 'core', [(0, 1), (1, 0)])  4.01 us
    mul x2, other arithmetic, slab(): part * lax.dynamic_slice(keep, (first, 0), (quarter, mrows))[:, :, None]  3.43 us
  transfers between devices with their start and end apart: 32, of which 16 were waited for; matrix products, arithmetic and copies ran while one was open for 2% of the time, Pallas kernels for 8%

profile of v2, /device:TPU:1, one launch (start us, length us, event | category | flops | bytes accessed | tf_op | source)
XLA Modules:
  0.0 135.9 jit_solution(13349419797183877082)
XLA Ops:
  0.0 0.8 dynamic-slice_convert_fusion
  0.8 0.1 copy.8
  0.9 0.1 broadcast_in_dim.2
  1.1 2.7 %dynamic-slice_multiply_fusion.2 = (bf16[4,512,256]{2,1,0:T(8,128)(2,1)S(1)}, bf16[4,512,256]{2,1,0:T(8,128)(2,1)}) fusion(bf16[16,512,256]{2,1,0:T(8,128)(2,1)} %slab, s32[]{:T(128)S(6)} %select_n.53, bf16[4,512]{1,0:T(4,128)(2,1)S(1)} %get-tuple-element.116, bf16[4,512]{1,0:T(4,128)(2,1)S(1)} %get-tuple-element.117, s32[]{:T(128)S(6)} %select_n.50), kind=kLoop, calls=%fused_computation.2 | loop fusion | flops 1048576 | bytes 4202504 | tf_op jit(solution)/shard_map/mul | solution.py:237
  3.8 2.1 %collective-permute-start.1 = (bf16[4,512,256]{2,1,0:T(8,128)(2,1)}, bf16[4,512,256]{2,1,0:T(8,128)(2,1)S(1)}, u32[]{:S(2)}, u32[]{:S(2)}) collective-permute-start(bf16[4,512,256]{2,1,0:T(8,128)(2,1)} %get-tuple-element.49), channel_id=1, source_target_pairs={{0,64},{64,128},{128,192},{192,0},{1,65},{65,129},{129,193},{193,1... | collective-permute-start | bytes 3145736 | tf_op jit(solution)/shard_map/ppermute | solution.py:19
  6.0 1.4 %collective-permute-start.2 = (bf16[4,512,256]{2,1,0:T(8,128)(2,1)S(1)}, bf16[4,512,256]{2,1,0:T(8,128)(2,1)S(1)}, u32[]{:S(2)}, u32[]{:S(2)}) collective-permute-start(bf16[4,512,256]{2,1,0:T(8,128)(2,1)S(1)} %get-tuple-element.50), channel_id=1, source_target_pairs={{0,192},{64,0},{128,64},{192,128},{1,193},{65,1},{129,65},{193,129... | collective-permute-start | bytes 3145736 | tf_op jit(solution)/shard_map/ppermute | solution.py:19
  7.6 2.2 %copy-done = bf16[16,512,256]{2,1,0:T(8,128)(2,1)S(1)} copy-done((bf16[16,512,256]{2,1,0:T(8,128)(2,1)S(1)}, bf16[16,512,256]{2,1,0:T(8,128)(2,1)}, u32[]{:S(2)}) %copy-start) | copy-done | bytes 4194328
  9.8 4.6 %diagonal.1 = (f32[256,512]{1,0:T(8,128)S(1)}, f32[256,512]{1,0:T(8,128)S(1)}) custom-call(s32[4]{0:T(128)S(1)} %pad_add_fusion.place, s32[64,16]{1,0:T(8,128)S(1)} %copy.9.screen, bf16[16,512,256]{2,1,0:T(8,128)(2,1)S(1)} %copy-done), custom_call_target="tpu_custom_call" | custom-call | flops 1 | bytes 1 | tf_op jit(solution)/shard_map/diagonal/pallas_call | solution.py:66
  14.4 3.0 %collective-permute-start.3 = (f32[256,512]{1,0:T(8,128)S(1)}, f32[256,512]{1,0:T(8,128)S(1)}, u32[]{:S(2)}, u32[]{:S(2)}) collective-permute-start(f32[256,512]{1,0:T(8,128)S(1)} %get-tuple-element.52), channel_id=1, source_target_pairs={{0,4},{4,0},{1,5},{5,1},{2,6},{6,2},{3,7},{7,3},{8,12},{12,8},{9,1... | collective-permute-start | bytes 1572872 | tf_op jit(solution)/shard_map/ppermute | solution.py:23
  17.4 1.5 %collective-permute-done.3.got = f32[256,512]{1,0:T(8,128)S(1)} collective-permute-done((f32[256,512]{1,0:T(8,128)S(1)}, f32[256,512]{1,0:T(8,128)S(1)}, u32[]{:S(2)}, u32[]{:S(2)}) %collective-permute-start.3) | collective-permute-done | bytes 524320 | tf_op jit(solution)/shard_map/ppermute | solution.py:23
  18.9 0.7 split_kernel.1
  19.6 0.1 collective-permute-start.4
  19.7 1.9 %collective-permute-start.5 = (f32[64,512]{1,0:T(8,128)S(1)}, f32[64,512]{1,0:T(8,128)S(1)}, u32[]{:S(2)}, u32[]{:S(2)}) collective-permute-start(f32[64,512]{1,0:T(8,128)S(1)} %get-tuple-element.55), channel_id=1, source_target_pairs={{0,2},{1,3},{2,0},{3,1},{4,6},{5,7},{6,4},{7,5},{8,10},{9,11},{10,... | collective-permute-start | bytes 393224 | tf_op jit(solution)/shard_map/ppermute | solution.py:19
  21.6 1.2 collective-permute-start.6
  22.8 0.7 dynamic-slice_multiply_fusion
  23.5 2.9 %collective-permute-done.4.refs_5_ = f32[64,512]{1,0:T(8,128)S(1)} collective-permute-done((f32[64,512]{1,0:T(8,128)S(1)}, f32[64,512]{1,0:T(8,128)S(1)}, u32[]{:S(2)}, u32[]{:S(2)}) %collective-permute-start.4) | collective-permute-done | bytes 131104 | tf_op jit(solution)/shard_map/ppermute | solution.py:19
  26.3 3.3 %collective-permute-start = (bf16[4,512,256]{2,1,0:T(8,128)(2,1)S(1)}, bf16[4,512,256]{2,1,0:T(8,128)(2,1)S(1)}, u32[]{:S(2)}, u32[]{:S(2)}) collective-permute-start(bf16[4,512,256]{2,1,0:T(8,128)(2,1)S(1)} %get-tuple-element.92), channel_id=1, source_target_pairs={{0,4},{4,0},{1,5},{5,1},{2,6},{6,2},{3,7},{7,3},{8,12},{12,8},{9,1... | collective-permute-start | bytes 3145736 | tf_op jit(solution)/shard_map/ppermute | solution.py:23
  29.6 2.1 %collective-permute-start.7 = (bf16[4,512,256]{2,1,0:T(8,128)(2,1)S(1)}, bf16[4,512,256]{2,1,0:T(8,128)(2,1)S(1)}, u32[]{:S(2)}, u32[]{:S(2)}) collective-permute-start(bf16[4,512,256]{2,1,0:T(8,128)(2,1)S(1)} %collective-permute-done.2), channel_id=1, source_target_pairs={{0,4},{4,0},{1,5},{5,1},{2,6},{6,2},{3,7},{7,3},{8,12},{12,8},{9,1... | collective-permute-start | bytes 3145736 | tf_op jit(solution)/shard_map/ppermute | solution.py:23
  31.7 2.4 %collective-permute-start.12 = (bf16[4,512,256]{2,1,0:T(8,128)(2,1)S(1)}, bf16[4,512,256]{2,1,0:T(8,128)(2,1)S(1)}, u32[]{:S(2)}, u32[]{:S(2)}) collective-permute-start(bf16[4,512,256]{2,1,0:T(8,128)(2,1)S(1)} %get-tuple-element.72), channel_id=1, source_target_pairs={{0,128},{64,192},{128,0},{192,64},{1,129},{65,193},{129,1},{193,65... | collective-permute-start | bytes 3145736 | tf_op jit(solution)/shard_map/ppermute | solution.py:19
  34.2 1.3 collective-permute-done.8
  35.5 3.2 %early_kernel.1 = (f32[64,1536]{1,0:T(8,128)S(1)}, f32[64,1536]{1,0:T(8,128)S(1)}, f32[64,1536]{1,0:T(8,128)S(1)}, f32[64,1536]{1,0:T(8,128)S(1)}) custom-call(s32[4]{0:T(128)S(1)} %pad_add_fusion.place, bf16[4,8,2,32,256]{4,3,2,1,0:T(8,128)(2,1)S(1)} %bitcast.67, bf16[4,8,2,32,256]{4,3,2,1,0:T(8,128)(2,1)S(1)} %bitcast.73, ...), custom_call_target="tpu_custom_call" | custom-call | flops 1 | bytes 1 | tf_op jit(solution)/shard_map/early_kernel/pallas_call | solution.py:128
  38.7 1.3 collective-permute-start.9
  40.0 2.5 %collective-permute-start.10 = (f32[64,1536]{1,0:T(8,128)S(1)}, f32[64,1536]{1,0:T(8,128)S(1)}, u32[]{:S(2)}, u32[]{:S(2)}) collective-permute-start(f32[64,1536]{1,0:T(8,128)S(1)} %get-tuple-element.61), channel_id=1, source_target_pairs={{0,2},{1,3},{2,0},{3,1},{4,6},{5,7},{6,4},{7,5},{8,10},{9,11},{10,... | collective-permute-start | bytes 1179656 | tf_op jit(solution)/shard_map/ppermute | solution.py:19
  42.4 1.2 collective-permute-start.11
  43.6 13.9 %collective-permute-done.12 = bf16[4,512,256]{2,1,0:T(8,128)(2,1)S(1)} collective-permute-done((bf16[4,512,256]{2,1,0:T(8,128)(2,1)S(1)}, bf16[4,512,256]{2,1,0:T(8,128)(2,1)S(1)}, u32[]{:S(2)}, u32[]{:S(2)}) %collective-permute-start.12) | collective-permute-done | bytes 1048608 | tf_op jit(solution)/shard_map/ppermute | solution.py:19
  57.4 0.6 pick.1
  58.0 1.4 %collective-permute-start.13 = (bf16[4,8,1,32,256]{4,3,2,1,0:T(8,128)(2,1)S(1)}, bf16[4,8,1,32,256]{4,3,2,1,0:T(8,128)(2,1)S(1)}, u32[]{:S(2)}, u32[]{:S(2)}) collective-permute-start(bf16[4,8,1,32,256]{4,3,2,1,0:T(8,128)(2,1)S(1)} %pick.1), channel_id=1, source_target_pairs={{0,4},{4,0},{1,5},{5,1},{2,6},{6,2},{3,7},{7,3},{8,12},{12,8},{9,1... | collective-permute-start | bytes 1572872 | tf_op jit(solution)/shard_map/ppermute | solution.py:23
  59.5 0.2 collective-permute-done.10.refs_2_
  59.7 1.0 pack.2
  60.7 0.3 collective-permute-done.13.across2
  61.0 3.0 %late_kernel.1 = (f32[64,1536]{1,0:T(8,128)S(1)}, f32[64,1536]{1,0:T(8,128)S(1)}, f32[64,1536]{1,0:T(8,128)S(1)}, f32[64,1536]{1,0:T(8,128)S(1)}) custom-call(s32[4]{0:T(128)S(1)} %pad_add_fusion.place, bf16[4,8,2,32,256]{4,3,2,1,0:T(8,128)(2,1)S(1)} %bitcast.70, bf16[4,8,2,32,256]{4,3,2,1,0:T(8,128)(2,1)S(1)} %bitcast.78, ...), custom_call_target="tpu_custom_call" | custom-call | flops 1 | bytes 1 | tf_op jit(solution)/shard_map/late_kernel/pallas_call | solution.py:128
  64.0 5.7 %collective-permute-start.15 = (f32[3,8,3584]{2,1,0:T(8,128)S(1)}, f32[3,8,3584]{2,1,0:T(8,128)S(1)}, u32[]{:S(2)}, u32[]{:S(2)}) collective-permute-start(f32[3,8,3584]{2,1,0:T(8,128)S(1)} %get-tuple-element.79), channel_id=1, source_target_pairs={{0,56},{8,0},{16,8},{24,16},{32,24},{40,32},{48,40},{56,48},{1,57}... | collective-permute-start | bytes 1032200 | tf_op jit(solution)/shard_map/ppermute | solution.py:19
  69.7 1.2 collective-permute-start.18
  70.9 2.5 %collective-permute-start.19 = (f32[64,1536]{1,0:T(8,128)S(1)}, f32[64,1536]{1,0:T(8,128)S(1)}, u32[]{:S(2)}, u32[]{:S(2)}) collective-permute-start(f32[64,1536]{1,0:T(8,128)S(1)} %get-tuple-element.84), channel_id=1, source_target_pairs={{0,2},{1,3},{2,0},{3,1},{4,6},{5,7},{6,4},{7,5},{8,10},{9,11},{10,... | collective-permute-start | bytes 1179656 | tf_op jit(solution)/shard_map/ppermute | solution.py:19
  73.3 1.1 collective-permute-start.20
  74.5 2.3 %collective-permute-done.14 = f32[2,8,3584]{2,1,0:T(8,128)S(1)} collective-permute-done((f32[2,8,3584]{2,1,0:T(8,128)S(1)}, f32[2,8,3584]{2,1,0:T(8,128)S(1)}, u32[]{:S(2)}, u32[]{:S(2)}) %collective-permute-start.14) | collective-permute-done | bytes 229408 | tf_op jit(solution)/shard_map/ppermute | solution.py:19
  76.8 2.5 %collective-permute-start.17 = (f32[8,3584]{1,0:T(8,128)S(1)}, f32[8,3584]{1,0:T(8,128)S(1)}, u32[]{:S(2)}, u32[]{:S(2)}) collective-permute-start(f32[8,3584]{1,0:T(8,128)S(1)} %get-tuple-element.96), channel_id=1, source_target_pairs={{0,40},{8,48},{16,56},{24,0},{32,8},{40,16},{48,24},{56,32},{1,41}... | collective-permute-start | bytes 344072 | tf_op jit(solution)/shard_map/ppermute | solution.py:19
  79.3 0.8 collective-permute-start.16
  80.1 0.1 collective-permute-done.18.refs_1_
  80.3 10.0 %collective-permute-done.19.refs_2_ = f32[64,1536]{1,0:T(8,128)S(1)} collective-permute-done((f32[64,1536]{1,0:T(8,128)S(1)}, f32[64,1536]{1,0:T(8,128)S(1)}, u32[]{:S(2)}, u32[]{:S(2)}) %collective-permute-start.19) | collective-permute-done | bytes 393248 | tf_op jit(solution)/shard_map/ppermute | solution.py:19
  90.2 1.0 pack.3
  91.2 2.4 %collective-permute-start.22 = (f32[3,8,3072]{2,1,0:T(8,128)S(1)}, f32[3,8,3072]{2,1,0:T(8,128)S(1)}, u32[]{:S(2)}, u32[]{:S(2)}) collective-permute-start(f32[3,8,3072]{2,1,0:T(8,128)S(1)} %get-tuple-element.88), channel_id=1, source_target_pairs={{0,56},{8,0},{16,8},{24,16},{32,24},{40,32},{48,40},{56,48},{1,57}... | collective-permute-start | bytes 884744 | tf_op jit(solution)/shard_map/ppermute | solution.py:19
  93.7 5.7 %collective-permute-done.21 = f32[2,8,3072]{2,1,0:T(8,128)S(1)} collective-permute-done((f32[2,8,3072]{2,1,0:T(8,128)S(1)}, f32[2,8,3072]{2,1,0:T(8,128)S(1)}, u32[]{:S(2)}, u32[]{:S(2)}) %collective-permute-start.21) | collective-permute-done | bytes 196640 | tf_op jit(solution)/shard_map/ppermute | solution.py:19
  99.4 0.6 collective-permute-start.24
  100.0 2.7 %collective-permute-start.23 = (f32[8,3072]{1,0:T(8,128)S(1)}, f32[8,3072]{1,0:T(8,128)S(1)}, u32[]{:S(2)}, u32[]{:S(2)}) collective-permute-start(f32[8,3072]{1,0:T(8,128)S(1)} %get-tuple-element.97), channel_id=1, source_target_pairs={{0,24},{8,32},{16,40},{24,48},{32,56},{40,0},{48,8},{56,16},{1,25}... | collective-permute-start | bytes 294920 | tf_op jit(solution)/shard_map/ppermute | solution.py:19
  102.8 4.0 %collective-permute-done.24 = f32[8,3072]{1,0:T(8,128)S(1)} collective-permute-done((f32[8,3072]{1,0:T(8,128)S(1)}, f32[8,3072]{1,0:T(8,128)S(1)}, u32[]{:S(2)}, u32[]{:S(2)}) %collective-permute-start.24) | collective-permute-done | bytes 98336 | tf_op jit(solution)/shard_map/ppermute | solution.py:19
  106.8 0.9 collective-permute-done.23
  107.8 2.6 %collective-permute-start.26 = (f32[8,1536]{1,0:T(8,128)S(1)}, f32[8,1536]{1,0:T(8,128)S(1)}, u32[]{:S(2)}, u32[]{:S(2)}) collective-permute-start(f32[8,1536]{1,0:T(8,128)S(1)} %pad_maximum_fusion), channel_id=1, source_target_pairs={{0,192},{64,0},{128,64},{192,128},{1,193},{65,1},{129,65},{193,129... | collective-permute-start | bytes 147464 | tf_op jit(solution)/shard_map/ppermute | solution.py:19
  110.3 1.2 collective-permute-done.26
  111.5 1.0 collective-permute-start.27
  112.5 3.7 %collective-permute-done.27 = f32[8,1536]{1,0:T(8,128)S(1)} collective-permute-done((f32[8,1536]{1,0:T(8,128)S(1)}, f32[8,1536]{1,0:T(8,128)S(1)}, u32[]{:S(2)}, u32[]{:S(2)}) %collective-permute-start.27) | collective-permute-done | bytes 49184 | tf_op jit(solution)/shard_map/ppermute | solution.py:19
  116.3 6.3 %collective-permute-start.28 = (f32[8,3,256]{2,0,1:T(8,128)S(1)}, f32[8,3,256]{2,0,1:T(8,128)S(1)}, u32[]{:S(2)}, u32[]{:S(2)}) collective-permute-start(f32[8,3,256]{2,0,1:T(8,128)S(1)} %dynamic-slice_bitcast_fusion), channel_id=1, source_target_pairs={{0,4},{4,0},{1,5},{5,1},{2,6},{6,2},{3,7},{7,3},{8,12},{12,8},{9,1... | collective-permute-start | bytes 73736 | tf_op jit(solution)/shard_map/ppermute | solution.py:23
  122.6 0.8 collective-permute-done.28
  123.5 0.1 stack.61
  123.5 0.1 stack.60
  123.7 0.1 reshape.66
  123.9 4.6 %collective-permute-start.29 = (f32[2,8,192]{2,1,0:T(8,128)S(1)}, f32[2,8,192]{2,1,0:T(8,128)S(1)}, u32[]{:S(2)}, u32[]{:S(2)}) collective-permute-start(f32[2,8,192]{2,1,0:T(8,128)S(1)} %get-tuple-element.113), channel_id=1, source_target_pairs={{0,3},{1,0},{2,1},{3,2},{4,7},{5,4},{6,5},{7,6},{8,11},{9,8},{10,9... | collective-permute-start | bytes 36872 | tf_op jit(solution)/shard_map/ppermute | solution.py:19
  128.5 0.9 collective-permute-start.25
  129.4 0.7 collective-permute-start.31
  130.1 3.4 %collective-permute-done.30 = f32[2,8,192]{2,1,0:T(8,128)S(1)} collective-permute-done((f32[2,8,192]{2,1,0:T(8,128)S(1)}, f32[2,8,192]{2,1,0:T(8,128)S(1)}, u32[]{:S(2)}, u32[]{:S(2)}) %collective-permute-start.30) | collective-permute-done | bytes 12320 | tf_op jit(solution)/shard_map/ppermute | solution.py:19
  133.5 0.3 reshape.67
  133.8 0.5 copy.11
  134.4 0.8 reshape.68
  135.3 0.6 constant_dynamic-slice_fusion
  (62 shorter events, 0.6 us)
Async XLA Ops:
  0.0 7.4 %copy-start.2 = (s32[64,16]{0,1:T(8,128)S(1)}, s32[64,16]{0,1:T(8,128)}, u32[]{:S(2)}) copy-start(s32[64,16]{0,1:T(8,128)} %param.3) | copy-start | bytes 12292
  3.8 25.8 %collective-permute-start.1 = (bf16[4,512,256]{2,1,0:T(8,128)(2,1)}, bf16[4,512,256]{2,1,0:T(8,128)(2,1)S(1)}, u32[]{:S(2)}, u32[]{:S(2)}) collective-permute-start(bf16[4,512,256]{2,1,0:T(8,128)(2,1)} %get-tuple-element.49), channel_id=1, source_target_pairs={{0,64},{64,128},{128,192},{192,0},{1,65},{65,129},{129,193},{193,1... | collective-permute-start | bytes 3145736 | tf_op jit(solution)/shard_map/ppermute | solution.py:19
  6.0 23.7 %collective-permute-start.2 = (bf16[4,512,256]{2,1,0:T(8,128)(2,1)S(1)}, bf16[4,512,256]{2,1,0:T(8,128)(2,1)S(1)}, u32[]{:S(2)}, u32[]{:S(2)}) collective-permute-start(bf16[4,512,256]{2,1,0:T(8,128)(2,1)S(1)} %get-tuple-element.50), channel_id=1, source_target_pairs={{0,192},{64,0},{128,64},{192,128},{1,193},{65,1},{129,65},{193,129... | collective-permute-start | bytes 3145736 | tf_op jit(solution)/shard_map/ppermute | solution.py:19
  7.6 2.2 %copy-start = (bf16[16,512,256]{2,1,0:T(8,128)(2,1)S(1)}, bf16[16,512,256]{2,1,0:T(8,128)(2,1)}, u32[]{:S(2)}) copy-start(bf16[16,512,256]{2,1,0:T(8,128)(2,1)} %slab) | copy-start | bytes 12582916
  9.8 13.0 %copy-start.1 = (bf16[16,512,256]{2,1,0:T(8,128)(2,1)S(1)}, bf16[16,512,256]{2,1,0:T(8,128)(2,1)}, u32[]{:S(2)}) copy-start(bf16[16,512,256]{2,1,0:T(8,128)(2,1)} %slab) | copy-start | bytes 12582916
  14.4 4.5 %collective-permute-start.3 = (f32[256,512]{1,0:T(8,128)S(1)}, f32[256,512]{1,0:T(8,128)S(1)}, u32[]{:S(2)}, u32[]{:S(2)}) collective-permute-start(f32[256,512]{1,0:T(8,128)S(1)} %get-tuple-element.52), channel_id=1, source_target_pairs={{0,4},{4,0},{1,5},{5,1},{2,6},{6,2},{3,7},{7,3},{8,12},{12,8},{9,1... | collective-permute-start | bytes 1572872 | tf_op jit(solution)/shard_map/ppermute | solution.py:23
  19.6 6.7 %collective-permute-start.4 = (f32[64,512]{1,0:T(8,128)S(1)}, f32[64,512]{1,0:T(8,128)S(1)}, u32[]{:S(2)}, u32[]{:S(2)}) collective-permute-start(f32[64,512]{1,0:T(8,128)S(1)} %get-tuple-element.54), channel_id=1, source_target_pairs={{0,1},{1,2},{2,3},{3,0},{4,5},{5,6},{6,7},{7,4},{8,9},{9,10},{10,1... | collective-permute-start | bytes 393224 | tf_op jit(solution)/shard_map/ppermute | solution.py:19
  19.7 9.9 %collective-permute-start.5 = (f32[64,512]{1,0:T(8,128)S(1)}, f32[64,512]{1,0:T(8,128)S(1)}, u32[]{:S(2)}, u32[]{:S(2)}) collective-permute-start(f32[64,512]{1,0:T(8,128)S(1)} %get-tuple-element.55), channel_id=1, source_target_pairs={{0,2},{1,3},{2,0},{3,1},{4,6},{5,7},{6,4},{7,5},{8,10},{9,11},{10,... | collective-permute-start | bytes 393224 | tf_op jit(solution)/shard_map/ppermute | solution.py:19
  21.6 8.0 %collective-permute-start.6 = (f32[64,512]{1,0:T(8,128)S(1)}, f32[64,512]{1,0:T(8,128)S(1)}, u32[]{:S(2)}, u32[]{:S(2)}) collective-permute-start(f32[64,512]{1,0:T(8,128)S(1)} %get-tuple-element.56), channel_id=1, source_target_pairs={{0,3},{1,0},{2,1},{3,2},{4,7},{5,4},{6,5},{7,6},{8,11},{9,8},{10,9... | collective-permute-start | bytes 393224 | tf_op jit(solution)/shard_map/ppermute | solution.py:19
  26.3 7.8 %collective-permute-start = (bf16[4,512,256]{2,1,0:T(8,128)(2,1)S(1)}, bf16[4,512,256]{2,1,0:T(8,128)(2,1)S(1)}, u32[]{:S(2)}, u32[]{:S(2)}) collective-permute-start(bf16[4,512,256]{2,1,0:T(8,128)(2,1)S(1)} %get-tuple-element.92), channel_id=1, source_target_pairs={{0,4},{4,0},{1,5},{5,1},{2,6},{6,2},{3,7},{7,3},{8,12},{12,8},{9,1... | collective-permute-start | bytes 3145736 | tf_op jit(solution)/shard_map/ppermute | solution.py:23
  29.6 4.5 %collective-permute-start.7 = (bf16[4,512,256]{2,1,0:T(8,128)(2,1)S(1)}, bf16[4,512,256]{2,1,0:T(8,128)(2,1)S(1)}, u32[]{:S(2)}, u32[]{:S(2)}) collective-permute-start(bf16[4,512,256]{2,1,0:T(8,128)(2,1)S(1)} %collective-permute-done.2), channel_id=1, source_target_pairs={{0,4},{4,0},{1,5},{5,1},{2,6},{6,2},{3,7},{7,3},{8,12},{12,8},{9,1... | collective-permute-start | bytes 3145736 | tf_op jit(solution)/shard_map/ppermute | solution.py:23
  31.7 3.8 %collective-permute-start.8 = (bf16[4,512,256]{2,1,0:T(8,128)(2,1)S(1)}, bf16[4,512,256]{2,1,0:T(8,128)(2,1)S(1)}, u32[]{:S(2)}, u32[]{:S(2)}) collective-permute-start(bf16[4,512,256]{2,1,0:T(8,128)(2,1)S(1)} %collective-permute-done.1), channel_id=1, source_target_pairs={{0,4},{4,0},{1,5},{5,1},{2,6},{6,2},{3,7},{7,3},{8,12},{12,8},{9,1... | collective-permute-start | bytes 3145736 | tf_op jit(solution)/shard_map/ppermute | solution.py:23
  31.7 25.7 %collective-permute-start.12 = (bf16[4,512,256]{2,1,0:T(8,128)(2,1)S(1)}, bf16[4,512,256]{2,1,0:T(8,128)(2,1)S(1)}, u32[]{:S(2)}, u32[]{:S(2)}) collective-permute-start(bf16[4,512,256]{2,1,0:T(8,128)(2,1)S(1)} %get-tuple-element.72), channel_id=1, source_target_pairs={{0,128},{64,192},{128,0},{192,64},{1,129},{65,193},{129,1},{193,65... | collective-permute-start | bytes 3145736 | tf_op jit(solution)/shard_map/ppermute | solution.py:19
  38.7 20.8 %collective-permute-start.9 = (f32[64,1536]{1,0:T(8,128)S(1)}, f32[64,1536]{1,0:T(8,128)S(1)}, u32[]{:S(2)}, u32[]{:S(2)}) collective-permute-start(f32[64,1536]{1,0:T(8,128)S(1)} %get-tuple-element.60), channel_id=1, source_target_pairs={{0,1},{1,2},{2,3},{3,0},{4,5},{5,6},{6,7},{7,4},{8,9},{9,10},{10,1... | collective-permute-start | bytes 1179656 | tf_op jit(solution)/shard_map/ppermute | solution.py:19
  40.0 19.8 %collective-permute-start.10 = (f32[64,1536]{1,0:T(8,128)S(1)}, f32[64,1536]{1,0:T(8,128)S(1)}, u32[]{:S(2)}, u32[]{:S(2)}) collective-permute-start(f32[64,1536]{1,0:T(8,128)S(1)} %get-tuple-element.61), channel_id=1, source_target_pairs={{0,2},{1,3},{2,0},{3,1},{4,6},{5,7},{6,4},{7,5},{8,10},{9,11},{10,... | collective-permute-start | bytes 1179656 | tf_op jit(solution)/shard_map/ppermute | solution.py:19
  42.4 17.3 %collective-permute-start.11 = (f32[64,1536]{1,0:T(8,128)S(1)}, f32[64,1536]{1,0:T(8,128)S(1)}, u32[]{:S(2)}, u32[]{:S(2)}) collective-permute-start(f32[64,1536]{1,0:T(8,128)S(1)} %get-tuple-element.62), channel_id=1, source_target_pairs={{0,3},{1,0},{2,1},{3,2},{4,7},{5,4},{6,5},{7,6},{8,11},{9,8},{10,9... | collective-permute-start | bytes 1179656 | tf_op jit(solution)/shard_map/ppermute | solution.py:19
  58.0 3.0 %collective-permute-start.13 = (bf16[4,8,1,32,256]{4,3,2,1,0:T(8,128)(2,1)S(1)}, bf16[4,8,1,32,256]{4,3,2,1,0:T(8,128)(2,1)S(1)}, u32[]{:S(2)}, u32[]{:S(2)}) collective-permute-start(bf16[4,8,1,32,256]{4,3,2,1,0:T(8,128)(2,1)S(1)} %pick.1), channel_id=1, source_target_pairs={{0,4},{4,0},{1,5},{5,1},{2,6},{6,2},{3,7},{7,3},{8,12},{12,8},{9,1... | collective-permute-start | bytes 1572872 | tf_op jit(solution)/shard_map/ppermute | solution.py:23
  64.0 12.7 %collective-permute-start.15 = (f32[3,8,3584]{2,1,0:T(8,128)S(1)}, f32[3,8,3584]{2,1,0:T(8,128)S(1)}, u32[]{:S(2)}, u32[]{:S(2)}) collective-permute-start(f32[3,8,3584]{2,1,0:T(8,128)S(1)} %get-tuple-element.79), channel_id=1, source_target_pairs={{0,56},{8,0},{16,8},{24,16},{32,24},{40,32},{48,40},{56,48},{1,57}... | collective-permute-start | bytes 1032200 | tf_op jit(solution)/shard_map/ppermute | solution.py:19
  69.6 7.1 %collective-permute-start.14 = (f32[2,8,3584]{2,1,0:T(8,128)S(1)}, f32[2,8,3584]{2,1,0:T(8,128)S(1)}, u32[]{:S(2)}, u32[]{:S(2)}) collective-permute-start(f32[2,8,3584]{2,1,0:T(8,128)S(1)} %get-tuple-element.78), channel_id=1, source_target_pairs={{0,8},{8,16},{16,24},{24,32},{32,40},{40,48},{48,56},{56,0},{1,9},... | collective-permute-start | bytes 688136 | tf_op jit(solution)/shard_map/ppermute | solution.py:19
  69.7 10.6 %collective-permute-start.18 = (f32[64,1536]{1,0:T(8,128)S(1)}, f32[64,1536]{1,0:T(8,128)S(1)}, u32[]{:S(2)}, u32[]{:S(2)}) collective-permute-start(f32[64,1536]{1,0:T(8,128)S(1)} %get-tuple-element.83), channel_id=1, source_target_pairs={{0,1},{1,2},{2,3},{3,0},{4,5},{5,6},{6,7},{7,4},{8,9},{9,10},{10,1... | collective-permute-start | bytes 1179656 | tf_op jit(solution)/shard_map/ppermute | solution.py:19
  70.9 19.4 %collective-permute-start.19 = (f32[64,1536]{1,0:T(8,128)S(1)}, f32[64,1536]{1,0:T(8,128)S(1)}, u32[]{:S(2)}, u32[]{:S(2)}) collective-permute-start(f32[64,1536]{1,0:T(8,128)S(1)} %get-tuple-element.84), channel_id=1, source_target_pairs={{0,2},{1,3},{2,0},{3,1},{4,6},{5,7},{6,4},{7,5},{8,10},{9,11},{10,... | collective-permute-start | bytes 1179656 | tf_op jit(solution)/shard_map/ppermute | solution.py:19
  73.3 16.9 %collective-permute-start.20 = (f32[64,1536]{1,0:T(8,128)S(1)}, f32[64,1536]{1,0:T(8,128)S(1)}, u32[]{:S(2)}, u32[]{:S(2)}) collective-permute-start(f32[64,1536]{1,0:T(8,128)S(1)} %get-tuple-element.85), channel_id=1, source_target_pairs={{0,3},{1,0},{2,1},{3,2},{4,7},{5,4},{6,5},{7,6},{8,11},{9,8},{10,9... | collective-permute-start | bytes 1179656 | tf_op jit(solution)/shard_map/ppermute | solution.py:19
  76.8 16.9 %collective-permute-start.17 = (f32[8,3584]{1,0:T(8,128)S(1)}, f32[8,3584]{1,0:T(8,128)S(1)}, u32[]{:S(2)}, u32[]{:S(2)}) collective-permute-start(f32[8,3584]{1,0:T(8,128)S(1)} %get-tuple-element.96), channel_id=1, source_target_pairs={{0,40},{8,48},{16,56},{24,0},{32,8},{40,16},{48,24},{56,32},{1,41}... | collective-permute-start | bytes 344072 | tf_op jit(solution)/shard_map/ppermute | solution.py:19
  79.3 14.4 %collective-permute-start.16 = (f32[8,3584]{1,0:T(8,128)S(1)}, f32[8,3584]{1,0:T(8,128)S(1)}, u32[]{:S(2)}, u32[]{:S(2)}) collective-permute-start(f32[8,3584]{1,0:T(8,128)S(1)} %get-tuple-element.95), channel_id=1, source_target_pairs={{0,24},{8,32},{16,40},{24,48},{32,56},{40,0},{48,8},{56,16},{1,25}... | collective-permute-start | bytes 344072 | tf_op jit(solution)/shard_map/ppermute | solution.py:19
  91.2 8.2 %collective-permute-start.22 = (f32[3,8,3072]{2,1,0:T(8,128)S(1)}, f32[3,8,3072]{2,1,0:T(8,128)S(1)}, u32[]{:S(2)}, u32[]{:S(2)}) collective-permute-start(f32[3,8,3072]{2,1,0:T(8,128)S(1)} %get-tuple-element.88), channel_id=1, source_target_pairs={{0,56},{8,0},{16,8},{24,16},{32,24},{40,32},{48,40},{56,48},{1,57}... | collective-permute-start | bytes 884744 | tf_op jit(solution)/shard_map/ppermute | solution.py:19
  93.7 5.7 %collective-permute-start.21 = (f32[2,8,3072]{2,1,0:T(8,128)S(1)}, f32[2,8,3072]{2,1,0:T(8,128)S(1)}, u32[]{:S(2)}, u32[]{:S(2)}) collective-permute-start(f32[2,8,3072]{2,1,0:T(8,128)S(1)} %get-tuple-element.87), channel_id=1, source_target_pairs={{0,8},{8,16},{16,24},{24,32},{32,40},{40,48},{48,56},{56,0},{1,9},... | collective-permute-start | bytes 589832 | tf_op jit(solution)/shard_map/ppermute | solution.py:19
  99.4 7.4 %collective-permute-start.24 = (f32[8,3072]{1,0:T(8,128)S(1)}, f32[8,3072]{1,0:T(8,128)S(1)}, u32[]{:S(2)}, u32[]{:S(2)}) collective-permute-start(f32[8,3072]{1,0:T(8,128)S(1)} %get-tuple-element.98), channel_id=1, source_target_pairs={{0,40},{8,48},{16,56},{24,0},{32,8},{40,16},{48,24},{56,32},{1,41}... | collective-permute-start | bytes 294920 | tf_op jit(solution)/shard_map/ppermute | solution.py:19
  100.0 7.7 %collective-permute-start.23 = (f32[8,3072]{1,0:T(8,128)S(1)}, f32[8,3072]{1,0:T(8,128)S(1)}, u32[]{:S(2)}, u32[]{:S(2)}) collective-permute-start(f32[8,3072]{1,0:T(8,128)S(1)} %get-tuple-element.97), channel_id=1, source_target_pairs={{0,24},{8,32},{16,40},{24,48},{32,56},{40,0},{48,8},{56,16},{1,25}... | collective-permute-start | bytes 294920 | tf_op jit(solution)/shard_map/ppermute | solution.py:19
  107.8 3.7 %collective-permute-start.26 = (f32[8,1536]{1,0:T(8,128)S(1)}, f32[8,1536]{1,0:T(8,128)S(1)}, u32[]{:S(2)}, u32[]{:S(2)}) collective-permute-start(f32[8,1536]{1,0:T(8,128)S(1)} %pad_maximum_fusion), channel_id=1, source_target_pairs={{0,192},{64,0},{128,64},{192,128},{1,193},{65,1},{129,65},{193,129... | collective-permute-start | bytes 147464 | tf_op jit(solution)/shard_map/ppermute | solution.py:19
  111.5 4.8 %collective-permute-start.27 = (f32[8,1536]{1,0:T(8,128)S(1)}, f32[8,1536]{1,0:T(8,128)S(1)}, u32[]{:S(2)}, u32[]{:S(2)}) collective-permute-start(f32[8,1536]{1,0:T(8,128)S(1)} %pad_maximum_fusion.1), channel_id=1, source_target_pairs={{0,64},{64,128},{128,192},{192,0},{1,65},{65,129},{129,193},{193,1... | collective-permute-start | bytes 147464 | tf_op jit(solution)/shard_map/ppermute | solution.py:19
  116.3 7.1 %collective-permute-start.28 = (f32[8,3,256]{2,0,1:T(8,128)S(1)}, f32[8,3,256]{2,0,1:T(8,128)S(1)}, u32[]{:S(2)}, u32[]{:S(2)}) collective-permute-start(f32[8,3,256]{2,0,1:T(8,128)S(1)} %dynamic-slice_bitcast_fusion), channel_id=1, source_target_pairs={{0,4},{4,0},{1,5},{5,1},{2,6},{6,2},{3,7},{7,3},{8,12},{12,8},{9,1... | collective-permute-start | bytes 73736 | tf_op jit(solution)/shard_map/ppermute | solution.py:23
  123.9 6.2 %collective-permute-start.29 = (f32[2,8,192]{2,1,0:T(8,128)S(1)}, f32[2,8,192]{2,1,0:T(8,128)S(1)}, u32[]{:S(2)}, u32[]{:S(2)}) collective-permute-start(f32[2,8,192]{2,1,0:T(8,128)S(1)} %get-tuple-element.113), channel_id=1, source_target_pairs={{0,3},{1,0},{2,1},{3,2},{4,7},{5,4},{6,5},{7,6},{8,11},{9,8},{10,9... | collective-permute-start | bytes 36872 | tf_op jit(solution)/shard_map/ppermute | solution.py:19
  128.5 6.7 %collective-permute-start.25 = (f32[8,1536]{1,0:T(8,128)S(1)}, f32[8,1536]{1,0:T(8,128)S(1)}, u32[]{:S(2)}, u32[]{:S(2)}) collective-permute-start(f32[8,1536]{1,0:T(8,128)S(1)} %slice.164), channel_id=1, source_target_pairs={{0,128},{64,192},{128,0},{192,64},{1,129},{65,193},{129,1},{193,65... | collective-permute-start | bytes 147464 | tf_op jit(solution)/shard_map/ppermute | solution.py:19
  129.4 4.1 %collective-permute-start.30 = (f32[2,8,192]{2,1,0:T(8,128)S(1)}, f32[2,8,192]{2,1,0:T(8,128)S(1)}, u32[]{:S(2)}, u32[]{:S(2)}) collective-permute-start(f32[2,8,192]{2,1,0:T(8,128)S(1)} %get-tuple-element.112), channel_id=1, source_target_pairs={{0,2},{1,3},{2,0},{3,1},{4,6},{5,7},{6,4},{7,5},{8,10},{9,11},{10,... | collective-permute-start | bytes 36872 | tf_op jit(solution)/shard_map/ppermute | solution.py:19
  129.4 4.1 %collective-permute-start.31 = (f32[2,8,192]{2,1,0:T(8,128)S(1)}, f32[2,8,192]{2,1,0:T(8,128)S(1)}, u32[]{:S(2)}, u32[]{:S(2)}) collective-permute-start(f32[2,8,192]{2,1,0:T(8,128)S(1)} %get-tuple-element.110), channel_id=1, source_target_pairs={{0,1},{1,2},{2,3},{3,0},{4,5},{5,6},{6,7},{7,4},{8,9},{9,10},{10,1... | collective-permute-start | bytes 36872 | tf_op jit(solution)/shard_map/ppermute | solution.py:19

commit v3 on v2

v3 whole, which is shorter than its diff:
```python
import functools

import jax
import jax.numpy as jnp
from jax import lax
from jax.experimental import pallas as pl
from jax.experimental.pallas import tpu as pltpu
from jax.sharding import Mesh, PartitionSpec as P

TILE = 128
MIB = 1024 * 1024
ANYWHERE = pl.BlockSpec(memory_space=pltpu.VMEM)
SOME = 10_000_000_000
LESS = 1_000_000_000
MORE = 6_000_000_000
AFTER = pl.BlockSpec(memory_space=pl.ANY)
SCALARS = pl.BlockSpec(memory_space=pltpu.SMEM)


def shift(value, axis, step, size):
    return lax.ppermute(value, axis, [(i, (i + step) % size) for i in range(size)])


def sibling(value):
    return lax.ppermute(value, "core", [(0, 1), (1, 0)])


def times_transposed(left, right):
    return lax.dot_general(left, right, (((1,), (1,)), ((), ())), preferred_element_type=jnp.float32)


def diagonal_kernel(place, screen, slab, keep, give, total):
    step = pl.program_id(0)
    core, row, aux = place[0], place[1], place[2]
    group, mrows, _ = slab.shape
    depth = pl.num_programs(0) * group
    tiles = mrows // TILE

    def masked(q):
        at = aux * depth + step * group + q
        parts = [
            slab[q, t * TILE : (t + 1) * TILE, :] * screen[at, row * tiles + t].astype(jnp.bfloat16)
            for t in range(tiles)
        ]
        return jnp.concatenate(parts, axis=0)

    rows = jnp.concatenate([masked(q) for q in range(group)], axis=1)
    product = times_transposed(rows, rows)

    @pl.when(step == 0)
    def _():
        total[...] = product.reshape(total.shape)

    @pl.when(step > 0)
    def _():
        total[...] += product.reshape(total.shape)

    @pl.when(step == pl.num_programs(0) - 1)
    def _():
        keep[...] = total[:, core].reshape(keep.shape)
        give[...] = total[:, 1 - core].reshape(give.shape)


def diagonal(place, screen, block, zs, group=4):
    depth, rows, width = block.shape
    half = jax.ShapeDtypeStruct((rows // 2, rows), jnp.float32)
    whole = pl.BlockSpec((rows // 2, rows), lambda q: (0, 0))
    return pl.pallas_call(
        diagonal_kernel,
        grid=(depth // group,),
        in_specs=[SCALARS, SCALARS, pl.BlockSpec((group, rows, width), lambda q: (q, 0, 0))],
        out_specs=[whole, whole],
        scratch_shapes=[pltpu.VMEM((zs, 2, rows // zs // 2, rows), jnp.float32)],
        out_shape=[half, half],
        compiler_params=pltpu.CompilerParams(vmem_limit_bytes=16 * MIB),
        cost_estimate=pl.CostEstimate(flops=1, bytes_accessed=1, transcendentals=0),
        name="diagonal",
    )(place, screen, block)


def store_by_aux(aux, product, outs, row, col):
    xs = len(outs)
    grouped = product.reshape(-1, xs, 8, product.shape[1])
    size = grouped.shape[0] * 8
    for there in range(xs):
        piece = grouped[:, there].reshape(size, -1)
        for d in range(xs):
            @pl.when(lax.rem(aux + d, xs) == there)
            def _():
                outs[d][row : row + size, col : col + piece.shape[1]] = piece


def wide(refs, core=None):
    parts = []
    for ref in refs:
        for q in range(ref.shape[0]):
            part = ref[q] if core is None else ref[q, :, core]
            parts.append(part.reshape(-1, part.shape[-1]))
    return jnp.concatenate(parts, axis=1)


def split_kernel(place, kept, got, *outs):
    store_by_aux(place[2], kept[...] + got[...], outs, 0, 0)


def early_kernel(place, mine, mine2, above, above2, below, below2, *outs):
    core, aux = place[0], place[2]
    n = above.shape[1] * above.shape[2] * above.shape[3]
    own, up = wide((mine, mine2), core), wide((above, above2), core)
    store_by_aux(aux, times_transposed(own, wide((above, above2))), outs, 0, 0)
    both = times_transposed(jnp.concatenate([up, own], axis=0), wide((below, below2)))
    store_by_aux(aux, both[: up.shape[0]], outs, 0, n)
    store_by_aux(aux, both[up.shape[0] :], outs, 0, 2 * n)


def late_kernel(place, below, below2, mine, mine2, above, above2, across, across2, _, *outs):
    core, aux = place[0], place[2]
    right = wide((across, across2))
    for at, slabs in enumerate(((below, below2), (mine, mine2), (above, above2))):
        product = times_transposed(wide(slabs, core), right)
        store_by_aux(aux, product, outs, at * (product.shape[0] // len(outs)), 0)


def pairs(kernel, place, operands, shape, xs, after=(), flops=1, limit=24 * MIB):
    out = jax.ShapeDtypeStruct(shape, jnp.float32)
    return pl.pallas_call(
        kernel,
        in_specs=[SCALARS] + [ANYWHERE] * len(operands) + [AFTER] * len(after),
        out_specs=[ANYWHERE] * xs,
        out_shape=[out] * xs,
        compiler_params=pltpu.CompilerParams(vmem_limit_bytes=limit),
        cost_estimate=pl.CostEstimate(flops=flops, bytes_accessed=1, transcendentals=0),
        name=kernel.__name__,
    )(place, *operands, *after)


def spread_kernel(ys, place, rows, out):
    peers = out.shape[0] // ys
    n = rows.shape[1] // 7
    size = n // peers
    out[...] = jnp.zeros_like(out)
    for step in range(1, ys):
        first = lax.rem(place[1] + step, ys) * peers
        for k in range(peers):
            begin = (ys - 1 + step) * n + k * size
            out[first + k, :, :size] = rows[:, begin : begin + size]


def finish_kernel(ys, place, rows, pieces, out):
    peers = pieces.shape[0] // ys
    n = out.shape[1] // ys
    zs = n // peers // 8
    for step in range(ys):
        owner = lax.rem(place[1] + step, ys)
        block = rows[:, step * n : (step + 1) * n]
        if step:
            came = [pieces[owner * peers + k] for k in range(peers)]
            parts = [came[k][:, at * 8 : (at + 1) * 8] for at in range(zs) for k in range(peers)]
            block = block + jnp.concatenate(parts, axis=1)
        out[:, pl.ds(pl.multiple_of(owner * n, n), n)] = block


def small(kernel, shape, *operands):
    ys = 4
    return pl.pallas_call(
        functools.partial(kernel, ys),
        in_specs=[SCALARS] + [ANYWHERE] * (len(operands) - 1),
        out_specs=ANYWHERE,
        out_shape=jax.ShapeDtypeStruct(shape, jnp.float32),
        compiler_params=pltpu.CompilerParams(vmem_limit_bytes=4 * MIB),
        cost_estimate=pl.CostEstimate(flops=1, bytes_accessed=1, transcendentals=0),
        name=kernel.__name__,
    )(*operands)


def over_aux(parts, xs):
    there = {d: shift(parts[d], "aux", d, xs) for d in (2, 1, 3)}
    return [parts[0], there[1], there[2], there[3]]


SLOTS = ((0,), (3,), (5,), (1, 6), (7, 4, 2))


def turn(block, zs):
    rows, cols = block.shape
    turned = block.T.reshape(zs, cols // zs // 8, 8, rows)
    return [[turned[at, k] for k in range(turned.shape[1])] for at in range(zs)]


def send_out(place, buffer, outs):
    zs = buffer.shape[0]
    for out, steps in zip(outs, SLOTS):
        for at, step in enumerate(steps):
            out[at] = buffer[lax.rem(place[3] + step, zs)]


def pack_kernel(place, *refs):
    diags, (early, third, middle, up, down), outs, buffer = refs[:4], refs[4:9], refs[9:-1], refs[-1]
    zs = buffer.shape[0]
    n = third.shape[1]
    buffer[:, :, :n] = (diags[0][...] + diags[1][...] + diags[2][...] + diags[3][...]).reshape(zs, 8, n)
    blocks = (early[:, :n] + up[...], third[...] + middle[...], early[:, 2 * n :] + down[...])
    for at, block in enumerate(blocks):
        buffer[:, :, (1 + at) * n : (2 + at) * n] = block.reshape(zs, 8, n)
        size = block.shape[0]
        for owner, pieces in enumerate(turn(block, zs)):
            for k, piece in enumerate(pieces):
                lane = (4 + at) * n + k * size
                buffer[owner, :, lane : lane + size] = piece
    send_out(place, buffer, outs)


def pack(place, *operands):
    zs = 8
    width = 7 * operands[0].shape[1]
    shapes = [(len(steps), 8, width) for steps in SLOTS]
    return pl.pallas_call(
        pack_kernel,
        in_specs=[SCALARS] + [ANYWHERE] * len(operands),
        out_specs=[ANYWHERE] * len(shapes),
        out_shape=[jax.ShapeDtypeStruct(s, jnp.float32) for s in shapes],
        scratch_shapes=[pltpu.VMEM((zs, 8, width), jnp.float32)],
        compiler_params=pltpu.CompilerParams(vmem_limit_bytes=8 * MIB),
        cost_estimate=pl.CostEstimate(flops=1, bytes_accessed=1, transcendentals=0),
        name="pack",
    )(place, *operands)


def first_z(packed):
    zs = 8
    here, forward, backward, up, down = packed
    up, down = shift(up, "z", 1, zs), shift(down, "z", -1, zs)
    return here[0] + up[0] + down[0], forward[0] + down[2], backward[0] + up[1] + down[1]


def second_z(here, forward, backward):
    zs = 8
    return here, shift(forward, "z", 3, zs), shift(backward, "z", -3, zs)


def total_kernel(waits, *refs):
    parts, out = refs[: len(refs) - 1 - waits], refs[-1]
    value = parts[0][...]
    for part in parts[1:]:
        value = value + part[...]
    out[...] = value


def total(parts, after=(), flops=1):
    return pl.pallas_call(
        functools.partial(total_kernel, len(after)),
        in_specs=[ANYWHERE] * len(parts) + [AFTER] * len(after),
        out_specs=ANYWHERE,
        out_shape=jax.ShapeDtypeStruct(parts[0].shape, parts[0].dtype),
        compiler_params=pltpu.CompilerParams(vmem_limit_bytes=4 * MIB),
        cost_estimate=pl.CostEstimate(flops=flops, bytes_accessed=1, transcendentals=0),
        name="total",
    )(*parts, *after)


def body(half_transformed, screen):
    qrows, mrows, icols = half_transformed.shape
    ys, zs, xs = 4, 8, 4
    quarter = qrows // ys
    row, z = lax.axis_index("row"), lax.axis_index("z")
    core, aux = lax.axis_index("core"), lax.axis_index("aux")
    place = jnp.stack([core, row, aux, z]).astype(jnp.int32)
    n = mrows
    tiles = mrows // TILE
    local = lax.dynamic_slice(screen, (aux * qrows, row * tiles), (qrows, tiles))
    keep = jnp.repeat(local, TILE, axis=1).astype(jnp.bfloat16)

    def slab(block, step):
        first = lax.rem(row + step, ys) * quarter
        part = lax.dynamic_slice(block, (first, 0, 0), (quarter, mrows, icols))
        return part * lax.dynamic_slice(keep, (first, 0), (quarter, mrows))[:, :, None]

    to_up, to_down = slab(half_transformed, 1), slab(half_transformed, 3)
    block, to_up, to_down = lax.optimization_barrier((half_transformed, to_up, to_down))
    below = shift(to_up, "row", 1, ys)
    above = shift(to_down, "row", -1, ys)
    mine, far = slab(block, 0), slab(block, 2)
    mine2 = sibling(mine)
    kept, given = diagonal(place, screen, block, zs)
    diag = pairs(split_kernel, place, (kept, sibling(given)), (zs * 8, n), xs, limit=4 * MIB)
    diag = over_aux(diag, xs)
    below, above, far, diag = lax.optimization_barrier((below, above, far, diag))
    across = shift(far, "row", 2, ys)

    def grouped(*slabs):
        return [s.reshape(quarter, zs, 2, n // zs // 2, icols) for s in slabs]

    mine, mine2 = grouped(mine, mine2)
    below, above = grouped(below, sibling(below)), grouped(above, sibling(above))
    early_parts = pairs(early_kernel, place, (mine, mine2, *above, *below), (zs * 8, 3 * n), xs)
    early = total(over_aux(early_parts, xs), flops=SOME)
    third = shift(early[:, n : 2 * n], "row", 1, ys)
    late_parts = pairs(
        late_kernel,
        place,
        (*below, mine, mine2, *above, *grouped(across, sibling(across))),
        (3 * zs * 8, n),
        xs,
        (early,),
    )
    late = total(over_aux(late_parts, xs), (third,))
    down, middle, up = late.reshape(3, zs * 8, n)
    up, down = shift(up, "row", 1, ys), shift(down, "row", -1, ys)
    rows = first_z(pack(place, *diag, early, third, middle, up, down))
    here, forward, backward = second_z(*rows)
    rows = here + forward + backward
    peers = 2 * xs
    pieces = small(spread_kernel, (ys * peers, 8, 128), place, rows)
    pieces = lax.all_to_all(pieces, ("row", "core", "aux"), 0, 0, tiled=True)
    return small(finish_kernel, (8, ys * n), place, rows, pieces)


def solution(mesh):
    rows, cols, aux = mesh.devices.shape
    split = Mesh(mesh.devices.reshape(rows, cols // 2, 2, aux), ("row", "z", "core", "aux"))
    in_specs = (P("aux", "row", ("z", "core")), P())
    out_specs = P(("row", "z", "core", "aux"), None)
    return jax.shard_map(body, mesh=split, in_specs=in_specs, out_specs=out_specs, check_vma=False)
```

time: 138 us -> 135 us (0.978); the launches traced: 136 us -> 134 us
  blocking collectives: 0 us -> 20.7 us
  starting transfers between devices: 59.4 us -> 42.2 us
  local copies, waits for them, and re-layouts: 5.19 us -> 2.52 us
  waiting for transfers between devices: 52.3 us -> 50.1 us
    all_to_all x0 -> x1, blocking collectives: none -> 20.7 us  [body(): pieces = lax.all_to_all(pieces, ('row', 'core', 'aux'), 0, 0, tiled=True)]
    ppermute x26 -> x19, starting transfers between devices: 43.4 us -> 32.5 us  [shift(): lax.ppermute(value, axis, [(i, (i + step) % size) for i in range(size)])]
    ppermute x6 -> x5, starting transfers between devices: 16.1 us -> 9.71 us  [sibling(): return lax.ppermute(value, 'core', [(0, 1), (1, 0)])]
    ppermute x26 -> x19, waiting for transfers between devices: 48.3 us -> 45.6 us  [shift(): lax.ppermute(value, axis, [(i, (i + step) % size) for i in range(size)])]
    pallas_call x3 -> x5, Pallas kernels: 2.56 us -> 3.23 us  [the longest x2 2.05 us: small(): pl.pallas_call(functools.partial(kernel, ys), in_specs=[SCALARS] + [ANYWH...]
    ppermute x6 -> x5, waiting for transfers between devices: 4.01 us -> 4.5 us  [sibling(): return lax.ppermute(value, 'core', [(0, 1), (1, 0)])]
  transfers between devices with their start and end apart: 32 -> 24, of which waited for: 16 -> 12; matrix products, arithmetic and copies ran while one was open for 2% -> 1% of each run, Pallas kernels for 8% -> 6%
where the time goes in v3:
time: 135 us; the launch traced here: 134 us
  waiting for transfers between devices  50.1 us (37%)
  starting transfers between devices  42.2 us (31%)
  blocking collectives  20.7 us (15%)
  Pallas kernels  14.3 us (11%)
  other arithmetic  4.37 us (3%)
  local copies, waits for them, and re-layouts  2.52 us (2%)
    ppermute x19, waiting for transfers between devices, shift(): lax.ppermute(value, axis, [(i, (i + step) % size) for i in range(size)])  45.6 us
    ppermute x19, starting transfers between devices, shift(): lax.ppermute(value, axis, [(i, (i + step) % size) for i in range(size)])  32.5 us
    all_to_all x1, blocking collectives, body(): pieces = lax.all_to_all(pieces, ('row', 'core', 'aux'), 0, 0, tiled=True)  20.7 us
    ppermute x5, starting transfers between devices, sibling(): return lax.ppermute(value, 'core', [(0, 1), (1, 0)])  9.71 us
    pallas_call x3, Pallas kernels, pairs(): pl.pallas_call(kernel, in_specs=[SCALARS] + [ANYWHERE] * len(operands) +...  6.49 us
    pallas_call x1, Pallas kernels, diagonal(): pl.pallas_call(diagonal_kernel, grid=(depth // group,), in_specs=[SCALARS...  4.62 us
    ppermute x5, waiting for transfers between devices, sibling(): return lax.ppermute(value, 'core', [(0, 1), (1, 0)])  4.5 us
    mul x2, other arithmetic, slab(): part * lax.dynamic_slice(keep, (first, 0), (quarter, mrows))[:, :, None]  3.4 us
  transfers between devices with their start and end apart: 24, of which 12 were waited for; matrix products, arithmetic and copies ran while one was open for 1% of the time, Pallas kernels for 6%

profile of v3, /device:TPU:1, one launch (start us, length us, event | category | flops | bytes accessed | tf_op | source)
XLA Modules:
  0.0 134.5 jit_solution(665570863483991295)
XLA Ops:
  0.0 0.8 dynamic-slice_convert_fusion
  0.8 0.1 copy.3
  0.9 0.1 broadcast_in_dim.2
  1.1 2.7 %dynamic-slice_multiply_fusion.2 = (bf16[4,512,256]{2,1,0:T(8,128)(2,1)S(1)}, bf16[4,512,256]{2,1,0:T(8,128)(2,1)}) fusion(bf16[16,512,256]{2,1,0:T(8,128)(2,1)} %slab, s32[]{:T(128)S(6)} %select_n.25, bf16[4,512]{1,0:T(4,128)(2,1)S(1)} %get-tuple-element.74, bf16[4,512]{1,0:T(4,128)(2,1)S(1)} %get-tuple-element.75, s32[]{:T(128)S(6)} %select_n.22), kind=kLoop, calls=%fused_computation.2 | loop fusion | flops 1048576 | bytes 4202504 | tf_op jit(solution)/shard_map/mul | solution.py:276
  3.8 2.1 %collective-permute-start = (bf16[4,512,256]{2,1,0:T(8,128)(2,1)}, bf16[4,512,256]{2,1,0:T(8,128)(2,1)S(1)}, u32[]{:S(2)}, u32[]{:S(2)}) collective-permute-start(bf16[4,512,256]{2,1,0:T(8,128)(2,1)} %get-tuple-element.34), channel_id=1, source_target_pairs={{0,64},{64,128},{128,192},{192,0},{1,65},{65,129},{129,193},{193,1... | collective-permute-start | bytes 3145736 | tf_op jit(solution)/shard_map/ppermute | solution.py:21
  5.9 1.4 %collective-permute-start.1 = (bf16[4,512,256]{2,1,0:T(8,128)(2,1)S(1)}, bf16[4,512,256]{2,1,0:T(8,128)(2,1)S(1)}, u32[]{:S(2)}, u32[]{:S(2)}) collective-permute-start(bf16[4,512,256]{2,1,0:T(8,128)(2,1)S(1)} %get-tuple-element.35), channel_id=1, source_target_pairs={{0,192},{64,0},{128,64},{192,128},{1,193},{65,1},{129,65},{193,129... | collective-permute-start | bytes 3145736 | tf_op jit(solution)/shard_map/ppermute | solution.py:21
  7.4 0.1 copy.4.screen
  7.5 0.1 pad_add_fusion.place
  7.5 2.2 %copy-done = bf16[16,512,256]{2,1,0:T(8,128)(2,1)S(1)} copy-done((bf16[16,512,256]{2,1,0:T(8,128)(2,1)S(1)}, bf16[16,512,256]{2,1,0:T(8,128)(2,1)}, u32[]{:S(2)}) %copy-start) | copy-done | bytes 4194328
  9.7 4.6 %diagonal.1 = (f32[256,512]{1,0:T(8,128)S(1)}, f32[256,512]{1,0:T(8,128)S(1)}) custom-call(s32[4]{0:T(128)S(1)} %pad_add_fusion.place, s32[64,16]{1,0:T(8,128)S(1)} %copy.4.screen, bf16[16,512,256]{2,1,0:T(8,128)(2,1)S(1)} %copy-done), custom_call_target="tpu_custom_call" | custom-call | flops 1 | bytes 1 | tf_op jit(solution)/shard_map/diagonal/pallas_call | solution.py:68
  14.4 3.0 %collective-permute-start.2 = (f32[256,512]{1,0:T(8,128)S(1)}, f32[256,512]{1,0:T(8,128)S(1)}, u32[]{:S(2)}, u32[]{:S(2)}) collective-permute-start(f32[256,512]{1,0:T(8,128)S(1)} %get-tuple-element.38), channel_id=1, source_target_pairs={{0,4},{4,0},{1,5},{5,1},{2,6},{6,2},{3,7},{7,3},{8,12},{12,8},{9,1... | collective-permute-start | bytes 1572872 | tf_op jit(solution)/shard_map/ppermute | solution.py:25
  17.4 1.5 %collective-permute-done.2.got = f32[256,512]{1,0:T(8,128)S(1)} collective-permute-done((f32[256,512]{1,0:T(8,128)S(1)}, f32[256,512]{1,0:T(8,128)S(1)}, u32[]{:S(2)}, u32[]{:S(2)}) %collective-permute-start.2) | collective-permute-done | bytes 524320 | tf_op jit(solution)/shard_map/ppermute | solution.py:25
  18.9 0.7 split_kernel.1
  19.6 0.1 collective-permute-start.3
  19.7 1.9 %collective-permute-start.4 = (f32[64,512]{1,0:T(8,128)S(1)}, f32[64,512]{1,0:T(8,128)S(1)}, u32[]{:S(2)}, u32[]{:S(2)}) collective-permute-start(f32[64,512]{1,0:T(8,128)S(1)} %get-tuple-element.41), channel_id=1, source_target_pairs={{0,2},{1,3},{2,0},{3,1},{4,6},{5,7},{6,4},{7,5},{8,10},{9,11},{10,... | collective-permute-start | bytes 393224 | tf_op jit(solution)/shard_map/ppermute | solution.py:21
  21.6 1.2 collective-permute-start.5
  22.7 0.7 dynamic-slice_multiply_fusion
  23.4 2.9 %collective-permute-done.3.refs_1_ = f32[64,512]{1,0:T(8,128)S(1)} collective-permute-done((f32[64,512]{1,0:T(8,128)S(1)}, f32[64,512]{1,0:T(8,128)S(1)}, u32[]{:S(2)}, u32[]{:S(2)}) %collective-permute-start.3) | collective-permute-done | bytes 131104 | tf_op jit(solution)/shard_map/ppermute | solution.py:21
  26.3 3.3 %collective-permute-start.6 = (bf16[4,512,256]{2,1,0:T(8,128)(2,1)S(1)}, bf16[4,512,256]{2,1,0:T(8,128)(2,1)S(1)}, u32[]{:S(2)}, u32[]{:S(2)}) collective-permute-start(bf16[4,512,256]{2,1,0:T(8,128)(2,1)S(1)} %get-tuple-element.63), channel_id=1, source_target_pairs={{0,4},{4,0},{1,5},{5,1},{2,6},{6,2},{3,7},{7,3},{8,12},{12,8},{9,1... | collective-permute-start | bytes 3145736 | tf_op jit(solution)/shard_map/ppermute | solution.py:25
  29.6 0.0 collective-permute-done.4.refs_2_
  29.6 0.0 collective-permute-done.5.refs_3_
  29.6 0.0 collective-permute-done
  29.6 0.0 collective-permute-done.1
  29.6 2.1 %collective-permute-start.7 = (bf16[4,512,256]{2,1,0:T(8,128)(2,1)S(1)}, bf16[4,512,256]{2,1,0:T(8,128)(2,1)S(1)}, u32[]{:S(2)}, u32[]{:S(2)}) collective-permute-start(bf16[4,512,256]{2,1,0:T(8,128)(2,1)S(1)} %collective-permute-done.1), channel_id=1, source_target_pairs={{0,4},{4,0},{1,5},{5,1},{2,6},{6,2},{3,7},{7,3},{8,12},{12,8},{9,1... | collective-permute-start | bytes 3145736 | tf_op jit(solution)/shard_map/ppermute | solution.py:25
  31.7 0.0 collective-permute-start.8
  31.7 2.4 %collective-permute-start.13 = (bf16[4,512,256]{2,1,0:T(8,128)(2,1)S(1)}, bf16[4,512,256]{2,1,0:T(8,128)(2,1)S(1)}, u32[]{:S(2)}, u32[]{:S(2)}) collective-permute-start(bf16[4,512,256]{2,1,0:T(8,128)(2,1)S(1)} %get-tuple-element.53), channel_id=1, source_target_pairs={{0,128},{64,192},{128,0},{192,64},{1,129},{65,193},{129,1},{193,65... | collective-permute-start | bytes 3145736 | tf_op jit(solution)/shard_map/ppermute | solution.py:21
  34.1 0.0 collective-permute-done.6
  34.1 0.0 collective-permute-done.7
  34.1 1.3 collective-permute-done.8
  35.5 2.8 %early_kernel.1 = (f32[64,1536]{1,0:T(8,128)S(1)}, f32[64,1536]{1,0:T(8,128)S(1)}, f32[64,1536]{1,0:T(8,128)S(1)}, f32[64,1536]{1,0:T(8,128)S(1)}) custom-call(s32[4]{0:T(128)S(1)} %pad_add_fusion.place, bf16[4,8,2,32,256]{4,3,2,1,0:T(8,128)(2,1)S(1)} %bitcast.26, bf16[4,8,2,32,256]{4,3,2,1,0:T(8,128)(2,1)S(1)} %bitcast.32, ...), custom_call_target="tpu_custom_call" | custom-call | flops 1 | bytes 1 | tf_op jit(solution)/shard_map/early_kernel/pallas_call | solution.py:126
  38.3 2.8 %collective-permute-start.10 = (f32[64,1536]{1,0:T(8,128)S(1)}, f32[64,1536]{1,0:T(8,128)S(1)}, u32[]{:S(2)}, u32[]{:S(2)}) collective-permute-start(f32[64,1536]{1,0:T(8,128)S(1)} %get-tuple-element.51), channel_id=1, source_target_pairs={{0,2},{1,3},{2,0},{3,1},{4,6},{5,7},{6,4},{7,5},{8,10},{9,11},{10,... | collective-permute-start | bytes 1179656 | tf_op jit(solution)/shard_map/ppermute | solution.py:21
  41.2 0.9 collective-permute-start.11
  42.0 0.6 collective-permute-start.9
  42.6 14.8 %collective-permute-done.13 = bf16[4,512,256]{2,1,0:T(8,128)(2,1)S(1)} collective-permute-done((bf16[4,512,256]{2,1,0:T(8,128)(2,1)S(1)}, bf16[4,512,256]{2,1,0:T(8,128)(2,1)S(1)}, u32[]{:S(2)}, u32[]{:S(2)}) %collective-permute-start.13) | collective-permute-done | bytes 1048608 | tf_op jit(solution)/shard_map/ppermute | solution.py:21
  57.4 1.4 %collective-permute-start.14 = (bf16[4,512,256]{2,1,0:T(8,128)(2,1)S(1)}, bf16[4,512,256]{2,1,0:T(8,128)(2,1)S(1)}, u32[]{:S(2)}, u32[]{:S(2)}) collective-permute-start(bf16[4,512,256]{2,1,0:T(8,128)(2,1)S(1)} %collective-permute-done.13), channel_id=1, source_target_pairs={{0,4},{4,0},{1,5},{5,1},{2,6},{6,2},{3,7},{7,3},{8,12},{12,8},{9,1... | collective-permute-start | bytes 3145736 | tf_op jit(solution)/shard_map/ppermute | solution.py:25
  58.8 0.0 collective-permute-done.10.refs_2_
  58.8 0.0 collective-permute-done.11.refs_3_
  58.8 0.6 collective-permute-done.9.refs_1_
  59.4 0.1 total.2._.refs_4_
  59.5 1.6 %collective-permute-done.14 = bf16[4,512,256]{2,1,0:T(8,128)(2,1)S(1)} collective-permute-done((bf16[4,512,256]{2,1,0:T(8,128)(2,1)S(1)}, bf16[4,512,256]{2,1,0:T(8,128)(2,1)S(1)}, u32[]{:S(2)}, u32[]{:S(2)}) %collective-permute-start.14) | collective-permute-done | bytes 1048608 | tf_op jit(solution)/shard_map/ppermute | solution.py:25
  61.1 3.0 %late_kernel.1 = (f32[192,512]{1,0:T(8,128)S(1)}, f32[192,512]{1,0:T(8,128)S(1)}, f32[192,512]{1,0:T(8,128)S(1)}, f32[192,512]{1,0:T(8,128)S(1)}) custom-call(s32[4]{0:T(128)S(1)} %pad_add_fusion.place, bf16[4,8,2,32,256]{4,3,2,1,0:T(8,128)(2,1)S(1)} %bitcast.29, bf16[4,8,2,32,256]{4,3,2,1,0:T(8,128)(2,1)S(1)} %bitcast.37, ...), custom_call_target="tpu_custom_call" | custom-call | flops 1 | bytes 1 | tf_op jit(solution)/shard_map/late_kernel/pallas_call | solution.py:126
  64.0 1.3 collective-permute-start.15
  65.3 2.5 %collective-permute-start.16 = (f32[192,512]{1,0:T(8,128)S(1)}, f32[192,512]{1,0:T(8,128)S(1)}, u32[]{:S(2)}, u32[]{:S(2)}) collective-permute-start(f32[192,512]{1,0:T(8,128)S(1)} %get-tuple-element.56), channel_id=1, source_target_pairs={{0,2},{1,3},{2,0},{3,1},{4,6},{5,7},{6,4},{7,5},{8,10},{9,11},{10,... | collective-permute-start | bytes 1179656 | tf_op jit(solution)/shard_map/ppermute | solution.py:21
  67.8 1.2 collective-permute-start.17
  69.0 1.2 collective-permute-start.12
  70.1 4.2 %collective-permute-done.12.refs_4_.refs_5_ = f32[64,512]{1,0:T(8,128)S(1)} collective-permute-done((f32[64,512]{1,0:T(8,128)S(1)}, f32[64,512]{1,0:T(8,128)S(1)}, u32[]{:S(2)}, u32[]{:S(2)}) %collective-permute-start.12) | collective-permute-done | bytes 131104 | tf_op jit(solution)/shard_map/ppermute | solution.py:21
  74.4 1.3 collective-permute-done.15.refs_1_
  75.7 9.4 %collective-permute-done.16.refs_2_ = f32[192,512]{1,0:T(8,128)S(1)} collective-permute-done((f32[192,512]{1,0:T(8,128)S(1)}, f32[192,512]{1,0:T(8,128)S(1)}, u32[]{:S(2)}, u32[]{:S(2)}) %collective-permute-start.16) | collective-permute-done | bytes 393248 | tf_op jit(solution)/shard_map/ppermute | solution.py:21
  85.1 0.0 collective-permute-done.17.refs_3_
  85.1 0.1 total.3
  85.2 1.2 collective-permute-start.18
  86.4 1.6 %collective-permute-start.19 = (f32[64,512]{1,0:T(8,128)S(1)}, f32[64,512]{1,0:T(8,128)S(1)}, u32[]{:S(2)}, u32[]{:S(2)}) collective-permute-start(f32[64,512]{1,0:T(8,128)S(1)} %get-tuple-element.67), channel_id=1, source_target_pairs={{0,192},{64,0},{128,64},{192,128},{1,193},{65,1},{129,65},{193,129... | collective-permute-start | bytes 393224 | tf_op jit(solution)/shard_map/ppermute | solution.py:21
  88.0 2.4 %collective-permute-done.18.refs_7_ = f32[64,512]{1,0:T(8,128)S(1)} collective-permute-done((f32[64,512]{1,0:T(8,128)S(1)}, f32[64,512]{1,0:T(8,128)S(1)}, u32[]{:S(2)}, u32[]{:S(2)}) %collective-permute-start.18) | collective-permute-done | bytes 131104 | tf_op jit(solution)/shard_map/ppermute | solution.py:21
  90.3 0.0 collective-permute-done.19.refs_8_
  90.3 1.0 pack.1
  91.3 5.7 %collective-permute-start.21 = (f32[3,8,3584]{2,1,0:T(8,128)S(1)}, f32[3,8,3584]{2,1,0:T(8,128)S(1)}, u32[]{:S(2)}, u32[]{:S(2)}) collective-permute-start(f32[3,8,3584]{2,1,0:T(8,128)S(1)} %get-tuple-element.60), channel_id=1, source_target_pairs={{0,56},{8,0},{16,8},{24,16},{32,24},{40,32},{48,40},{56,48},{1,57}... | collective-permute-start | bytes 1032200 | tf_op jit(solution)/shard_map/ppermute | solution.py:21
  97.0 6.1 %collective-permute-done.20 = f32[2,8,3584]{2,1,0:T(8,128)S(1)} collective-permute-done((f32[2,8,3584]{2,1,0:T(8,128)S(1)}, f32[2,8,3584]{2,1,0:T(8,128)S(1)}, u32[]{:S(2)}, u32[]{:S(2)}) %collective-permute-start.20) | collective-permute-done | bytes 229408 | tf_op jit(solution)/shard_map/ppermute | solution.py:21
  103.1 0.0 collective-permute-done.21
  103.1 1.4 %collective-permute-start.22 = (f32[8,3584]{1,0:T(8,128)S(1)}, f32[8,3584]{1,0:T(8,128)S(1)}, u32[]{:S(2)}, u32[]{:S(2)}) collective-permute-start(f32[8,3584]{1,0:T(8,128)S(1)} %get-tuple-element.70), channel_id=1, source_target_pairs={{0,24},{8,32},{16,40},{24,48},{32,56},{40,0},{48,8},{56,16},{1,25}... | collective-permute-start | bytes 344072 | tf_op jit(solution)/shard_map/ppermute | solution.py:21
  104.5 3.2 %collective-permute-start.23 = (f32[8,3584]{1,0:T(8,128)S(1)}, f32[8,3584]{1,0:T(8,128)S(1)}, u32[]{:S(2)}, u32[]{:S(2)}) collective-permute-start(f32[8,3584]{1,0:T(8,128)S(1)} %get-tuple-element.71), channel_id=1, source_target_pairs={{0,40},{8,48},{16,56},{24,0},{32,8},{40,16},{48,24},{56,32},{1,41}... | collective-permute-start | bytes 344072 | tf_op jit(solution)/shard_map/ppermute | solution.py:21
  107.7 4.0 %collective-permute-done.22 = f32[8,3584]{1,0:T(8,128)S(1)} collective-permute-done((f32[8,3584]{1,0:T(8,128)S(1)}, f32[8,3584]{1,0:T(8,128)S(1)}, u32[]{:S(2)}, u32[]{:S(2)}) %collective-permute-start.22) | collective-permute-done | bytes 114720 | tf_op jit(solution)/shard_map/ppermute | solution.py:21
  111.7 0.6 spread_kernel.1
  112.3 20.7 %all_to_all.5.pieces = f32[32,8,128]{2,1,0:T(8,128)S(1)} all-to-all(f32[32,8,128]{2,1,0:T(8,128)S(1)} %spread_kernel.1), channel_id=1, replica_groups=mesh['row'=4,'z'=8,'core'=2,'aux'=4] {'row','core','aux'}, dimensions={0} | all-to-all | bytes 262144 | tf_op jit(solution)/shard_map/all_to_all | solution.py:314
  133.1 1.4 %finish_kernel.1 = f32[8,2048]{1,0:T(8,128)} custom-call(s32[4]{0:T(128)S(1)} %pad_add_fusion.place, f32[8,3584]{1,0:T(8,128)S(1)} %fusion.4.rows, f32[32,8,128]{2,1,0:T(8,128)S(1)} %all_to_all.5.pieces), custom_call_target="tpu_custom_call" | custom-call | flops 1 | bytes 1 | tf_op jit(solution)/shard_map/finish_kernel/pallas_call | solution.py:165
  (11 shorter events, 0.1 us)
Async XLA Ops:
  0.0 7.4 %copy-start.1 = (s32[64,16]{0,1:T(8,128)S(1)}, s32[64,16]{0,1:T(8,128)}, u32[]{:S(2)}) copy-start(s32[64,16]{0,1:T(8,128)} %param.3) | copy-start | bytes 12292
  3.8 25.8 %collective-permute-start = (bf16[4,512,256]{2,1,0:T(8,128)(2,1)}, bf16[4,512,256]{2,1,0:T(8,128)(2,1)S(1)}, u32[]{:S(2)}, u32[]{:S(2)}) collective-permute-start(bf16[4,512,256]{2,1,0:T(8,128)(2,1)} %get-tuple-element.34), channel_id=1, source_target_pairs={{0,64},{64,128},{128,192},{192,0},{1,65},{65,129},{129,193},{193,1... | collective-permute-start | bytes 3145736 | tf_op jit(solution)/shard_map/ppermute | solution.py:21
  5.9 23.7 %collective-permute-start.1 = (bf16[4,512,256]{2,1,0:T(8,128)(2,1)S(1)}, bf16[4,512,256]{2,1,0:T(8,128)(2,1)S(1)}, u32[]{:S(2)}, u32[]{:S(2)}) collective-permute-start(bf16[4,512,256]{2,1,0:T(8,128)(2,1)S(1)} %get-tuple-element.35), channel_id=1, source_target_pairs={{0,192},{64,0},{128,64},{192,128},{1,193},{65,1},{129,65},{193,129... | collective-permute-start | bytes 3145736 | tf_op jit(solution)/shard_map/ppermute | solution.py:21
  7.5 2.2 %copy-start = (bf16[16,512,256]{2,1,0:T(8,128)(2,1)S(1)}, bf16[16,512,256]{2,1,0:T(8,128)(2,1)}, u32[]{:S(2)}) copy-start(bf16[16,512,256]{2,1,0:T(8,128)(2,1)} %slab) | copy-start | bytes 12582916
  14.4 4.5 %collective-permute-start.2 = (f32[256,512]{1,0:T(8,128)S(1)}, f32[256,512]{1,0:T(8,128)S(1)}, u32[]{:S(2)}, u32[]{:S(2)}) collective-permute-start(f32[256,512]{1,0:T(8,128)S(1)} %get-tuple-element.38), channel_id=1, source_target_pairs={{0,4},{4,0},{1,5},{5,1},{2,6},{6,2},{3,7},{7,3},{8,12},{12,8},{9,1... | collective-permute-start | bytes 1572872 | tf_op jit(solution)/shard_map/ppermute | solution.py:25
  19.6 6.7 %collective-permute-start.3 = (f32[64,512]{1,0:T(8,128)S(1)}, f32[64,512]{1,0:T(8,128)S(1)}, u32[]{:S(2)}, u32[]{:S(2)}) collective-permute-start(f32[64,512]{1,0:T(8,128)S(1)} %get-tuple-element.40), channel_id=1, source_target_pairs={{0,1},{1,2},{2,3},{3,0},{4,5},{5,6},{6,7},{7,4},{8,9},{9,10},{10,1... | collective-permute-start | bytes 393224 | tf_op jit(solution)/shard_map/ppermute | solution.py:21
  19.7 9.9 %collective-permute-start.4 = (f32[64,512]{1,0:T(8,128)S(1)}, f32[64,512]{1,0:T(8,128)S(1)}, u32[]{:S(2)}, u32[]{:S(2)}) collective-permute-start(f32[64,512]{1,0:T(8,128)S(1)} %get-tuple-element.41), channel_id=1, source_target_pairs={{0,2},{1,3},{2,0},{3,1},{4,6},{5,7},{6,4},{7,5},{8,10},{9,11},{10,... | collective-permute-start | bytes 393224 | tf_op jit(solution)/shard_map/ppermute | solution.py:21
  21.6 8.0 %collective-permute-start.5 = (f32[64,512]{1,0:T(8,128)S(1)}, f32[64,512]{1,0:T(8,128)S(1)}, u32[]{:S(2)}, u32[]{:S(2)}) collective-permute-start(f32[64,512]{1,0:T(8,128)S(1)} %get-tuple-element.42), channel_id=1, source_target_pairs={{0,3},{1,0},{2,1},{3,2},{4,7},{5,4},{6,5},{7,6},{8,11},{9,8},{10,9... | collective-permute-start | bytes 393224 | tf_op jit(solution)/shard_map/ppermute | solution.py:21
  26.3 7.8 %collective-permute-start.6 = (bf16[4,512,256]{2,1,0:T(8,128)(2,1)S(1)}, bf16[4,512,256]{2,1,0:T(8,128)(2,1)S(1)}, u32[]{:S(2)}, u32[]{:S(2)}) collective-permute-start(bf16[4,512,256]{2,1,0:T(8,128)(2,1)S(1)} %get-tuple-element.63), channel_id=1, source_target_pairs={{0,4},{4,0},{1,5},{5,1},{2,6},{6,2},{3,7},{7,3},{8,12},{12,8},{9,1... | collective-permute-start | bytes 3145736 | tf_op jit(solution)/shard_map/ppermute | solution.py:25
  29.6 4.5 %collective-permute-start.7 = (bf16[4,512,256]{2,1,0:T(8,128)(2,1)S(1)}, bf16[4,512,256]{2,1,0:T(8,128)(2,1)S(1)}, u32[]{:S(2)}, u32[]{:S(2)}) collective-permute-start(bf16[4,512,256]{2,1,0:T(8,128)(2,1)S(1)} %collective-permute-done.1), channel_id=1, source_target_pairs={{0,4},{4,0},{1,5},{5,1},{2,6},{6,2},{3,7},{7,3},{8,12},{12,8},{9,1... | collective-permute-start | bytes 3145736 | tf_op jit(solution)/shard_map/ppermute | solution.py:25
  31.7 3.8 %collective-permute-start.8 = (bf16[4,512,256]{2,1,0:T(8,128)(2,1)S(1)}, bf16[4,512,256]{2,1,0:T(8,128)(2,1)S(1)}, u32[]{:S(2)}, u32[]{:S(2)}) collective-permute-start(bf16[4,512,256]{2,1,0:T(8,128)(2,1)S(1)} %collective-permute-done), channel_id=1, source_target_pairs={{0,4},{4,0},{1,5},{5,1},{2,6},{6,2},{3,7},{7,3},{8,12},{12,8},{9,1... | collective-permute-start | bytes 3145736 | tf_op jit(solution)/shard_map/ppermute | solution.py:25
  31.7 25.7 %collective-permute-start.13 = (bf16[4,512,256]{2,1,0:T(8,128)(2,1)S(1)}, bf16[4,512,256]{2,1,0:T(8,128)(2,1)S(1)}, u32[]{:S(2)}, u32[]{:S(2)}) collective-permute-start(bf16[4,512,256]{2,1,0:T(8,128)(2,1)S(1)} %get-tuple-element.53), channel_id=1, source_target_pairs={{0,128},{64,192},{128,0},{192,64},{1,129},{65,193},{129,1},{193,65... | collective-permute-start | bytes 3145736 | tf_op jit(solution)/shard_map/ppermute | solution.py:21
  38.3 20.5 %collective-permute-start.10 = (f32[64,1536]{1,0:T(8,128)S(1)}, f32[64,1536]{1,0:T(8,128)S(1)}, u32[]{:S(2)}, u32[]{:S(2)}) collective-permute-start(f32[64,1536]{1,0:T(8,128)S(1)} %get-tuple-element.51), channel_id=1, source_target_pairs={{0,2},{1,3},{2,0},{3,1},{4,6},{5,7},{6,4},{7,5},{8,10},{9,11},{10,... | collective-permute-start | bytes 1179656 | tf_op jit(solution)/shard_map/ppermute | solution.py:21
  41.2 17.6 %collective-permute-start.11 = (f32[64,1536]{1,0:T(8,128)S(1)}, f32[64,1536]{1,0:T(8,128)S(1)}, u32[]{:S(2)}, u32[]{:S(2)}) collective-permute-start(f32[64,1536]{1,0:T(8,128)S(1)} %get-tuple-element.52), channel_id=1, source_target_pairs={{0,3},{1,0},{2,1},{3,2},{4,7},{5,4},{6,5},{7,6},{8,11},{9,8},{10,9... | collective-permute-start | bytes 1179656 | tf_op jit(solution)/shard_map/ppermute | solution.py:21
  42.0 17.4 %collective-permute-start.9 = (f32[64,1536]{1,0:T(8,128)S(1)}, f32[64,1536]{1,0:T(8,128)S(1)}, u32[]{:S(2)}, u32[]{:S(2)}) collective-permute-start(f32[64,1536]{1,0:T(8,128)S(1)} %get-tuple-element.50), channel_id=1, source_target_pairs={{0,1},{1,2},{2,3},{3,0},{4,5},{5,6},{6,7},{7,4},{8,9},{9,10},{10,1... | collective-permute-start | bytes 1179656 | tf_op jit(solution)/shard_map/ppermute | solution.py:21
  57.4 3.6 %collective-permute-start.14 = (bf16[4,512,256]{2,1,0:T(8,128)(2,1)S(1)}, bf16[4,512,256]{2,1,0:T(8,128)(2,1)S(1)}, u32[]{:S(2)}, u32[]{:S(2)}) collective-permute-start(bf16[4,512,256]{2,1,0:T(8,128)(2,1)S(1)} %collective-permute-done.13), channel_id=1, source_target_pairs={{0,4},{4,0},{1,5},{5,1},{2,6},{6,2},{3,7},{7,3},{8,12},{12,8},{9,1... | collective-permute-start | bytes 3145736 | tf_op jit(solution)/shard_map/ppermute | solution.py:25
  64.0 11.6 %collective-permute-start.15 = (f32[192,512]{1,0:T(8,128)S(1)}, f32[192,512]{1,0:T(8,128)S(1)}, u32[]{:S(2)}, u32[]{:S(2)}) collective-permute-start(f32[192,512]{1,0:T(8,128)S(1)} %get-tuple-element.55), channel_id=1, source_target_pairs={{0,1},{1,2},{2,3},{3,0},{4,5},{5,6},{6,7},{7,4},{8,9},{9,10},{10,1... | collective-permute-start | bytes 1179656 | tf_op jit(solution)/shard_map/ppermute | solution.py:21
  65.3 19.7 %collective-permute-start.16 = (f32[192,512]{1,0:T(8,128)S(1)}, f32[192,512]{1,0:T(8,128)S(1)}, u32[]{:S(2)}, u32[]{:S(2)}) collective-permute-start(f32[192,512]{1,0:T(8,128)S(1)} %get-tuple-element.56), channel_id=1, source_target_pairs={{0,2},{1,3},{2,0},{3,1},{4,6},{5,7},{6,4},{7,5},{8,10},{9,11},{10,... | collective-permute-start | bytes 1179656 | tf_op jit(solution)/shard_map/ppermute | solution.py:21
  67.8 17.3 %collective-permute-start.17 = (f32[192,512]{1,0:T(8,128)S(1)}, f32[192,512]{1,0:T(8,128)S(1)}, u32[]{:S(2)}, u32[]{:S(2)}) collective-permute-start(f32[192,512]{1,0:T(8,128)S(1)} %get-tuple-element.57), channel_id=1, source_target_pairs={{0,3},{1,0},{2,1},{3,2},{4,7},{5,4},{6,5},{7,6},{8,11},{9,8},{10,9... | collective-permute-start | bytes 1179656 | tf_op jit(solution)/shard_map/ppermute | solution.py:21
  69.0 5.4 %collective-permute-start.12 = (f32[64,512]{1,0:T(8,128)S(1)}, f32[64,512]{1,0:T(8,128)S(1)}, u32[]{:S(2)}, u32[]{:S(2)}) collective-permute-start(f32[64,512]{1,0:T(8,128)S(1)} %slice.27), channel_id=1, source_target_pairs={{0,64},{64,128},{128,192},{192,0},{1,65},{65,129},{129,193},{193,1... | collective-permute-start | bytes 393224 | tf_op jit(solution)/shard_map/ppermute | solution.py:21
  85.2 5.1 %collective-permute-start.18 = (f32[64,512]{1,0:T(8,128)S(1)}, f32[64,512]{1,0:T(8,128)S(1)}, u32[]{:S(2)}, u32[]{:S(2)}) collective-permute-start(f32[64,512]{1,0:T(8,128)S(1)} %get-tuple-element.68), channel_id=1, source_target_pairs={{0,64},{64,128},{128,192},{192,0},{1,65},{65,129},{129,193},{193,1... | collective-permute-start | bytes 393224 | tf_op jit(solution)/shard_map/ppermute | solution.py:21
  86.4 3.9 %collective-permute-start.19 = (f32[64,512]{1,0:T(8,128)S(1)}, f32[64,512]{1,0:T(8,128)S(1)}, u32[]{:S(2)}, u32[]{:S(2)}) collective-permute-start(f32[64,512]{1,0:T(8,128)S(1)} %get-tuple-element.67), channel_id=1, source_target_pairs={{0,192},{64,0},{128,64},{192,128},{1,193},{65,1},{129,65},{193,129... | collective-permute-start | bytes 393224 | tf_op jit(solution)/shard_map/ppermute | solution.py:21
  91.3 11.8 %collective-permute-start.21 = (f32[3,8,3584]{2,1,0:T(8,128)S(1)}, f32[3,8,3584]{2,1,0:T(8,128)S(1)}, u32[]{:S(2)}, u32[]{:S(2)}) collective-permute-start(f32[3,8,3584]{2,1,0:T(8,128)S(1)} %get-tuple-element.60), channel_id=1, source_target_pairs={{0,56},{8,0},{16,8},{24,16},{32,24},{40,32},{48,40},{56,48},{1,57}... | collective-permute-start | bytes 1032200 | tf_op jit(solution)/shard_map/ppermute | solution.py:21
  97.0 6.1 %collective-permute-start.20 = (f32[2,8,3584]{2,1,0:T(8,128)S(1)}, f32[2,8,3584]{2,1,0:T(8,128)S(1)}, u32[]{:S(2)}, u32[]{:S(2)}) collective-permute-start(f32[2,8,3584]{2,1,0:T(8,128)S(1)} %get-tuple-element.59), channel_id=1, source_target_pairs={{0,8},{8,16},{16,24},{24,32},{32,40},{40,48},{48,56},{56,0},{1,9},... | collective-permute-start | bytes 688136 | tf_op jit(solution)/shard_map/ppermute | solution.py:21
  103.1 8.5 %collective-permute-start.22 = (f32[8,3584]{1,0:T(8,128)S(1)}, f32[8,3584]{1,0:T(8,128)S(1)}, u32[]{:S(2)}, u32[]{:S(2)}) collective-permute-start(f32[8,3584]{1,0:T(8,128)S(1)} %get-tuple-element.70), channel_id=1, source_target_pairs={{0,24},{8,32},{16,40},{24,48},{32,56},{40,0},{48,8},{56,16},{1,25}... | collective-permute-start | bytes 344072 | tf_op jit(solution)/shard_map/ppermute | solution.py:21
  104.5 7.2 %collective-permute-start.23 = (f32[8,3584]{1,0:T(8,128)S(1)}, f32[8,3584]{1,0:T(8,128)S(1)}, u32[]{:S(2)}, u32[]{:S(2)}) collective-permute-start(f32[8,3584]{1,0:T(8,128)S(1)} %get-tuple-element.71), channel_id=1, source_target_pairs={{0,40},{8,48},{16,56},{24,0},{32,8},{40,16},{48,24},{56,32},{1,41}... | collective-permute-start | bytes 344072 | tf_op jit(solution)/shard_map/ppermute | solution.py:21

commit v4 on v3

--- a/solution.py
+++ b/solution.py
@@ -113,12 +113,21 @@
     store_by_aux(aux, both[up.shape[0] :], outs, 0, 2 * n)
 
 
-def late_kernel(place, below, below2, mine, mine2, above, above2, across, across2, _, *outs):
+def late_kernel(place, below, mine, above, across, *refs):
+    given, *outs = refs
     core, aux = place[0], place[2]
-    right = wide((across, across2))
-    for at, slabs in enumerate(((below, below2), (mine, mine2), (above, above2))):
-        product = times_transposed(wide(slabs, core), right)
-        store_by_aux(aux, product, outs, at * (product.shape[0] // len(outs)), 0)
+    left = [wide((slab,), core) for slab in (below, mine, above)]
+    product = times_transposed(jnp.concatenate(left, axis=0), wide((across,)))
+    size = left[0].shape[0]
+    for at in range(3):
+        rows = slice(at * size, (at + 1) * size)
+        store_by_aux(aux, product[rows] + given[rows, :], outs, at * (size // len(outs)), 0)
+
+
+def own_kernel(place, below, mine, above, across, _, out):
+    core = place[0]
+    left = [wide((slab,), core) for slab in (below, mine, above)]
+    out[...] = times_transposed(jnp.concatenate(left, axis=0), wide((across,)))
 
 
 def pairs(kernel, place, operands, shape, xs, after=(), flops=1, limit=24 * MIB):
@@ -175,10 +184,7 @@
 
 def over_aux(parts, xs):
     there = {d: shift(parts[d], "aux", d, xs) for d in (2, 1, 3)}
-    return [parts[0], there[1], there[2], there[3]]
-
-
-SLOTS = ((0,), (3,), (5,), (1, 6), (7, 4, 2))
+    return [parts[0], there[2], there[3], there[1]]
 
 
 def turn(block, zs):
@@ -188,10 +194,17 @@
 
 
 def send_out(place, buffer, outs):
-    zs = buffer.shape[0]
-    for out, steps in zip(outs, SLOTS):
+    zs, _, width = buffer.shape
+    here, forward, backward, up, down = outs
+    for out, step in ((here, 0), (forward, 3), (backward, 5)):
+        out[...] = buffer[lax.rem(place[3] + step, zs)]
+    for out, steps in ((up, (1, 6)), (down, (7, 2))):
         for at, step in enumerate(steps):
-            out[at] = buffer[lax.rem(place[3] + step, zs)]
+            out[:, at * width : (at + 1) * width] = buffer[lax.rem(place[3] + step, zs)]
+    half = width // 2
+    opposite = lax.rem(place[3] + zs // 2, zs)
+    up[:, 2 * width :] = buffer[opposite, :, :half]
+    down[:, 2 * width :] = buffer[opposite, :, half:]
 
 
 def pack_kernel(place, *refs):
@@ -213,7 +226,7 @@
 def pack(place, *operands):
     zs = 8
     width = 7 * operands[0].shape[1]
-    shapes = [(len(steps), 8, width) for steps in SLOTS]
+    shapes = [(8, width)] * 3 + [(8, 2 * width + width // 2)] * 2
     return pl.pallas_call(
         pack_kernel,
         in_specs=[SCALARS] + [ANYWHERE] * len(operands),
@@ -229,8 +242,15 @@
 def first_z(packed):
     zs = 8
     here, forward, backward, up, down = packed
+    width = here.shape[1]
+    half = width // 2
     up, down = shift(up, "z", 1, zs), shift(down, "z", -1, zs)
-    return here[0] + up[0] + down[0], forward[0] + down[2], backward[0] + up[1] + down[1]
+    here = here + up[:, :width] + down[:, :width]
+    forward = forward + down[:, width : 2 * width]
+    forward = jnp.concatenate([forward[:, :half] + up[:, 2 * width :], forward[:, half:]], axis=1)
+    backward = backward + up[:, width : 2 * width]
+    backward = jnp.concatenate([backward[:, :half], backward[:, half:] + down[:, 2 * width :]], axis=1)
+    return here, forward, backward
 
 
 def second_z(here, forward, backward):
@@ -295,13 +315,11 @@
     early_parts = pairs(early_kernel, place, (mine, mine2, *above, *below), (zs * 8, 3 * n), xs)
     early = total(over_aux(early_parts, xs), flops=SOME)
     third = shift(early[:, n : 2 * n], "row", 1, ys)
+    (across_own,) = grouped(across)
+    (across_sibling,) = grouped(sibling(across))
+    (own,) = pairs(own_kernel, place, (below[0], mine, above[0], across_own), (3 * n // 2, n), 1, (early,))
     late_parts = pairs(
-        late_kernel,
-        place,
-        (*below, mine, mine2, *above, *grouped(across, sibling(across))),
-        (3 * zs * 8, n),
-        xs,
-        (early,),
+        late_kernel, place, (below[1], mine2, above[1], across_sibling, own), (3 * zs * 8, n), xs
     )
     late = total(over_aux(late_parts, xs), (third,))
     down, middle, up = late.reshape(3, zs * 8, n)

time: 135 us -> 132 us (0.978)
  blocking collectives: 20.7 us -> 14.9 us
  waiting for transfers between devices: 50.1 us -> 55.7 us
  starting transfers between devices: 42.2 us -> 39.7 us
    ppermute x19, waiting for transfers between devices: 45.6 us -> 52.8 us  [shift(): lax.ppermute(value, axis, [(i, (i + step) % size) for i in range(size)])]
    all_to_all x1, blocking collectives: 20.7 us -> 14.9 us  [body(): pieces = lax.all_to_all(pieces, ('row', 'core', 'aux'), 0, 0, tiled=True)]
    ppermute x5, waiting for transfers between devices: 4.5 us -> 2.89 us  [sibling(): return lax.ppermute(value, 'core', [(0, 1), (1, 0)])]
    ppermute x19, starting transfers between devices: 32.5 us -> 31.1 us  [shift(): lax.ppermute(value, axis, [(i, (i + step) % size) for i in range(size)])]
    pallas_call x3 -> x4, Pallas kernels: 6.49 us -> 6.95 us  [pairs(): pl.pallas_call(kernel, in_specs=[SCALARS] + [ANYWHERE] * len(operands) +...]
  transfers between devices with their start and end apart: 24 -> 24, of which waited for: 12 -> 16; matrix products, arithmetic and copies ran while one was open for 1% -> 1% of each run, Pallas kernels for 6% -> 7%
where the time goes in v4:
time: 132 us
  waiting for transfers between devices  55.7 us (42%)
  starting transfers between devices  39.7 us (30%)
  blocking collectives  14.9 us (11%)
  Pallas kernels  14.8 us (11%)
  other arithmetic  4.43 us (3%)
  local copies, waits for them, and re-layouts  2.52 us (2%)
    ppermute x19, waiting for transfers between devices, shift(): lax.ppermute(value, axis, [(i, (i + step) % size) for i in range(size)])  52.8 us
    ppermute x19, starting transfers between devices, shift(): lax.ppermute(value, axis, [(i, (i + step) % size) for i in range(size)])  31.1 us
    all_to_all x1, blocking collectives, body(): pieces = lax.all_to_all(pieces, ('row', 'core', 'aux'), 0, 0, tiled=True)  14.9 us
    ppermute x5, starting transfers between devices, sibling(): return lax.ppermute(value, 'core', [(0, 1), (1, 0)])  8.59 us
    pallas_call x4, Pallas kernels, pairs(): pl.pallas_call(kernel, in_specs=[SCALARS] + [ANYWHERE] * len(operands) +...  6.95 us
    pallas_call x1, Pallas kernels, diagonal(): pl.pallas_call(diagonal_kernel, grid=(depth // group,), in_specs=[SCALARS...  4.62 us
    mul x2, other arithmetic, slab(): part * lax.dynamic_slice(keep, (first, 0), (quarter, mrows))[:, :, None]  3.4 us
    ppermute x5, waiting for transfers between devices, sibling(): return lax.ppermute(value, 'core', [(0, 1), (1, 0)])  2.89 us
  transfers between devices with their start and end apart: 24, of which 16 were waited for; matrix products, arithmetic and copies ran while one was open for 1% of the time, Pallas kernels for 7%

profile of v4, /device:TPU:1, one launch (start us, length us, event | category | flops | bytes accessed | tf_op | source)
XLA Modules:
  0.0 132.3 jit_solution(5272700547810085984)
XLA Ops:
  0.0 0.8 dynamic-slice_convert_fusion
  0.8 0.1 copy.3
  0.9 0.1 broadcast_in_dim.2
  1.1 2.7 %dynamic-slice_multiply_fusion.2 = (bf16[4,512,256]{2,1,0:T(8,128)(2,1)S(1)}, bf16[4,512,256]{2,1,0:T(8,128)(2,1)}) fusion(bf16[16,512,256]{2,1,0:T(8,128)(2,1)} %slab, s32[]{:T(128)S(6)} %select_n.25, bf16[4,512]{1,0:T(4,128)(2,1)S(1)} %get-tuple-element.76, bf16[4,512]{1,0:T(4,128)(2,1)S(1)} %get-tuple-element.77, s32[]{:T(128)S(6)} %select_n.22), kind=kLoop, calls=%fused_computation.2 | loop fusion | flops 1048576 | bytes 4202504 | tf_op jit(solution)/shard_map/mul | solution.py:296
  3.8 2.1 %collective-permute-start = (bf16[4,512,256]{2,1,0:T(8,128)(2,1)}, bf16[4,512,256]{2,1,0:T(8,128)(2,1)S(1)}, u32[]{:S(2)}, u32[]{:S(2)}) collective-permute-start(bf16[4,512,256]{2,1,0:T(8,128)(2,1)} %get-tuple-element.34), channel_id=1, source_target_pairs={{0,64},{64,128},{128,192},{192,0},{1,65},{65,129},{129,193},{193,1... | collective-permute-start | bytes 3145736 | tf_op jit(solution)/shard_map/ppermute | solution.py:21
  5.9 1.4 %collective-permute-start.1 = (bf16[4,512,256]{2,1,0:T(8,128)(2,1)S(1)}, bf16[4,512,256]{2,1,0:T(8,128)(2,1)S(1)}, u32[]{:S(2)}, u32[]{:S(2)}) collective-permute-start(bf16[4,512,256]{2,1,0:T(8,128)(2,1)S(1)} %get-tuple-element.35), channel_id=1, source_target_pairs={{0,192},{64,0},{128,64},{192,128},{1,193},{65,1},{129,65},{193,129... | collective-permute-start | bytes 3145736 | tf_op jit(solution)/shard_map/ppermute | solution.py:21
  7.4 0.1 copy.4.screen
  7.5 0.1 pad_add_fusion.place
  7.5 2.2 %copy-done = bf16[16,512,256]{2,1,0:T(8,128)(2,1)S(1)} copy-done((bf16[16,512,256]{2,1,0:T(8,128)(2,1)S(1)}, bf16[16,512,256]{2,1,0:T(8,128)(2,1)}, u32[]{:S(2)}) %copy-start) | copy-done | bytes 4194328
  9.7 4.6 %diagonal.1 = (f32[256,512]{1,0:T(8,128)S(1)}, f32[256,512]{1,0:T(8,128)S(1)}) custom-call(s32[4]{0:T(128)S(1)} %pad_add_fusion.place, s32[64,16]{1,0:T(8,128)S(1)} %copy.4.screen, bf16[16,512,256]{2,1,0:T(8,128)(2,1)S(1)} %copy-done), custom_call_target="tpu_custom_call" | custom-call | flops 1 | bytes 1 | tf_op jit(solution)/shard_map/diagonal/pallas_call | solution.py:68
  14.4 3.0 %collective-permute-start.2 = (f32[256,512]{1,0:T(8,128)S(1)}, f32[256,512]{1,0:T(8,128)S(1)}, u32[]{:S(2)}, u32[]{:S(2)}) collective-permute-start(f32[256,512]{1,0:T(8,128)S(1)} %get-tuple-element.38), channel_id=1, source_target_pairs={{0,4},{4,0},{1,5},{5,1},{2,6},{6,2},{3,7},{7,3},{8,12},{12,8},{9,1... | collective-permute-start | bytes 1572872 | tf_op jit(solution)/shard_map/ppermute | solution.py:25
  17.4 1.5 %collective-permute-done.2.got = f32[256,512]{1,0:T(8,128)S(1)} collective-permute-done((f32[256,512]{1,0:T(8,128)S(1)}, f32[256,512]{1,0:T(8,128)S(1)}, u32[]{:S(2)}, u32[]{:S(2)}) %collective-permute-start.2) | collective-permute-done | bytes 524320 | tf_op jit(solution)/shard_map/ppermute | solution.py:25
  18.9 0.7 split_kernel.1
  19.6 1.1 collective-permute-start.3
  20.7 0.9 collective-permute-start.4
  21.5 0.6 collective-permute-start.5
  22.1 0.7 dynamic-slice_multiply_fusion
  22.8 3.0 %collective-permute-done.3.refs_1_ = f32[64,512]{1,0:T(8,128)S(1)} collective-permute-done((f32[64,512]{1,0:T(8,128)S(1)}, f32[64,512]{1,0:T(8,128)S(1)}, u32[]{:S(2)}, u32[]{:S(2)}) %collective-permute-start.3) | collective-permute-done | bytes 131104 | tf_op jit(solution)/shard_map/ppermute | solution.py:21
  25.9 2.0 %collective-permute-start.6 = (bf16[4,512,256]{2,1,0:T(8,128)(2,1)S(1)}, bf16[4,512,256]{2,1,0:T(8,128)(2,1)S(1)}, u32[]{:S(2)}, u32[]{:S(2)}) collective-permute-start(bf16[4,512,256]{2,1,0:T(8,128)(2,1)S(1)} %get-tuple-element.63), channel_id=1, source_target_pairs={{0,4},{4,0},{1,5},{5,1},{2,6},{6,2},{3,7},{7,3},{8,12},{12,8},{9,1... | collective-permute-start | bytes 3145736 | tf_op jit(solution)/shard_map/ppermute | solution.py:25
  27.9 0.0 collective-permute-done.4.refs_2_
  27.9 1.1 collective-permute-done.5.refs_3_
  29.0 0.0 collective-permute-done
  29.0 0.5 collective-permute-done.1
  29.5 2.2 %collective-permute-start.7 = (bf16[4,512,256]{2,1,0:T(8,128)(2,1)S(1)}, bf16[4,512,256]{2,1,0:T(8,128)(2,1)S(1)}, u32[]{:S(2)}, u32[]{:S(2)}) collective-permute-start(bf16[4,512,256]{2,1,0:T(8,128)(2,1)S(1)} %collective-permute-done.1), channel_id=1, source_target_pairs={{0,4},{4,0},{1,5},{5,1},{2,6},{6,2},{3,7},{7,3},{8,12},{12,8},{9,1... | collective-permute-start | bytes 3145736 | tf_op jit(solution)/shard_map/ppermute | solution.py:25
  31.7 0.0 collective-permute-start.8
  31.7 2.4 %collective-permute-start.13 = (bf16[4,512,256]{2,1,0:T(8,128)(2,1)S(1)}, bf16[4,512,256]{2,1,0:T(8,128)(2,1)S(1)}, u32[]{:S(2)}, u32[]{:S(2)}) collective-permute-start(bf16[4,512,256]{2,1,0:T(8,128)(2,1)S(1)} %get-tuple-element.53), channel_id=1, source_target_pairs={{0,128},{64,192},{128,0},{192,64},{1,129},{65,193},{129,1},{193,65... | collective-permute-start | bytes 3145736 | tf_op jit(solution)/shard_map/ppermute | solution.py:21
  34.1 1.3 %collective-permute-done.8 = bf16[4,512,256]{2,1,0:T(8,128)(2,1)S(1)} collective-permute-done((bf16[4,512,256]{2,1,0:T(8,128)(2,1)S(1)}, bf16[4,512,256]{2,1,0:T(8,128)(2,1)S(1)}, u32[]{:S(2)}, u32[]{:S(2)}) %collective-permute-start.8) | collective-permute-done | bytes 1048608 | tf_op jit(solution)/shard_map/ppermute | solution.py:25
  35.5 2.8 %early_kernel.1 = (f32[64,1536]{1,0:T(8,128)S(1)}, f32[64,1536]{1,0:T(8,128)S(1)}, f32[64,1536]{1,0:T(8,128)S(1)}, f32[64,1536]{1,0:T(8,128)S(1)}) custom-call(s32[4]{0:T(128)S(1)} %pad_add_fusion.place, bf16[4,8,2,32,256]{4,3,2,1,0:T(8,128)(2,1)S(1)} %bitcast.16, bf16[4,8,2,32,256]{4,3,2,1,0:T(8,128)(2,1)S(1)} %bitcast.22, ...), custom_call_target="tpu_custom_call" | custom-call | flops 1 | bytes 1 | tf_op jit(solution)/shard_map/early_kernel/pallas_call | solution.py:135
  38.3 2.6 %collective-permute-start.10 = (f32[64,1536]{1,0:T(8,128)S(1)}, f32[64,1536]{1,0:T(8,128)S(1)}, u32[]{:S(2)}, u32[]{:S(2)}) collective-permute-start(f32[64,1536]{1,0:T(8,128)S(1)} %get-tuple-element.51), channel_id=1, source_target_pairs={{0,3},{1,0},{2,1},{3,2},{4,7},{5,4},{6,5},{7,6},{8,11},{9,8},{10,9... | collective-permute-start | bytes 1179656 | tf_op jit(solution)/shard_map/ppermute | solution.py:21
  40.9 0.0 collective-permute-start.11
  40.9 1.7 %collective-permute-start.9 = (f32[64,1536]{1,0:T(8,128)S(1)}, f32[64,1536]{1,0:T(8,128)S(1)}, u32[]{:S(2)}, u32[]{:S(2)}) collective-permute-start(f32[64,1536]{1,0:T(8,128)S(1)} %get-tuple-element.50), channel_id=1, source_target_pairs={{0,2},{1,3},{2,0},{3,1},{4,6},{5,7},{6,4},{7,5},{8,10},{9,11},{10,... | collective-permute-start | bytes 1179656 | tf_op jit(solution)/shard_map/ppermute | solution.py:21
  42.6 14.8 %collective-permute-done.13 = bf16[4,512,256]{2,1,0:T(8,128)(2,1)S(1)} collective-permute-done((bf16[4,512,256]{2,1,0:T(8,128)(2,1)S(1)}, bf16[4,512,256]{2,1,0:T(8,128)(2,1)S(1)}, u32[]{:S(2)}, u32[]{:S(2)}) %collective-permute-start.13) | collective-permute-done | bytes 1048608 | tf_op jit(solution)/shard_map/ppermute | solution.py:21
  57.4 1.4 %collective-permute-start.14 = (bf16[4,512,256]{2,1,0:T(8,128)(2,1)S(1)}, bf16[4,512,256]{2,1,0:T(8,128)(2,1)S(1)}, u32[]{:S(2)}, u32[]{:S(2)}) collective-permute-start(bf16[4,512,256]{2,1,0:T(8,128)(2,1)S(1)} %collective-permute-done.13), channel_id=1, source_target_pairs={{0,4},{4,0},{1,5},{5,1},{2,6},{6,2},{3,7},{7,3},{8,12},{12,8},{9,1... | collective-permute-start | bytes 3145736 | tf_op jit(solution)/shard_map/ppermute | solution.py:25
  58.8 0.0 collective-permute-done.10.refs_2_
  58.8 0.0 collective-permute-done.11.refs_3_
  58.8 0.9 collective-permute-done.9.refs_1_
  59.7 0.1 total.2._.refs_4_
  59.7 1.5 %own_kernel.1.refs_0_ = f32[768,512]{1,0:T(8,128)S(1)} custom-call(s32[4]{0:T(128)S(1)} %pad_add_fusion.place, bf16[4,8,2,32,256]{4,3,2,1,0:T(8,128)(2,1)S(1)} %bitcast.19, bf16[4,8,2,32,256]{4,3,2,1,0:T(8,128)(2,1)S(1)} %bitcast.17, bf16[4,8,2,32,256]{4,3,2,1,0:T(8,128)(2,1)S(1)} %bitcast.21, bf16[4,8,2,32,256]{4,3,2,1,0:T(8,128)(2,1)S(1)} %bitcast.28, ...), custom_call_target="tpu_custom_call" | custom-call | flops 1 | bytes 1 | tf_op jit(solution)/shard_map/own_kernel/pallas_call | solution.py:135
  61.3 0.0 collective-permute-done.14
  61.3 1.9 %late_kernel.1 = (f32[192,512]{1,0:T(8,128)S(1)}, f32[192,512]{1,0:T(8,128)S(1)}, f32[192,512]{1,0:T(8,128)S(1)}, f32[192,512]{1,0:T(8,128)S(1)}) custom-call(s32[4]{0:T(128)S(1)} %pad_add_fusion.place, bf16[4,8,2,32,256]{4,3,2,1,0:T(8,128)(2,1)S(1)} %bitcast.27, bf16[4,8,2,32,256]{4,3,2,1,0:T(8,128)(2,1)S(1)} %bitcast.23, ...), custom_call_target="tpu_custom_call" | custom-call | flops 1 | bytes 1 | tf_op jit(solution)/shard_map/late_kernel/pallas_call | solution.py:135
  63.2 2.6 %collective-permute-start.15 = (f32[192,512]{1,0:T(8,128)S(1)}, f32[192,512]{1,0:T(8,128)S(1)}, u32[]{:S(2)}, u32[]{:S(2)}) collective-permute-start(f32[192,512]{1,0:T(8,128)S(1)} %get-tuple-element.55), channel_id=1, source_target_pairs={{0,2},{1,3},{2,0},{3,1},{4,6},{5,7},{6,4},{7,5},{8,10},{9,11},{10,... | collective-permute-start | bytes 1179656 | tf_op jit(solution)/shard_map/ppermute | solution.py:21
  65.8 0.9 collective-permute-start.16
  66.7 0.6 collective-permute-start.17
  67.3 1.2 collective-permute-start.12
  68.5 4.2 %collective-permute-done.12.refs_4_.refs_5_ = f32[64,512]{1,0:T(8,128)S(1)} collective-permute-done((f32[64,512]{1,0:T(8,128)S(1)}, f32[64,512]{1,0:T(8,128)S(1)}, u32[]{:S(2)}, u32[]{:S(2)}) %collective-permute-start.12) | collective-permute-done | bytes 131104 | tf_op jit(solution)/shard_map/ppermute | solution.py:21
  72.7 1.3 collective-permute-done.15.refs_1_
  74.0 9.5 %collective-permute-done.16.refs_2_ = f32[192,512]{1,0:T(8,128)S(1)} collective-permute-done((f32[192,512]{1,0:T(8,128)S(1)}, f32[192,512]{1,0:T(8,128)S(1)}, u32[]{:S(2)}, u32[]{:S(2)}) %collective-permute-start.16) | collective-permute-done | bytes 393248 | tf_op jit(solution)/shard_map/ppermute | solution.py:21
  83.4 0.8 collective-permute-done.17.refs_3_
  84.2 0.1 total.3
  84.4 1.1 collective-permute-start.18
  85.5 1.6 %collective-permute-start.19 = (f32[64,512]{1,0:T(8,128)S(1)}, f32[64,512]{1,0:T(8,128)S(1)}, u32[]{:S(2)}, u32[]{:S(2)}) collective-permute-start(f32[64,512]{1,0:T(8,128)S(1)} %get-tuple-element.67), channel_id=1, source_target_pairs={{0,192},{64,0},{128,64},{192,128},{1,193},{65,1},{129,65},{193,129... | collective-permute-start | bytes 393224 | tf_op jit(solution)/shard_map/ppermute | solution.py:21
  87.1 3.1 %collective-permute-done.18.refs_7_ = f32[64,512]{1,0:T(8,128)S(1)} collective-permute-done((f32[64,512]{1,0:T(8,128)S(1)}, f32[64,512]{1,0:T(8,128)S(1)}, u32[]{:S(2)}, u32[]{:S(2)}) %collective-permute-start.18) | collective-permute-done | bytes 131104 | tf_op jit(solution)/shard_map/ppermute | solution.py:21
  90.2 0.0 collective-permute-done.19.refs_8_
  90.2 1.0 pack.1
  91.2 5.6 %collective-permute-start.21 = (f32[8,8960]{1,0:T(8,128)S(1)}, f32[8,8960]{1,0:T(8,128)S(1)}, u32[]{:S(2)}, u32[]{:S(2)}) collective-permute-start(f32[8,8960]{1,0:T(8,128)S(1)} %get-tuple-element.60), channel_id=1, source_target_pairs={{0,56},{8,0},{16,8},{24,16},{32,24},{40,32},{48,40},{56,48},{1,57}... | collective-permute-start | bytes 860168 | tf_op jit(solution)/shard_map/ppermute | solution.py:21
  96.9 4.8 %collective-permute-done.21 = f32[8,8960]{1,0:T(8,128)S(1)} collective-permute-done((f32[8,8960]{1,0:T(8,128)S(1)}, f32[8,8960]{1,0:T(8,128)S(1)}, u32[]{:S(2)}, u32[]{:S(2)}) %collective-permute-start.21) | collective-permute-done | bytes 286752 | tf_op jit(solution)/shard_map/ppermute | solution.py:21
  101.7 3.1 %collective-permute-done.20 = f32[8,8960]{1,0:T(8,128)S(1)} collective-permute-done((f32[8,8960]{1,0:T(8,128)S(1)}, f32[8,8960]{1,0:T(8,128)S(1)}, u32[]{:S(2)}, u32[]{:S(2)}) %collective-permute-start.20) | collective-permute-done | bytes 286752 | tf_op jit(solution)/shard_map/ppermute | solution.py:21
  104.8 0.1 collective-permute-start.22
  105.0 4.5 %collective-permute-start.23 = (f32[8,3584]{1,0:T(8,128)S(1)}, f32[8,3584]{1,0:T(8,128)S(1)}, u32[]{:S(2)}, u32[]{:S(2)}) collective-permute-start(f32[8,3584]{1,0:T(8,128)S(1)} %pad_maximum_fusion.1), channel_id=1, source_target_pairs={{0,40},{8,48},{16,56},{24,0},{32,8},{40,16},{48,24},{56,32},{1,41}... | collective-permute-start | bytes 344072 | tf_op jit(solution)/shard_map/ppermute | solution.py:21
  109.5 4.0 %collective-permute-done.22 = f32[8,3584]{1,0:T(8,128)S(1)} collective-permute-done((f32[8,3584]{1,0:T(8,128)S(1)}, f32[8,3584]{1,0:T(8,128)S(1)}, u32[]{:S(2)}, u32[]{:S(2)}) %collective-permute-start.22) | collective-permute-done | bytes 114720 | tf_op jit(solution)/shard_map/ppermute | solution.py:21
  113.5 1.8 %collective-permute-done.23 = f32[8,3584]{1,0:T(8,128)S(1)} collective-permute-done((f32[8,3584]{1,0:T(8,128)S(1)}, f32[8,3584]{1,0:T(8,128)S(1)}, u32[]{:S(2)}, u32[]{:S(2)}) %collective-permute-start.23) | collective-permute-done | bytes 114720 | tf_op jit(solution)/shard_map/ppermute | solution.py:21
  115.3 0.6 spread_kernel.1
  115.9 14.9 %all_to_all.5.pieces = f32[32,8,128]{2,1,0:T(8,128)S(1)} all-to-all(f32[32,8,128]{2,1,0:T(8,128)S(1)} %spread_kernel.1), channel_id=1, replica_groups=mesh['row'=4,'z'=8,'core'=2,'aux'=4] {'row','core','aux'}, dimensions={0} | all-to-all | bytes 262144 | tf_op jit(solution)/shard_map/all_to_all | solution.py:332
  130.8 1.4 %finish_kernel.1 = f32[8,2048]{1,0:T(8,128)} custom-call(s32[4]{0:T(128)S(1)} %pad_add_fusion.place, f32[8,3584]{1,0:T(8,128)S(1)} %fusion.1.rows, f32[32,8,128]{2,1,0:T(8,128)S(1)} %all_to_all.5.pieces), custom_call_target="tpu_custom_call" | custom-call | flops 1 | bytes 1 | tf_op jit(solution)/shard_map/finish_kernel/pallas_call | solution.py:174
  (17 shorter events, 0.2 us)
Async XLA Ops:
  0.0 7.4 %copy-start.1 = (s32[64,16]{0,1:T(8,128)S(1)}, s32[64,16]{0,1:T(8,128)}, u32[]{:S(2)}) copy-start(s32[64,16]{0,1:T(8,128)} %param.3) | copy-start | bytes 12292
  3.8 25.2 %collective-permute-start = (bf16[4,512,256]{2,1,0:T(8,128)(2,1)}, bf16[4,512,256]{2,1,0:T(8,128)(2,1)S(1)}, u32[]{:S(2)}, u32[]{:S(2)}) collective-permute-start(bf16[4,512,256]{2,1,0:T(8,128)(2,1)} %get-tuple-element.34), channel_id=1, source_target_pairs={{0,64},{64,128},{128,192},{192,0},{1,65},{65,129},{129,193},{193,1... | collective-permute-start | bytes 3145736 | tf_op jit(solution)/shard_map/ppermute | solution.py:21
  5.9 23.5 %collective-permute-start.1 = (bf16[4,512,256]{2,1,0:T(8,128)(2,1)S(1)}, bf16[4,512,256]{2,1,0:T(8,128)(2,1)S(1)}, u32[]{:S(2)}, u32[]{:S(2)}) collective-permute-start(bf16[4,512,256]{2,1,0:T(8,128)(2,1)S(1)} %get-tuple-element.35), channel_id=1, source_target_pairs={{0,192},{64,0},{128,64},{192,128},{1,193},{65,1},{129,65},{193,129... | collective-permute-start | bytes 3145736 | tf_op jit(solution)/shard_map/ppermute | solution.py:21
  7.5 2.2 %copy-start = (bf16[16,512,256]{2,1,0:T(8,128)(2,1)S(1)}, bf16[16,512,256]{2,1,0:T(8,128)(2,1)}, u32[]{:S(2)}) copy-start(bf16[16,512,256]{2,1,0:T(8,128)(2,1)} %slab) | copy-start | bytes 12582916
  14.4 4.5 %collective-permute-start.2 = (f32[256,512]{1,0:T(8,128)S(1)}, f32[256,512]{1,0:T(8,128)S(1)}, u32[]{:S(2)}, u32[]{:S(2)}) collective-permute-start(f32[256,512]{1,0:T(8,128)S(1)} %get-tuple-element.38), channel_id=1, source_target_pairs={{0,4},{4,0},{1,5},{5,1},{2,6},{6,2},{3,7},{7,3},{8,12},{12,8},{9,1... | collective-permute-start | bytes 1572872 | tf_op jit(solution)/shard_map/ppermute | solution.py:25
  19.6 6.3 %collective-permute-start.3 = (f32[64,512]{1,0:T(8,128)S(1)}, f32[64,512]{1,0:T(8,128)S(1)}, u32[]{:S(2)}, u32[]{:S(2)}) collective-permute-start(f32[64,512]{1,0:T(8,128)S(1)} %get-tuple-element.40), channel_id=1, source_target_pairs={{0,2},{1,3},{2,0},{3,1},{4,6},{5,7},{6,4},{7,5},{8,10},{9,11},{10,... | collective-permute-start | bytes 393224 | tf_op jit(solution)/shard_map/ppermute | solution.py:21
  20.7 7.2 %collective-permute-start.4 = (f32[64,512]{1,0:T(8,128)S(1)}, f32[64,512]{1,0:T(8,128)S(1)}, u32[]{:S(2)}, u32[]{:S(2)}) collective-permute-start(f32[64,512]{1,0:T(8,128)S(1)} %get-tuple-element.41), channel_id=1, source_target_pairs={{0,3},{1,0},{2,1},{3,2},{4,7},{5,4},{6,5},{7,6},{8,11},{9,8},{10,9... | collective-permute-start | bytes 393224 | tf_op jit(solution)/shard_map/ppermute | solution.py:21
  21.5 7.4 %collective-permute-start.5 = (f32[64,512]{1,0:T(8,128)S(1)}, f32[64,512]{1,0:T(8,128)S(1)}, u32[]{:S(2)}, u32[]{:S(2)}) collective-permute-start(f32[64,512]{1,0:T(8,128)S(1)} %get-tuple-element.42), channel_id=1, source_target_pairs={{0,1},{1,2},{2,3},{3,0},{4,5},{5,6},{6,7},{7,4},{8,9},{9,10},{10,1... | collective-permute-start | bytes 393224 | tf_op jit(solution)/shard_map/ppermute | solution.py:21
  25.9 8.3 %collective-permute-start.6 = (bf16[4,512,256]{2,1,0:T(8,128)(2,1)S(1)}, bf16[4,512,256]{2,1,0:T(8,128)(2,1)S(1)}, u32[]{:S(2)}, u32[]{:S(2)}) collective-permute-start(bf16[4,512,256]{2,1,0:T(8,128)(2,1)S(1)} %get-tuple-element.63), channel_id=1, source_target_pairs={{0,4},{4,0},{1,5},{5,1},{2,6},{6,2},{3,7},{7,3},{8,12},{12,8},{9,1... | collective-permute-start | bytes 3145736 | tf_op jit(solution)/shard_map/ppermute | solution.py:25
  29.5 4.7 %collective-permute-start.7 = (bf16[4,512,256]{2,1,0:T(8,128)(2,1)S(1)}, bf16[4,512,256]{2,1,0:T(8,128)(2,1)S(1)}, u32[]{:S(2)}, u32[]{:S(2)}) collective-permute-start(bf16[4,512,256]{2,1,0:T(8,128)(2,1)S(1)} %collective-permute-done.1), channel_id=1, source_target_pairs={{0,4},{4,0},{1,5},{5,1},{2,6},{6,2},{3,7},{7,3},{8,12},{12,8},{9,1... | collective-permute-start | bytes 3145736 | tf_op jit(solution)/shard_map/ppermute | solution.py:25
  31.7 3.8 %collective-permute-start.8 = (bf16[4,512,256]{2,1,0:T(8,128)(2,1)S(1)}, bf16[4,512,256]{2,1,0:T(8,128)(2,1)S(1)}, u32[]{:S(2)}, u32[]{:S(2)}) collective-permute-start(bf16[4,512,256]{2,1,0:T(8,128)(2,1)S(1)} %collective-permute-done), channel_id=1, source_target_pairs={{0,4},{4,0},{1,5},{5,1},{2,6},{6,2},{3,7},{7,3},{8,12},{12,8},{9,1... | collective-permute-start | bytes 3145736 | tf_op jit(solution)/shard_map/ppermute | solution.py:25
  31.7 25.7 %collective-permute-start.13 = (bf16[4,512,256]{2,1,0:T(8,128)(2,1)S(1)}, bf16[4,512,256]{2,1,0:T(8,128)(2,1)S(1)}, u32[]{:S(2)}, u32[]{:S(2)}) collective-permute-start(bf16[4,512,256]{2,1,0:T(8,128)(2,1)S(1)} %get-tuple-element.53), channel_id=1, source_target_pairs={{0,128},{64,192},{128,0},{192,64},{1,129},{65,193},{129,1},{193,65... | collective-permute-start | bytes 3145736 | tf_op jit(solution)/shard_map/ppermute | solution.py:21
  38.3 20.5 %collective-permute-start.10 = (f32[64,1536]{1,0:T(8,128)S(1)}, f32[64,1536]{1,0:T(8,128)S(1)}, u32[]{:S(2)}, u32[]{:S(2)}) collective-permute-start(f32[64,1536]{1,0:T(8,128)S(1)} %get-tuple-element.51), channel_id=1, source_target_pairs={{0,3},{1,0},{2,1},{3,2},{4,7},{5,4},{6,5},{7,6},{8,11},{9,8},{10,9... | collective-permute-start | bytes 1179656 | tf_op jit(solution)/shard_map/ppermute | solution.py:21
  40.9 17.9 %collective-permute-start.11 = (f32[64,1536]{1,0:T(8,128)S(1)}, f32[64,1536]{1,0:T(8,128)S(1)}, u32[]{:S(2)}, u32[]{:S(2)}) collective-permute-start(f32[64,1536]{1,0:T(8,128)S(1)} %get-tuple-element.52), channel_id=1, source_target_pairs={{0,1},{1,2},{2,3},{3,0},{4,5},{5,6},{6,7},{7,4},{8,9},{9,10},{10,1... | collective-permute-start | bytes 1179656 | tf_op jit(solution)/shard_map/ppermute | solution.py:21
  40.9 18.8 %collective-permute-start.9 = (f32[64,1536]{1,0:T(8,128)S(1)}, f32[64,1536]{1,0:T(8,128)S(1)}, u32[]{:S(2)}, u32[]{:S(2)}) collective-permute-start(f32[64,1536]{1,0:T(8,128)S(1)} %get-tuple-element.50), channel_id=1, source_target_pairs={{0,2},{1,3},{2,0},{3,1},{4,6},{5,7},{6,4},{7,5},{8,10},{9,11},{10,... | collective-permute-start | bytes 1179656 | tf_op jit(solution)/shard_map/ppermute | solution.py:21
  57.4 3.9 %collective-permute-start.14 = (bf16[4,512,256]{2,1,0:T(8,128)(2,1)S(1)}, bf16[4,512,256]{2,1,0:T(8,128)(2,1)S(1)}, u32[]{:S(2)}, u32[]{:S(2)}) collective-permute-start(bf16[4,512,256]{2,1,0:T(8,128)(2,1)S(1)} %collective-permute-done.13), channel_id=1, source_target_pairs={{0,4},{4,0},{1,5},{5,1},{2,6},{6,2},{3,7},{7,3},{8,12},{12,8},{9,1... | collective-permute-start | bytes 3145736 | tf_op jit(solution)/shard_map/ppermute | solution.py:25
  63.2 10.8 %collective-permute-start.15 = (f32[192,512]{1,0:T(8,128)S(1)}, f32[192,512]{1,0:T(8,128)S(1)}, u32[]{:S(2)}, u32[]{:S(2)}) collective-permute-start(f32[192,512]{1,0:T(8,128)S(1)} %get-tuple-element.55), channel_id=1, source_target_pairs={{0,2},{1,3},{2,0},{3,1},{4,6},{5,7},{6,4},{7,5},{8,10},{9,11},{10,... | collective-permute-start | bytes 1179656 | tf_op jit(solution)/shard_map/ppermute | solution.py:21
  65.8 17.6 %collective-permute-start.16 = (f32[192,512]{1,0:T(8,128)S(1)}, f32[192,512]{1,0:T(8,128)S(1)}, u32[]{:S(2)}, u32[]{:S(2)}) collective-permute-start(f32[192,512]{1,0:T(8,128)S(1)} %get-tuple-element.56), channel_id=1, source_target_pairs={{0,3},{1,0},{2,1},{3,2},{4,7},{5,4},{6,5},{7,6},{8,11},{9,8},{10,9... | collective-permute-start | bytes 1179656 | tf_op jit(solution)/shard_map/ppermute | solution.py:21
  66.7 17.6 %collective-permute-start.17 = (f32[192,512]{1,0:T(8,128)S(1)}, f32[192,512]{1,0:T(8,128)S(1)}, u32[]{:S(2)}, u32[]{:S(2)}) collective-permute-start(f32[192,512]{1,0:T(8,128)S(1)} %get-tuple-element.57), channel_id=1, source_target_pairs={{0,1},{1,2},{2,3},{3,0},{4,5},{5,6},{6,7},{7,4},{8,9},{9,10},{10,1... | collective-permute-start | bytes 1179656 | tf_op jit(solution)/shard_map/ppermute | solution.py:21
  67.3 5.4 %collective-permute-start.12 = (f32[64,512]{1,0:T(8,128)S(1)}, f32[64,512]{1,0:T(8,128)S(1)}, u32[]{:S(2)}, u32[]{:S(2)}) collective-permute-start(f32[64,512]{1,0:T(8,128)S(1)} %slice.47), channel_id=1, source_target_pairs={{0,64},{64,128},{128,192},{192,0},{1,65},{65,129},{129,193},{193,1... | collective-permute-start | bytes 393224 | tf_op jit(solution)/shard_map/ppermute | solution.py:21
  84.4 5.9 %collective-permute-start.18 = (f32[64,512]{1,0:T(8,128)S(1)}, f32[64,512]{1,0:T(8,128)S(1)}, u32[]{:S(2)}, u32[]{:S(2)}) collective-permute-start(f32[64,512]{1,0:T(8,128)S(1)} %get-tuple-element.68), channel_id=1, source_target_pairs={{0,64},{64,128},{128,192},{192,0},{1,65},{65,129},{129,193},{193,1... | collective-permute-start | bytes 393224 | tf_op jit(solution)/shard_map/ppermute | solution.py:21
  85.5 4.7 %collective-permute-start.19 = (f32[64,512]{1,0:T(8,128)S(1)}, f32[64,512]{1,0:T(8,128)S(1)}, u32[]{:S(2)}, u32[]{:S(2)}) collective-permute-start(f32[64,512]{1,0:T(8,128)S(1)} %get-tuple-element.67), channel_id=1, source_target_pairs={{0,192},{64,0},{128,64},{192,128},{1,193},{65,1},{129,65},{193,129... | collective-permute-start | bytes 393224 | tf_op jit(solution)/shard_map/ppermute | solution.py:21
  91.2 10.4 %collective-permute-start.21 = (f32[8,8960]{1,0:T(8,128)S(1)}, f32[8,8960]{1,0:T(8,128)S(1)}, u32[]{:S(2)}, u32[]{:S(2)}) collective-permute-start(f32[8,8960]{1,0:T(8,128)S(1)} %get-tuple-element.60), channel_id=1, source_target_pairs={{0,56},{8,0},{16,8},{24,16},{32,24},{40,32},{48,40},{56,48},{1,57}... | collective-permute-start | bytes 860168 | tf_op jit(solution)/shard_map/ppermute | solution.py:21
  96.9 7.9 %collective-permute-start.20 = (f32[8,8960]{1,0:T(8,128)S(1)}, f32[8,8960]{1,0:T(8,128)S(1)}, u32[]{:S(2)}, u32[]{:S(2)}) collective-permute-start(f32[8,8960]{1,0:T(8,128)S(1)} %get-tuple-element.59), channel_id=1, source_target_pairs={{0,8},{8,16},{16,24},{24,32},{32,40},{40,48},{48,56},{56,0},{1,9},... | collective-permute-start | bytes 860168 | tf_op jit(solution)/shard_map/ppermute | solution.py:21
  104.8 8.7 %collective-permute-start.22 = (f32[8,3584]{1,0:T(8,128)S(1)}, f32[8,3584]{1,0:T(8,128)S(1)}, u32[]{:S(2)}, u32[]{:S(2)}) collective-permute-start(f32[8,3584]{1,0:T(8,128)S(1)} %pad_maximum_fusion), channel_id=1, source_target_pairs={{0,24},{8,32},{16,40},{24,48},{32,56},{40,0},{48,8},{56,16},{1,25}... | collective-permute-start | bytes 344072 | tf_op jit(solution)/shard_map/ppermute | solution.py:21
  105.0 10.3 %collective-permute-start.23 = (f32[8,3584]{1,0:T(8,128)S(1)}, f32[8,3584]{1,0:T(8,128)S(1)}, u32[]{:S(2)}, u32[]{:S(2)}) collective-permute-start(f32[8,3584]{1,0:T(8,128)S(1)} %pad_maximum_fusion.1), channel_id=1, source_target_pairs={{0,40},{8,48},{16,56},{24,0},{32,8},{40,16},{48,24},{56,32},{1,41}... | collective-permute-start | bytes 344072 | tf_op jit(solution)/shard_map/ppermute | solution.py:21

commit v5 on v4

--- a/solution.py
+++ b/solution.py
@@ -119,9 +119,10 @@
     left = [wide((slab,), core) for slab in (below, mine, above)]
     product = times_transposed(jnp.concatenate(left, axis=0), wide((across,)))
     size = left[0].shape[0]
-    for at in range(3):
+    outer, middle = outs[: len(outs) // 2], outs[len(outs) // 2 :]
+    for at, (to, row) in enumerate(((outer, 0), (middle, 0), (outer, middle[0].shape[0]))):
         rows = slice(at * size, (at + 1) * size)
-        store_by_aux(aux, product[rows] + given[rows, :], outs, at * (size // len(outs)), 0)
+        store_by_aux(aux, product[rows] + given[rows, :], to, row, 0)
 
 
 def own_kernel(place, below, mine, above, across, _, out):
@@ -130,13 +131,12 @@
     out[...] = times_transposed(jnp.concatenate(left, axis=0), wide((across,)))
 
 
-def pairs(kernel, place, operands, shape, xs, after=(), flops=1, limit=24 * MIB):
-    out = jax.ShapeDtypeStruct(shape, jnp.float32)
+def pairs(kernel, place, operands, shapes, after=(), flops=1, limit=24 * MIB):
     return pl.pallas_call(
         kernel,
         in_specs=[SCALARS] + [ANYWHERE] * len(operands) + [AFTER] * len(after),
-        out_specs=[ANYWHERE] * xs,
-        out_shape=[out] * xs,
+        out_specs=[ANYWHERE] * len(shapes),
+        out_shape=[jax.ShapeDtypeStruct(shape, jnp.float32) for shape in shapes],
         compiler_params=pltpu.CompilerParams(vmem_limit_bytes=limit),
         cost_estimate=pl.CostEstimate(flops=flops, bytes_accessed=1, transcendentals=0),
         name=kernel.__name__,
@@ -302,7 +302,7 @@
     mine, far = slab(block, 0), slab(block, 2)
     mine2 = sibling(mine)
     kept, given = diagonal(place, screen, block, zs)
-    diag = pairs(split_kernel, place, (kept, sibling(given)), (zs * 8, n), xs, limit=4 * MIB)
+    diag = pairs(split_kernel, place, (kept, sibling(given)), [(zs * 8, n)] * xs, limit=4 * MIB)
     diag = over_aux(diag, xs)
     below, above, far, diag = lax.optimization_barrier((below, above, far, diag))
     across = shift(far, "row", 2, ys)
@@ -312,18 +312,17 @@
 
     mine, mine2 = grouped(mine, mine2)
     below, above = grouped(below, sibling(below)), grouped(above, sibling(above))
-    early_parts = pairs(early_kernel, place, (mine, mine2, *above, *below), (zs * 8, 3 * n), xs)
+    early_parts = pairs(early_kernel, place, (mine, mine2, *above, *below), [(zs * 8, 3 * n)] * xs)
     early = total(over_aux(early_parts, xs), flops=SOME)
     third = shift(early[:, n : 2 * n], "row", 1, ys)
     (across_own,) = grouped(across)
     (across_sibling,) = grouped(sibling(across))
-    (own,) = pairs(own_kernel, place, (below[0], mine, above[0], across_own), (3 * n // 2, n), 1, (early,))
-    late_parts = pairs(
-        late_kernel, place, (below[1], mine2, above[1], across_sibling, own), (3 * zs * 8, n), xs
-    )
-    late = total(over_aux(late_parts, xs), (third,))
-    down, middle, up = late.reshape(3, zs * 8, n)
-    up, down = shift(up, "row", 1, ys), shift(down, "row", -1, ys)
+    (own,) = pairs(own_kernel, place, (below[0], mine, above[0], across_own), [(3 * n // 2, n)], (early,))
+    shapes = [(2 * zs * 8, n)] * xs + [(zs * 8, n)] * xs
+    late_parts = pairs(late_kernel, place, (below[1], mine2, above[1], across_sibling, own), shapes)
+    outer = total(over_aux(late_parts[:xs], xs), (third,))
+    middle = total(over_aux(late_parts[xs:], xs))
+    up, down = shift(outer[zs * 8 :], "row", 1, ys), shift(outer[: zs * 8], "row", -1, ys)
     rows = first_z(pack(place, *diag, early, third, middle, up, down))
     here, forward, backward = second_z(*rows)
     rows = here + forward + backward

time: 132 us -> 129 us (0.977)
  waiting for transfers between devices: 55.7 us -> 43.8 us
  blocking collectives: 14.9 us -> 20.9 us
  starting transfers between devices: 39.7 us -> 42.5 us
    ppermute x19 -> x22, waiting for transfers between devices: 52.8 us -> 40.9 us  [shift(): lax.ppermute(value, axis, [(i, (i + step) % size) for i in range(size)])]
    all_to_all x1, blocking collectives: 14.9 us -> 20.9 us  [body(): pieces = lax.all_to_all(pieces, ('row', 'core', 'aux'), 0, 0, tiled=True)]
    ppermute x19 -> x22, starting transfers between devices: 31.1 us -> 33.9 us  [shift(): lax.ppermute(value, axis, [(i, (i + step) % size) for i in range(size)])]
  transfers between devices with their start and end apart: 24 -> 27, of which waited for: 16 -> 15; matrix products, arithmetic and copies ran while one was open for 1% -> 1% of each run, Pallas kernels for 7% -> 8%
where the time goes in v5:
time: 129 us
  waiting for transfers between devices  43.8 us (34%)
  starting transfers between devices  42.5 us (33%)
  blocking collectives  20.9 us (16%)
  Pallas kernels  14.8 us (11%)
  other arithmetic  4.43 us (3%)
  local copies, waits for them, and re-layouts  2.52 us (2%)
    ppermute x22, waiting for transfers between devices, shift(): lax.ppermute(value, axis, [(i, (i + step) % size) for i in range(size)])  40.9 us
    ppermute x22, starting transfers between devices, shift(): lax.ppermute(value, axis, [(i, (i + step) % size) for i in range(size)])  33.9 us
    all_to_all x1, blocking collectives, body(): pieces = lax.all_to_all(pieces, ('row', 'core', 'aux'), 0, 0, tiled=True)  20.9 us
    ppermute x5, starting transfers between devices, sibling(): return lax.ppermute(value, 'core', [(0, 1), (1, 0)])  8.59 us
    pallas_call x4, Pallas kernels, pairs(): pl.pallas_call(kernel, in_specs=[SCALARS] + [ANYWHERE] * len(operands) +...  6.95 us
    pallas_call x1, Pallas kernels, diagonal(): pl.pallas_call(diagonal_kernel, grid=(depth // group,), in_specs=[SCALARS...  4.62 us
    mul x2, other arithmetic, slab(): part * lax.dynamic_slice(keep, (first, 0), (quarter, mrows))[:, :, None]  3.41 us
    ppermute x5, waiting for transfers between devices, sibling(): return lax.ppermute(value, 'core', [(0, 1), (1, 0)])  2.89 us
  transfers between devices with their start and end apart: 27, of which 15 were waited for; matrix products, arithmetic and copies ran while one was open for 1% of the time, Pallas kernels for 8%

profile of v5, /device:TPU:1, one launch (start us, length us, event | category | flops | bytes accessed | tf_op | source)
XLA Modules:
  0.0 129.1 jit_solution(12061594062980049868)
XLA Ops:
  0.0 0.8 dynamic-slice_convert_fusion
  0.8 0.1 copy.3
  0.9 0.1 broadcast_in_dim.2
  1.1 2.7 %dynamic-slice_multiply_fusion.2 = (bf16[4,512,256]{2,1,0:T(8,128)(2,1)S(1)}, bf16[4,512,256]{2,1,0:T(8,128)(2,1)}) fusion(bf16[16,512,256]{2,1,0:T(8,128)(2,1)} %slab, s32[]{:T(128)S(6)} %select_n.25, bf16[4,512]{1,0:T(4,128)(2,1)S(1)} %get-tuple-element.83, bf16[4,512]{1,0:T(4,128)(2,1)S(1)} %get-tuple-element.84, s32[]{:T(128)S(6)} %select_n.22), kind=kLoop, calls=%fused_computation.2 | loop fusion | flops 1048576 | bytes 4202504 | tf_op jit(solution)/shard_map/mul | solution.py:296
  3.8 2.1 %collective-permute-start = (bf16[4,512,256]{2,1,0:T(8,128)(2,1)}, bf16[4,512,256]{2,1,0:T(8,128)(2,1)S(1)}, u32[]{:S(2)}, u32[]{:S(2)}) collective-permute-start(bf16[4,512,256]{2,1,0:T(8,128)(2,1)} %get-tuple-element.38), channel_id=1, source_target_pairs={{0,64},{64,128},{128,192},{192,0},{1,65},{65,129},{129,193},{193,1... | collective-permute-start | bytes 3145736 | tf_op jit(solution)/shard_map/ppermute | solution.py:21
  5.9 1.4 %collective-permute-start.1 = (bf16[4,512,256]{2,1,0:T(8,128)(2,1)S(1)}, bf16[4,512,256]{2,1,0:T(8,128)(2,1)S(1)}, u32[]{:S(2)}, u32[]{:S(2)}) collective-permute-start(bf16[4,512,256]{2,1,0:T(8,128)(2,1)S(1)} %get-tuple-element.39), channel_id=1, source_target_pairs={{0,192},{64,0},{128,64},{192,128},{1,193},{65,1},{129,65},{193,129... | collective-permute-start | bytes 3145736 | tf_op jit(solution)/shard_map/ppermute | solution.py:21
  7.4 0.1 copy.4.screen
  7.5 0.1 pad_add_fusion.place
  7.5 2.2 %copy-done = bf16[16,512,256]{2,1,0:T(8,128)(2,1)S(1)} copy-done((bf16[16,512,256]{2,1,0:T(8,128)(2,1)S(1)}, bf16[16,512,256]{2,1,0:T(8,128)(2,1)}, u32[]{:S(2)}) %copy-start) | copy-done | bytes 4194328
  9.7 4.6 %diagonal.1 = (f32[256,512]{1,0:T(8,128)S(1)}, f32[256,512]{1,0:T(8,128)S(1)}) custom-call(s32[4]{0:T(128)S(1)} %pad_add_fusion.place, s32[64,16]{1,0:T(8,128)S(1)} %copy.4.screen, bf16[16,512,256]{2,1,0:T(8,128)(2,1)S(1)} %copy-done), custom_call_target="tpu_custom_call" | custom-call | flops 1 | bytes 1 | tf_op jit(solution)/shard_map/diagonal/pallas_call | solution.py:68
  14.4 3.0 %collective-permute-start.2 = (f32[256,512]{1,0:T(8,128)S(1)}, f32[256,512]{1,0:T(8,128)S(1)}, u32[]{:S(2)}, u32[]{:S(2)}) collective-permute-start(f32[256,512]{1,0:T(8,128)S(1)} %get-tuple-element.42), channel_id=1, source_target_pairs={{0,4},{4,0},{1,5},{5,1},{2,6},{6,2},{3,7},{7,3},{8,12},{12,8},{9,1... | collective-permute-start | bytes 1572872 | tf_op jit(solution)/shard_map/ppermute | solution.py:25
  17.4 1.5 %collective-permute-done.2.got = f32[256,512]{1,0:T(8,128)S(1)} collective-permute-done((f32[256,512]{1,0:T(8,128)S(1)}, f32[256,512]{1,0:T(8,128)S(1)}, u32[]{:S(2)}, u32[]{:S(2)}) %collective-permute-start.2) | collective-permute-done | bytes 524320 | tf_op jit(solution)/shard_map/ppermute | solution.py:25
  18.9 0.7 split_kernel.1
  19.6 1.1 collective-permute-start.3
  20.7 0.9 collective-permute-start.4
  21.5 0.6 collective-permute-start.5
  22.2 0.7 dynamic-slice_multiply_fusion
  22.9 3.0 %collective-permute-done.3.refs_1_ = f32[64,512]{1,0:T(8,128)S(1)} collective-permute-done((f32[64,512]{1,0:T(8,128)S(1)}, f32[64,512]{1,0:T(8,128)S(1)}, u32[]{:S(2)}, u32[]{:S(2)}) %collective-permute-start.3) | collective-permute-done | bytes 131104 | tf_op jit(solution)/shard_map/ppermute | solution.py:21
  25.9 2.0 %collective-permute-start.6 = (bf16[4,512,256]{2,1,0:T(8,128)(2,1)S(1)}, bf16[4,512,256]{2,1,0:T(8,128)(2,1)S(1)}, u32[]{:S(2)}, u32[]{:S(2)}) collective-permute-start(bf16[4,512,256]{2,1,0:T(8,128)(2,1)S(1)} %get-tuple-element.71), channel_id=1, source_target_pairs={{0,4},{4,0},{1,5},{5,1},{2,6},{6,2},{3,7},{7,3},{8,12},{12,8},{9,1... | collective-permute-start | bytes 3145736 | tf_op jit(solution)/shard_map/ppermute | solution.py:25
  27.9 1.1 collective-permute-done.5.refs_3_
  29.0 0.5 collective-permute-done.1
  29.5 2.2 %collective-permute-start.7 = (bf16[4,512,256]{2,1,0:T(8,128)(2,1)S(1)}, bf16[4,512,256]{2,1,0:T(8,128)(2,1)S(1)}, u32[]{:S(2)}, u32[]{:S(2)}) collective-permute-start(bf16[4,512,256]{2,1,0:T(8,128)(2,1)S(1)} %collective-permute-done.1), channel_id=1, source_target_pairs={{0,4},{4,0},{1,5},{5,1},{2,6},{6,2},{3,7},{7,3},{8,12},{12,8},{9,1... | collective-permute-start | bytes 3145736 | tf_op jit(solution)/shard_map/ppermute | solution.py:25
  31.7 0.0 collective-permute-start.8
  31.7 2.4 %collective-permute-start.13 = (bf16[4,512,256]{2,1,0:T(8,128)(2,1)S(1)}, bf16[4,512,256]{2,1,0:T(8,128)(2,1)S(1)}, u32[]{:S(2)}, u32[]{:S(2)}) collective-permute-start(bf16[4,512,256]{2,1,0:T(8,128)(2,1)S(1)} %get-tuple-element.57), channel_id=1, source_target_pairs={{0,128},{64,192},{128,0},{192,64},{1,129},{65,193},{129,1},{193,65... | collective-permute-start | bytes 3145736 | tf_op jit(solution)/shard_map/ppermute | solution.py:21
  34.1 0.0 collective-permute-done.6
  34.1 0.0 collective-permute-done.7
  34.1 1.3 %collective-permute-done.8 = bf16[4,512,256]{2,1,0:T(8,128)(2,1)S(1)} collective-permute-done((bf16[4,512,256]{2,1,0:T(8,128)(2,1)S(1)}, bf16[4,512,256]{2,1,0:T(8,128)(2,1)S(1)}, u32[]{:S(2)}, u32[]{:S(2)}) %collective-permute-start.8) | collective-permute-done | bytes 1048608 | tf_op jit(solution)/shard_map/ppermute | solution.py:25
  35.5 2.8 %early_kernel.1 = (f32[64,1536]{1,0:T(8,128)S(1)}, f32[64,1536]{1,0:T(8,128)S(1)}, f32[64,1536]{1,0:T(8,128)S(1)}, f32[64,1536]{1,0:T(8,128)S(1)}) custom-call(s32[4]{0:T(128)S(1)} %pad_add_fusion.place, bf16[4,8,2,32,256]{4,3,2,1,0:T(8,128)(2,1)S(1)} %bitcast.16, bf16[4,8,2,32,256]{4,3,2,1,0:T(8,128)(2,1)S(1)} %bitcast.22, ...), custom_call_target="tpu_custom_call" | custom-call | flops 1 | bytes 1 | tf_op jit(solution)/shard_map/early_kernel/pallas_call | solution.py:135
  38.3 2.6 %collective-permute-start.10 = (f32[64,1536]{1,0:T(8,128)S(1)}, f32[64,1536]{1,0:T(8,128)S(1)}, u32[]{:S(2)}, u32[]{:S(2)}) collective-permute-start(f32[64,1536]{1,0:T(8,128)S(1)} %get-tuple-element.55), channel_id=1, source_target_pairs={{0,3},{1,0},{2,1},{3,2},{4,7},{5,4},{6,5},{7,6},{8,11},{9,8},{10,9... | collective-permute-start | bytes 1179656 | tf_op jit(solution)/shard_map/ppermute | solution.py:21
  40.9 1.7 %collective-permute-start.9 = (f32[64,1536]{1,0:T(8,128)S(1)}, f32[64,1536]{1,0:T(8,128)S(1)}, u32[]{:S(2)}, u32[]{:S(2)}) collective-permute-start(f32[64,1536]{1,0:T(8,128)S(1)} %get-tuple-element.54), channel_id=1, source_target_pairs={{0,2},{1,3},{2,0},{3,1},{4,6},{5,7},{6,4},{7,5},{8,10},{9,11},{10,... | collective-permute-start | bytes 1179656 | tf_op jit(solution)/shard_map/ppermute | solution.py:21
  42.6 14.8 %collective-permute-done.13 = bf16[4,512,256]{2,1,0:T(8,128)(2,1)S(1)} collective-permute-done((bf16[4,512,256]{2,1,0:T(8,128)(2,1)S(1)}, bf16[4,512,256]{2,1,0:T(8,128)(2,1)S(1)}, u32[]{:S(2)}, u32[]{:S(2)}) %collective-permute-start.13) | collective-permute-done | bytes 1048608 | tf_op jit(solution)/shard_map/ppermute | solution.py:21
  57.4 1.4 %collective-permute-start.14 = (bf16[4,512,256]{2,1,0:T(8,128)(2,1)S(1)}, bf16[4,512,256]{2,1,0:T(8,128)(2,1)S(1)}, u32[]{:S(2)}, u32[]{:S(2)}) collective-permute-start(bf16[4,512,256]{2,1,0:T(8,128)(2,1)S(1)} %collective-permute-done.13), channel_id=1, source_target_pairs={{0,4},{4,0},{1,5},{5,1},{2,6},{6,2},{3,7},{7,3},{8,12},{12,8},{9,1... | collective-permute-start | bytes 3145736 | tf_op jit(solution)/shard_map/ppermute | solution.py:25
  58.8 0.0 collective-permute-done.10.refs_2_
  58.8 0.0 collective-permute-done.11.refs_3_
  58.8 0.8 collective-permute-done.9.refs_1_
  59.6 0.1 total.3._.refs_4_
  59.7 1.5 %own_kernel.1.refs_0_ = f32[768,512]{1,0:T(8,128)S(1)} custom-call(s32[4]{0:T(128)S(1)} %pad_add_fusion.place, bf16[4,8,2,32,256]{4,3,2,1,0:T(8,128)(2,1)S(1)} %bitcast.19, bf16[4,8,2,32,256]{4,3,2,1,0:T(8,128)(2,1)S(1)} %bitcast.17, bf16[4,8,2,32,256]{4,3,2,1,0:T(8,128)(2,1)S(1)} %bitcast.21, bf16[4,8,2,32,256]{4,3,2,1,0:T(8,128)(2,1)S(1)} %bitcast.28, ...), custom_call_target="tpu_custom_call" | custom-call | flops 1 | bytes 1 | tf_op jit(solution)/shard_map/own_kernel/pallas_call | solution.py:135
  61.3 1.9 %late_kernel.1 = (f32[128,512]{1,0:T(8,128)S(1)}, f32[128,512]{1,0:T(8,128)S(1)}, f32[128,512]{1,0:T(8,128)S(1)}, f32[128,512]{1,0:T(8,128)S(1)}, f32[64,512]{1,...) custom-call(s32[4]{0:T(128)S(1)} %pad_add_fusion.place, ...), custom_call_target="tpu_custom_call" | custom-call | flops 1 | bytes 1 | tf_op jit(solution)/shard_map/late_kernel/pallas_call | solution.py:135
  63.2 2.6 %collective-permute-start.18 = (f32[128,512]{1,0:T(8,128)S(1)}, f32[128,512]{1,0:T(8,128)S(1)}, u32[]{:S(2)}, u32[]{:S(2)}) collective-permute-start(f32[128,512]{1,0:T(8,128)S(1)} %get-tuple-element.63), channel_id=1, source_target_pairs={{0,2},{1,3},{2,0},{3,1},{4,6},{5,7},{6,4},{7,5},{8,10},{9,11},{10,... | collective-permute-start | bytes 786440 | tf_op jit(solution)/shard_map/ppermute | solution.py:21
  65.8 0.9 collective-permute-start.19
  66.7 0.6 collective-permute-start.20
  67.3 1.2 collective-permute-start.12
  68.5 0.6 collective-permute-start.15
  69.1 3.6 %collective-permute-done.12.refs_4_.refs_5_ = f32[64,512]{1,0:T(8,128)S(1)} collective-permute-done((f32[64,512]{1,0:T(8,128)S(1)}, f32[64,512]{1,0:T(8,128)S(1)}, u32[]{:S(2)}, u32[]{:S(2)}) %collective-permute-start.12) | collective-permute-done | bytes 131104 | tf_op jit(solution)/shard_map/ppermute | solution.py:21
  72.7 2.1 %collective-permute-start.16 = (f32[64,512]{1,0:T(8,128)S(1)}, f32[64,512]{1,0:T(8,128)S(1)}, u32[]{:S(2)}, u32[]{:S(2)}) collective-permute-start(f32[64,512]{1,0:T(8,128)S(1)} %get-tuple-element.60), channel_id=1, source_target_pairs={{0,3},{1,0},{2,1},{3,2},{4,7},{5,4},{6,5},{7,6},{8,11},{9,8},{10,9... | collective-permute-start | bytes 393224 | tf_op jit(solution)/shard_map/ppermute | solution.py:21
  74.8 0.0 collective-permute-done.18.refs_1_
  74.8 0.0 collective-permute-start.17
  74.8 3.1 %collective-permute-done.19.refs_2_ = f32[128,512]{1,0:T(8,128)S(1)} collective-permute-done((f32[128,512]{1,0:T(8,128)S(1)}, f32[128,512]{1,0:T(8,128)S(1)}, u32[]{:S(2)}, u32[]{:S(2)}) %collective-permute-start.19) | collective-permute-done | bytes 262176 | tf_op jit(solution)/shard_map/ppermute | solution.py:21
  77.8 1.8 %collective-permute-done.20.refs_3_ = f32[128,512]{1,0:T(8,128)S(1)} collective-permute-done((f32[128,512]{1,0:T(8,128)S(1)}, f32[128,512]{1,0:T(8,128)S(1)}, u32[]{:S(2)}, u32[]{:S(2)}) %collective-permute-start.20) | collective-permute-done | bytes 262176 | tf_op jit(solution)/shard_map/ppermute | solution.py:21
  79.7 1.2 collective-permute-start.21
  80.8 1.6 %collective-permute-start.22 = (f32[64,512]{1,0:T(8,128)S(1)}, f32[64,512]{1,0:T(8,128)S(1)}, u32[]{:S(2)}, u32[]{:S(2)}) collective-permute-start(f32[64,512]{1,0:T(8,128)S(1)} %get-tuple-element.75), channel_id=1, source_target_pairs={{0,192},{64,0},{128,64},{192,128},{1,193},{65,1},{129,65},{193,129... | collective-permute-start | bytes 393224 | tf_op jit(solution)/shard_map/ppermute | solution.py:21
  82.4 1.1 collective-permute-done.16.refs_2_
  83.5 0.0 collective-permute-done.17.refs_3_
  83.5 1.3 collective-permute-done.21.refs_7_
  84.8 1.0 pack.1
  85.8 5.7 %collective-permute-start.24 = (f32[8,8960]{1,0:T(8,128)S(1)}, f32[8,8960]{1,0:T(8,128)S(1)}, u32[]{:S(2)}, u32[]{:S(2)}) collective-permute-start(f32[8,8960]{1,0:T(8,128)S(1)} %get-tuple-element.68), channel_id=1, source_target_pairs={{0,56},{8,0},{16,8},{24,16},{32,24},{40,32},{48,40},{56,48},{1,57}... | collective-permute-start | bytes 860168 | tf_op jit(solution)/shard_map/ppermute | solution.py:21
  91.4 3.6 %collective-permute-done.24 = f32[8,8960]{1,0:T(8,128)S(1)} collective-permute-done((f32[8,8960]{1,0:T(8,128)S(1)}, f32[8,8960]{1,0:T(8,128)S(1)}, u32[]{:S(2)}, u32[]{:S(2)}) %collective-permute-start.24) | collective-permute-done | bytes 286752 | tf_op jit(solution)/shard_map/ppermute | solution.py:21
  95.0 3.1 %collective-permute-done.23 = f32[8,8960]{1,0:T(8,128)S(1)} collective-permute-done((f32[8,8960]{1,0:T(8,128)S(1)}, f32[8,8960]{1,0:T(8,128)S(1)}, u32[]{:S(2)}, u32[]{:S(2)}) %collective-permute-start.23) | collective-permute-done | bytes 286752 | tf_op jit(solution)/shard_map/ppermute | solution.py:21
  98.2 0.1 collective-permute-start.25
  98.3 4.5 %collective-permute-start.26 = (f32[8,3584]{1,0:T(8,128)S(1)}, f32[8,3584]{1,0:T(8,128)S(1)}, u32[]{:S(2)}, u32[]{:S(2)}) collective-permute-start(f32[8,3584]{1,0:T(8,128)S(1)} %pad_maximum_fusion.1), channel_id=1, source_target_pairs={{0,40},{8,48},{16,56},{24,0},{32,8},{40,16},{48,24},{56,32},{1,41}... | collective-permute-start | bytes 344072 | tf_op jit(solution)/shard_map/ppermute | solution.py:21
  102.8 3.2 %collective-permute-done.25 = f32[8,3584]{1,0:T(8,128)S(1)} collective-permute-done((f32[8,3584]{1,0:T(8,128)S(1)}, f32[8,3584]{1,0:T(8,128)S(1)}, u32[]{:S(2)}, u32[]{:S(2)}) %collective-permute-start.25) | collective-permute-done | bytes 114720 | tf_op jit(solution)/shard_map/ppermute | solution.py:21
  106.1 0.6 spread_kernel.1
  106.8 20.9 %all_to_all.5.pieces = f32[32,8,128]{2,1,0:T(8,128)S(1)} all-to-all(f32[32,8,128]{2,1,0:T(8,128)S(1)} %spread_kernel.1), channel_id=1, replica_groups=mesh['row'=4,'z'=8,'core'=2,'aux'=4] {'row','core','aux'}, dimensions={0} | all-to-all | bytes 262144 | tf_op jit(solution)/shard_map/all_to_all | solution.py:331
  127.6 1.4 %finish_kernel.1 = f32[8,2048]{1,0:T(8,128)} custom-call(s32[4]{0:T(128)S(1)} %pad_add_fusion.place, f32[8,3584]{1,0:T(8,128)S(1)} %fusion.1.rows, f32[32,8,128]{2,1,0:T(8,128)S(1)} %all_to_all.5.pieces), custom_call_target="tpu_custom_call" | custom-call | flops 1 | bytes 1 | tf_op jit(solution)/shard_map/finish_kernel/pallas_call | solution.py:174
  (24 shorter events, 0.3 us)
Async XLA Ops:
  0.0 7.4 %copy-start.1 = (s32[64,16]{0,1:T(8,128)S(1)}, s32[64,16]{0,1:T(8,128)}, u32[]{:S(2)}) copy-start(s32[64,16]{0,1:T(8,128)} %param.3) | copy-start | bytes 12292
  3.8 25.2 %collective-permute-start = (bf16[4,512,256]{2,1,0:T(8,128)(2,1)}, bf16[4,512,256]{2,1,0:T(8,128)(2,1)S(1)}, u32[]{:S(2)}, u32[]{:S(2)}) collective-permute-start(bf16[4,512,256]{2,1,0:T(8,128)(2,1)} %get-tuple-element.38), channel_id=1, source_target_pairs={{0,64},{64,128},{128,192},{192,0},{1,65},{65,129},{129,193},{193,1... | collective-permute-start | bytes 3145736 | tf_op jit(solution)/shard_map/ppermute | solution.py:21
  5.9 23.5 %collective-permute-start.1 = (bf16[4,512,256]{2,1,0:T(8,128)(2,1)S(1)}, bf16[4,512,256]{2,1,0:T(8,128)(2,1)S(1)}, u32[]{:S(2)}, u32[]{:S(2)}) collective-permute-start(bf16[4,512,256]{2,1,0:T(8,128)(2,1)S(1)} %get-tuple-element.39), channel_id=1, source_target_pairs={{0,192},{64,0},{128,64},{192,128},{1,193},{65,1},{129,65},{193,129... | collective-permute-start | bytes 3145736 | tf_op jit(solution)/shard_map/ppermute | solution.py:21
  7.5 2.2 %copy-start = (bf16[16,512,256]{2,1,0:T(8,128)(2,1)S(1)}, bf16[16,512,256]{2,1,0:T(8,128)(2,1)}, u32[]{:S(2)}) copy-start(bf16[16,512,256]{2,1,0:T(8,128)(2,1)} %slab) | copy-start | bytes 12582916
  14.4 4.5 %collective-permute-start.2 = (f32[256,512]{1,0:T(8,128)S(1)}, f32[256,512]{1,0:T(8,128)S(1)}, u32[]{:S(2)}, u32[]{:S(2)}) collective-permute-start(f32[256,512]{1,0:T(8,128)S(1)} %get-tuple-element.42), channel_id=1, source_target_pairs={{0,4},{4,0},{1,5},{5,1},{2,6},{6,2},{3,7},{7,3},{8,12},{12,8},{9,1... | collective-permute-start | bytes 1572872 | tf_op jit(solution)/shard_map/ppermute | solution.py:25
  19.6 6.3 %collective-permute-start.3 = (f32[64,512]{1,0:T(8,128)S(1)}, f32[64,512]{1,0:T(8,128)S(1)}, u32[]{:S(2)}, u32[]{:S(2)}) collective-permute-start(f32[64,512]{1,0:T(8,128)S(1)} %get-tuple-element.44), channel_id=1, source_target_pairs={{0,2},{1,3},{2,0},{3,1},{4,6},{5,7},{6,4},{7,5},{8,10},{9,11},{10,... | collective-permute-start | bytes 393224 | tf_op jit(solution)/shard_map/ppermute | solution.py:21
  20.7 7.2 %collective-permute-start.4 = (f32[64,512]{1,0:T(8,128)S(1)}, f32[64,512]{1,0:T(8,128)S(1)}, u32[]{:S(2)}, u32[]{:S(2)}) collective-permute-start(f32[64,512]{1,0:T(8,128)S(1)} %get-tuple-element.45), channel_id=1, source_target_pairs={{0,3},{1,0},{2,1},{3,2},{4,7},{5,4},{6,5},{7,6},{8,11},{9,8},{10,9... | collective-permute-start | bytes 393224 | tf_op jit(solution)/shard_map/ppermute | solution.py:21
  21.5 7.4 %collective-permute-start.5 = (f32[64,512]{1,0:T(8,128)S(1)}, f32[64,512]{1,0:T(8,128)S(1)}, u32[]{:S(2)}, u32[]{:S(2)}) collective-permute-start(f32[64,512]{1,0:T(8,128)S(1)} %get-tuple-element.46), channel_id=1, source_target_pairs={{0,1},{1,2},{2,3},{3,0},{4,5},{5,6},{6,7},{7,4},{8,9},{9,10},{10,1... | collective-permute-start | bytes 393224 | tf_op jit(solution)/shard_map/ppermute | solution.py:21
  25.9 8.2 %collective-permute-start.6 = (bf16[4,512,256]{2,1,0:T(8,128)(2,1)S(1)}, bf16[4,512,256]{2,1,0:T(8,128)(2,1)S(1)}, u32[]{:S(2)}, u32[]{:S(2)}) collective-permute-start(bf16[4,512,256]{2,1,0:T(8,128)(2,1)S(1)} %get-tuple-element.71), channel_id=1, source_target_pairs={{0,4},{4,0},{1,5},{5,1},{2,6},{6,2},{3,7},{7,3},{8,12},{12,8},{9,1... | collective-permute-start | bytes 3145736 | tf_op jit(solution)/shard_map/ppermute | solution.py:25
  29.5 4.7 %collective-permute-start.7 = (bf16[4,512,256]{2,1,0:T(8,128)(2,1)S(1)}, bf16[4,512,256]{2,1,0:T(8,128)(2,1)S(1)}, u32[]{:S(2)}, u32[]{:S(2)}) collective-permute-start(bf16[4,512,256]{2,1,0:T(8,128)(2,1)S(1)} %collective-permute-done.1), channel_id=1, source_target_pairs={{0,4},{4,0},{1,5},{5,1},{2,6},{6,2},{3,7},{7,3},{8,12},{12,8},{9,1... | collective-permute-start | bytes 3145736 | tf_op jit(solution)/shard_map/ppermute | solution.py:25
  31.7 3.8 %collective-permute-start.8 = (bf16[4,512,256]{2,1,0:T(8,128)(2,1)S(1)}, bf16[4,512,256]{2,1,0:T(8,128)(2,1)S(1)}, u32[]{:S(2)}, u32[]{:S(2)}) collective-permute-start(bf16[4,512,256]{2,1,0:T(8,128)(2,1)S(1)} %collective-permute-done), channel_id=1, source_target_pairs={{0,4},{4,0},{1,5},{5,1},{2,6},{6,2},{3,7},{7,3},{8,12},{12,8},{9,1... | collective-permute-start | bytes 3145736 | tf_op jit(solution)/shard_map/ppermute | solution.py:25
  31.7 25.7 %collective-permute-start.13 = (bf16[4,512,256]{2,1,0:T(8,128)(2,1)S(1)}, bf16[4,512,256]{2,1,0:T(8,128)(2,1)S(1)}, u32[]{:S(2)}, u32[]{:S(2)}) collective-permute-start(bf16[4,512,256]{2,1,0:T(8,128)(2,1)S(1)} %get-tuple-element.57), channel_id=1, source_target_pairs={{0,128},{64,192},{128,0},{192,64},{1,129},{65,193},{129,1},{193,65... | collective-permute-start | bytes 3145736 | tf_op jit(solution)/shard_map/ppermute | solution.py:21
  38.3 20.5 %collective-permute-start.10 = (f32[64,1536]{1,0:T(8,128)S(1)}, f32[64,1536]{1,0:T(8,128)S(1)}, u32[]{:S(2)}, u32[]{:S(2)}) collective-permute-start(f32[64,1536]{1,0:T(8,128)S(1)} %get-tuple-element.55), channel_id=1, source_target_pairs={{0,3},{1,0},{2,1},{3,2},{4,7},{5,4},{6,5},{7,6},{8,11},{9,8},{10,9... | collective-permute-start | bytes 1179656 | tf_op jit(solution)/shard_map/ppermute | solution.py:21
  40.9 17.9 %collective-permute-start.11 = (f32[64,1536]{1,0:T(8,128)S(1)}, f32[64,1536]{1,0:T(8,128)S(1)}, u32[]{:S(2)}, u32[]{:S(2)}) collective-permute-start(f32[64,1536]{1,0:T(8,128)S(1)} %get-tuple-element.56), channel_id=1, source_target_pairs={{0,1},{1,2},{2,3},{3,0},{4,5},{5,6},{6,7},{7,4},{8,9},{9,10},{10,1... | collective-permute-start | bytes 1179656 | tf_op jit(solution)/shard_map/ppermute | solution.py:21
  40.9 18.7 %collective-permute-start.9 = (f32[64,1536]{1,0:T(8,128)S(1)}, f32[64,1536]{1,0:T(8,128)S(1)}, u32[]{:S(2)}, u32[]{:S(2)}) collective-permute-start(f32[64,1536]{1,0:T(8,128)S(1)} %get-tuple-element.54), channel_id=1, source_target_pairs={{0,2},{1,3},{2,0},{3,1},{4,6},{5,7},{6,4},{7,5},{8,10},{9,11},{10,... | collective-permute-start | bytes 1179656 | tf_op jit(solution)/shard_map/ppermute | solution.py:21
  57.4 3.8 %collective-permute-start.14 = (bf16[4,512,256]{2,1,0:T(8,128)(2,1)S(1)}, bf16[4,512,256]{2,1,0:T(8,128)(2,1)S(1)}, u32[]{:S(2)}, u32[]{:S(2)}) collective-permute-start(bf16[4,512,256]{2,1,0:T(8,128)(2,1)S(1)} %collective-permute-done.13), channel_id=1, source_target_pairs={{0,4},{4,0},{1,5},{5,1},{2,6},{6,2},{3,7},{7,3},{8,12},{12,8},{9,1... | collective-permute-start | bytes 3145736 | tf_op jit(solution)/shard_map/ppermute | solution.py:25
  63.2 11.6 %collective-permute-start.18 = (f32[128,512]{1,0:T(8,128)S(1)}, f32[128,512]{1,0:T(8,128)S(1)}, u32[]{:S(2)}, u32[]{:S(2)}) collective-permute-start(f32[128,512]{1,0:T(8,128)S(1)} %get-tuple-element.63), channel_id=1, source_target_pairs={{0,2},{1,3},{2,0},{3,1},{4,6},{5,7},{6,4},{7,5},{8,10},{9,11},{10,... | collective-permute-start | bytes 786440 | tf_op jit(solution)/shard_map/ppermute | solution.py:21
  65.8 12.0 %collective-permute-start.19 = (f32[128,512]{1,0:T(8,128)S(1)}, f32[128,512]{1,0:T(8,128)S(1)}, u32[]{:S(2)}, u32[]{:S(2)}) collective-permute-start(f32[128,512]{1,0:T(8,128)S(1)} %get-tuple-element.64), channel_id=1, source_target_pairs={{0,3},{1,0},{2,1},{3,2},{4,7},{5,4},{6,5},{7,6},{8,11},{9,8},{10,9... | collective-permute-start | bytes 786440 | tf_op jit(solution)/shard_map/ppermute | solution.py:21
  66.7 12.9 %collective-permute-start.20 = (f32[128,512]{1,0:T(8,128)S(1)}, f32[128,512]{1,0:T(8,128)S(1)}, u32[]{:S(2)}, u32[]{:S(2)}) collective-permute-start(f32[128,512]{1,0:T(8,128)S(1)} %get-tuple-element.65), channel_id=1, source_target_pairs={{0,1},{1,2},{2,3},{3,0},{4,5},{5,6},{6,7},{7,4},{8,9},{9,10},{10,1... | collective-permute-start | bytes 786440 | tf_op jit(solution)/shard_map/ppermute | solution.py:21
  67.3 5.4 %collective-permute-start.12 = (f32[64,512]{1,0:T(8,128)S(1)}, f32[64,512]{1,0:T(8,128)S(1)}, u32[]{:S(2)}, u32[]{:S(2)}) collective-permute-start(f32[64,512]{1,0:T(8,128)S(1)} %slice.52), channel_id=1, source_target_pairs={{0,64},{64,128},{128,192},{192,0},{1,65},{65,129},{129,193},{193,1... | collective-permute-start | bytes 393224 | tf_op jit(solution)/shard_map/ppermute | solution.py:21
  68.5 14.0 %collective-permute-start.15 = (f32[64,512]{1,0:T(8,128)S(1)}, f32[64,512]{1,0:T(8,128)S(1)}, u32[]{:S(2)}, u32[]{:S(2)}) collective-permute-start(f32[64,512]{1,0:T(8,128)S(1)} %get-tuple-element.59), channel_id=1, source_target_pairs={{0,2},{1,3},{2,0},{3,1},{4,6},{5,7},{6,4},{7,5},{8,10},{9,11},{10,... | collective-permute-start | bytes 393224 | tf_op jit(solution)/shard_map/ppermute | solution.py:21
  72.7 10.8 %collective-permute-start.16 = (f32[64,512]{1,0:T(8,128)S(1)}, f32[64,512]{1,0:T(8,128)S(1)}, u32[]{:S(2)}, u32[]{:S(2)}) collective-permute-start(f32[64,512]{1,0:T(8,128)S(1)} %get-tuple-element.60), channel_id=1, source_target_pairs={{0,3},{1,0},{2,1},{3,2},{4,7},{5,4},{6,5},{7,6},{8,11},{9,8},{10,9... | collective-permute-start | bytes 393224 | tf_op jit(solution)/shard_map/ppermute | solution.py:21
  74.8 8.7 %collective-permute-start.17 = (f32[64,512]{1,0:T(8,128)S(1)}, f32[64,512]{1,0:T(8,128)S(1)}, u32[]{:S(2)}, u32[]{:S(2)}) collective-permute-start(f32[64,512]{1,0:T(8,128)S(1)} %get-tuple-element.61), channel_id=1, source_target_pairs={{0,1},{1,2},{2,3},{3,0},{4,5},{5,6},{6,7},{7,4},{8,9},{9,10},{10,1... | collective-permute-start | bytes 393224 | tf_op jit(solution)/shard_map/ppermute | solution.py:21
  79.7 5.1 %collective-permute-start.21 = (f32[64,512]{1,0:T(8,128)S(1)}, f32[64,512]{1,0:T(8,128)S(1)}, u32[]{:S(2)}, u32[]{:S(2)}) collective-permute-start(f32[64,512]{1,0:T(8,128)S(1)} %get-tuple-element.76), channel_id=1, source_target_pairs={{0,64},{64,128},{128,192},{192,0},{1,65},{65,129},{129,193},{193,1... | collective-permute-start | bytes 393224 | tf_op jit(solution)/shard_map/ppermute | solution.py:21
  80.8 3.9 %collective-permute-start.22 = (f32[64,512]{1,0:T(8,128)S(1)}, f32[64,512]{1,0:T(8,128)S(1)}, u32[]{:S(2)}, u32[]{:S(2)}) collective-permute-start(f32[64,512]{1,0:T(8,128)S(1)} %get-tuple-element.75), channel_id=1, source_target_pairs={{0,192},{64,0},{128,64},{192,128},{1,193},{65,1},{129,65},{193,129... | collective-permute-start | bytes 393224 | tf_op jit(solution)/shard_map/ppermute | solution.py:21
  85.8 9.2 %collective-permute-start.24 = (f32[8,8960]{1,0:T(8,128)S(1)}, f32[8,8960]{1,0:T(8,128)S(1)}, u32[]{:S(2)}, u32[]{:S(2)}) collective-permute-start(f32[8,8960]{1,0:T(8,128)S(1)} %get-tuple-element.68), channel_id=1, source_target_pairs={{0,56},{8,0},{16,8},{24,16},{32,24},{40,32},{48,40},{56,48},{1,57}... | collective-permute-start | bytes 860168 | tf_op jit(solution)/shard_map/ppermute | solution.py:21
  91.4 6.7 %collective-permute-start.23 = (f32[8,8960]{1,0:T(8,128)S(1)}, f32[8,8960]{1,0:T(8,128)S(1)}, u32[]{:S(2)}, u32[]{:S(2)}) collective-permute-start(f32[8,8960]{1,0:T(8,128)S(1)} %get-tuple-element.67), channel_id=1, source_target_pairs={{0,8},{8,16},{16,24},{24,32},{32,40},{40,48},{48,56},{56,0},{1,9},... | collective-permute-start | bytes 860168 | tf_op jit(solution)/shard_map/ppermute | solution.py:21
  98.2 7.9 %collective-permute-start.25 = (f32[8,3584]{1,0:T(8,128)S(1)}, f32[8,3584]{1,0:T(8,128)S(1)}, u32[]{:S(2)}, u32[]{:S(2)}) collective-permute-start(f32[8,3584]{1,0:T(8,128)S(1)} %pad_maximum_fusion), channel_id=1, source_target_pairs={{0,24},{8,32},{16,40},{24,48},{32,56},{40,0},{48,8},{56,16},{1,25}... | collective-permute-start | bytes 344072 | tf_op jit(solution)/shard_map/ppermute | solution.py:21
  98.3 7.8 %collective-permute-start.26 = (f32[8,3584]{1,0:T(8,128)S(1)}, f32[8,3584]{1,0:T(8,128)S(1)}, u32[]{:S(2)}, u32[]{:S(2)}) collective-permute-start(f32[8,3584]{1,0:T(8,128)S(1)} %pad_maximum_fusion.1), channel_id=1, source_target_pairs={{0,40},{8,48},{16,56},{24,0},{32,8},{40,16},{48,24},{56,32},{1,41}... | collective-permute-start | bytes 344072 | tf_op jit(solution)/shard_map/ppermute | solution.py:21

commit v6 on v5

--- a/solution.py
+++ b/solution.py
@@ -147,12 +147,14 @@
     peers = out.shape[0] // ys
     n = rows.shape[1] // 7
     size = n // peers
-    out[...] = jnp.zeros_like(out)
     for step in range(1, ys):
         first = lax.rem(place[1] + step, ys) * peers
         for k in range(peers):
             begin = (ys - 1 + step) * n + k * size
             out[first + k, :, :size] = rows[:, begin : begin + size]
+            out[first + k, :, size:] = jnp.zeros((8, out.shape[2] - size), jnp.float32)
+    for k in range(peers):
+        out[place[1] * peers + k] = jnp.zeros(out.shape[1:], jnp.float32)
 
 
 def finish_kernel(ys, place, rows, pieces, out):
@@ -182,9 +184,9 @@
     )(*operands)
 
 
-def over_aux(parts, xs):
+def over_aux(parts, xs, order=(2, 3, 1)):
     there = {d: shift(parts[d], "aux", d, xs) for d in (2, 1, 3)}
-    return [parts[0], there[2], there[3], there[1]]
+    return [parts[0], *(there[d] for d in order)]
 
 
 def turn(block, zs):
@@ -303,7 +305,7 @@
     mine2 = sibling(mine)
     kept, given = diagonal(place, screen, block, zs)
     diag = pairs(split_kernel, place, (kept, sibling(given)), [(zs * 8, n)] * xs, limit=4 * MIB)
-    diag = over_aux(diag, xs)
+    diag = over_aux(diag, xs, (1, 2, 3))
     below, above, far, diag = lax.optimization_barrier((below, above, far, diag))
     across = shift(far, "row", 2, ys)
 
@@ -313,7 +315,7 @@
     mine, mine2 = grouped(mine, mine2)
     below, above = grouped(below, sibling(below)), grouped(above, sibling(above))
     early_parts = pairs(early_kernel, place, (mine, mine2, *above, *below), [(zs * 8, 3 * n)] * xs)
-    early = total(over_aux(early_parts, xs), flops=SOME)
+    early = total(over_aux(early_parts, xs, (1, 2, 3)), flops=SOME)
     third = shift(early[:, n : 2 * n], "row", 1, ys)
     (across_own,) = grouped(across)
     (across_sibling,) = grouped(sibling(across))

time: 129 us -> 129 us (level)
  waiting for transfers between devices: 43.8 us -> 41.5 us
  starting transfers between devices: 42.5 us -> 44.4 us
    ppermute x22, waiting for transfers between devices: 40.9 us -> 38.5 us  [shift(): lax.ppermute(value, axis, [(i, (i + step) % size) for i in range(size)])]
  transfers between devices with their start and end apart: 27 -> 27, of which waited for: 15 -> 14; matrix products, arithmetic and copies ran while one was open for 1% -> 1% of each run, Pallas kernels for 8% -> 8%
where the time goes in v6:
time: 129 us
  starting transfers between devices  44.4 us (34%)
  waiting for transfers between devices  41.5 us (32%)
  blocking collectives  21.3 us (17%)
  Pallas kernels  14.8 us (11%)
  other arithmetic  4.43 us (3%)
  local copies, waits for them, and re-layouts  2.52 us (2%)
    ppermute x22, waiting for transfers between devices, shift(): lax.ppermute(value, axis, [(i, (i + step) % size) for i in range(size)])  38.5 us
    ppermute x22, starting transfers between devices, shift(): lax.ppermute(value, axis, [(i, (i + step) % size) for i in range(size)])  34.7 us
    all_to_all x1, blocking collectives, body(): pieces = lax.all_to_all(pieces, ('row', 'core', 'aux'), 0, 0, tiled=True)  21.3 us
    ppermute x5, starting transfers between devices, sibling(): return lax.ppermute(value, 'core', [(0, 1), (1, 0)])  9.72 us
    pallas_call x4, Pallas kernels, pairs(): pl.pallas_call(kernel, in_specs=[SCALARS] + [ANYWHERE] * len(operands) +...  6.94 us
    pallas_call x1, Pallas kernels, diagonal(): pl.pallas_call(diagonal_kernel, grid=(depth // group,), in_specs=[SCALARS...  4.62 us
    mul x2, other arithmetic, slab(): part * lax.dynamic_slice(keep, (first, 0), (quarter, mrows))[:, :, None]  3.41 us
    ppermute x5, waiting for transfers between devices, sibling(): return lax.ppermute(value, 'core', [(0, 1), (1, 0)])  2.95 us
  transfers between devices with their start and end apart: 27, of which 14 were waited for; matrix products, arithmetic and copies ran while one was open for 1% of the time, Pallas kernels for 8%

profile of v6, /device:TPU:1, one launch (start us, length us, event | category | flops | bytes accessed | tf_op | source)
XLA Modules:
  0.0 129.2 jit_solution(5372179008516926014)
XLA Ops:
  0.0 0.8 dynamic-slice_convert_fusion
  0.8 0.1 copy.3
  0.9 0.1 broadcast_in_dim.2
  1.1 2.7 %dynamic-slice_multiply_fusion.2 = (bf16[4,512,256]{2,1,0:T(8,128)(2,1)S(1)}, bf16[4,512,256]{2,1,0:T(8,128)(2,1)}) fusion(bf16[16,512,256]{2,1,0:T(8,128)(2,1)} %slab, s32[]{:T(128)S(6)} %select_n.25, bf16[4,512]{1,0:T(4,128)(2,1)S(1)} %get-tuple-element.83, bf16[4,512]{1,0:T(4,128)(2,1)S(1)} %get-tuple-element.84, s32[]{:T(128)S(6)} %select_n.22), kind=kLoop, calls=%fused_computation.2 | loop fusion | flops 1048576 | bytes 4202504 | tf_op jit(solution)/shard_map/mul | solution.py:298
  3.8 2.1 %collective-permute-start = (bf16[4,512,256]{2,1,0:T(8,128)(2,1)}, bf16[4,512,256]{2,1,0:T(8,128)(2,1)S(1)}, u32[]{:S(2)}, u32[]{:S(2)}) collective-permute-start(bf16[4,512,256]{2,1,0:T(8,128)(2,1)} %get-tuple-element.38), channel_id=1, source_target_pairs={{0,64},{64,128},{128,192},{192,0},{1,65},{65,129},{129,193},{193,1... | collective-permute-start | bytes 3145736 | tf_op jit(solution)/shard_map/ppermute | solution.py:21
  5.9 1.4 %collective-permute-start.1 = (bf16[4,512,256]{2,1,0:T(8,128)(2,1)S(1)}, bf16[4,512,256]{2,1,0:T(8,128)(2,1)S(1)}, u32[]{:S(2)}, u32[]{:S(2)}) collective-permute-start(bf16[4,512,256]{2,1,0:T(8,128)(2,1)S(1)} %get-tuple-element.39), channel_id=1, source_target_pairs={{0,192},{64,0},{128,64},{192,128},{1,193},{65,1},{129,65},{193,129... | collective-permute-start | bytes 3145736 | tf_op jit(solution)/shard_map/ppermute | solution.py:21
  7.4 0.1 copy.4.screen
  7.5 0.1 pad_add_fusion.place
  7.5 2.2 %copy-done = bf16[16,512,256]{2,1,0:T(8,128)(2,1)S(1)} copy-done((bf16[16,512,256]{2,1,0:T(8,128)(2,1)S(1)}, bf16[16,512,256]{2,1,0:T(8,128)(2,1)}, u32[]{:S(2)}) %copy-start) | copy-done | bytes 4194328
  9.7 4.6 %diagonal.1 = (f32[256,512]{1,0:T(8,128)S(1)}, f32[256,512]{1,0:T(8,128)S(1)}) custom-call(s32[4]{0:T(128)S(1)} %pad_add_fusion.place, s32[64,16]{1,0:T(8,128)S(1)} %copy.4.screen, bf16[16,512,256]{2,1,0:T(8,128)(2,1)S(1)} %copy-done), custom_call_target="tpu_custom_call" | custom-call | flops 1 | bytes 1 | tf_op jit(solution)/shard_map/diagonal/pallas_call | solution.py:68
  14.4 3.0 %collective-permute-start.2 = (f32[256,512]{1,0:T(8,128)S(1)}, f32[256,512]{1,0:T(8,128)S(1)}, u32[]{:S(2)}, u32[]{:S(2)}) collective-permute-start(f32[256,512]{1,0:T(8,128)S(1)} %get-tuple-element.42), channel_id=1, source_target_pairs={{0,4},{4,0},{1,5},{5,1},{2,6},{6,2},{3,7},{7,3},{8,12},{12,8},{9,1... | collective-permute-start | bytes 1572872 | tf_op jit(solution)/shard_map/ppermute | solution.py:25
  17.4 1.5 %collective-permute-done.2.got = f32[256,512]{1,0:T(8,128)S(1)} collective-permute-done((f32[256,512]{1,0:T(8,128)S(1)}, f32[256,512]{1,0:T(8,128)S(1)}, u32[]{:S(2)}, u32[]{:S(2)}) %collective-permute-start.2) | collective-permute-done | bytes 524320 | tf_op jit(solution)/shard_map/ppermute | solution.py:25
  18.9 0.7 split_kernel.1
  19.6 0.1 collective-permute-start.3
  19.7 1.9 %collective-permute-start.4 = (f32[64,512]{1,0:T(8,128)S(1)}, f32[64,512]{1,0:T(8,128)S(1)}, u32[]{:S(2)}, u32[]{:S(2)}) collective-permute-start(f32[64,512]{1,0:T(8,128)S(1)} %get-tuple-element.45), channel_id=1, source_target_pairs={{0,2},{1,3},{2,0},{3,1},{4,6},{5,7},{6,4},{7,5},{8,10},{9,11},{10,... | collective-permute-start | bytes 393224 | tf_op jit(solution)/shard_map/ppermute | solution.py:21
  21.6 1.2 collective-permute-start.5
  22.7 0.7 dynamic-slice_multiply_fusion
  23.4 2.9 %collective-permute-done.3.refs_1_ = f32[64,512]{1,0:T(8,128)S(1)} collective-permute-done((f32[64,512]{1,0:T(8,128)S(1)}, f32[64,512]{1,0:T(8,128)S(1)}, u32[]{:S(2)}, u32[]{:S(2)}) %collective-permute-start.3) | collective-permute-done | bytes 131104 | tf_op jit(solution)/shard_map/ppermute | solution.py:21
  26.3 3.3 %collective-permute-start.6 = (bf16[4,512,256]{2,1,0:T(8,128)(2,1)S(1)}, bf16[4,512,256]{2,1,0:T(8,128)(2,1)S(1)}, u32[]{:S(2)}, u32[]{:S(2)}) collective-permute-start(bf16[4,512,256]{2,1,0:T(8,128)(2,1)S(1)} %get-tuple-element.71), channel_id=1, source_target_pairs={{0,4},{4,0},{1,5},{5,1},{2,6},{6,2},{3,7},{7,3},{8,12},{12,8},{9,1... | collective-permute-start | bytes 3145736 | tf_op jit(solution)/shard_map/ppermute | solution.py:25
  29.6 0.0 collective-permute-done.4.refs_2_
  29.6 0.0 collective-permute-done.5.refs_3_
  29.6 0.0 collective-permute-done.1
  29.6 2.1 %collective-permute-start.7 = (bf16[4,512,256]{2,1,0:T(8,128)(2,1)S(1)}, bf16[4,512,256]{2,1,0:T(8,128)(2,1)S(1)}, u32[]{:S(2)}, u32[]{:S(2)}) collective-permute-start(bf16[4,512,256]{2,1,0:T(8,128)(2,1)S(1)} %collective-permute-done.1), channel_id=1, source_target_pairs={{0,4},{4,0},{1,5},{5,1},{2,6},{6,2},{3,7},{7,3},{8,12},{12,8},{9,1... | collective-permute-start | bytes 3145736 | tf_op jit(solution)/shard_map/ppermute | solution.py:25
  31.7 0.0 collective-permute-start.8
  31.7 2.4 %collective-permute-start.13 = (bf16[4,512,256]{2,1,0:T(8,128)(2,1)S(1)}, bf16[4,512,256]{2,1,0:T(8,128)(2,1)S(1)}, u32[]{:S(2)}, u32[]{:S(2)}) collective-permute-start(bf16[4,512,256]{2,1,0:T(8,128)(2,1)S(1)} %get-tuple-element.57), channel_id=1, source_target_pairs={{0,128},{64,192},{128,0},{192,64},{1,129},{65,193},{129,1},{193,65... | collective-permute-start | bytes 3145736 | tf_op jit(solution)/shard_map/ppermute | solution.py:21
  34.1 0.0 collective-permute-done.6
  34.1 0.0 collective-permute-done.7
  34.1 1.3 %collective-permute-done.8 = bf16[4,512,256]{2,1,0:T(8,128)(2,1)S(1)} collective-permute-done((bf16[4,512,256]{2,1,0:T(8,128)(2,1)S(1)}, bf16[4,512,256]{2,1,0:T(8,128)(2,1)S(1)}, u32[]{:S(2)}, u32[]{:S(2)}) %collective-permute-start.8) | collective-permute-done | bytes 1048608 | tf_op jit(solution)/shard_map/ppermute | solution.py:25
  35.5 2.8 %early_kernel.1 = (f32[64,1536]{1,0:T(8,128)S(1)}, f32[64,1536]{1,0:T(8,128)S(1)}, f32[64,1536]{1,0:T(8,128)S(1)}, f32[64,1536]{1,0:T(8,128)S(1)}) custom-call(s32[4]{0:T(128)S(1)} %pad_add_fusion.place, bf16[4,8,2,32,256]{4,3,2,1,0:T(8,128)(2,1)S(1)} %bitcast.16, bf16[4,8,2,32,256]{4,3,2,1,0:T(8,128)(2,1)S(1)} %bitcast.22, ...), custom_call_target="tpu_custom_call" | custom-call | flops 1 | bytes 1 | tf_op jit(solution)/shard_map/early_kernel/pallas_call | solution.py:135
  38.3 2.8 %collective-permute-start.10 = (f32[64,1536]{1,0:T(8,128)S(1)}, f32[64,1536]{1,0:T(8,128)S(1)}, u32[]{:S(2)}, u32[]{:S(2)}) collective-permute-start(f32[64,1536]{1,0:T(8,128)S(1)} %get-tuple-element.55), channel_id=1, source_target_pairs={{0,2},{1,3},{2,0},{3,1},{4,6},{5,7},{6,4},{7,5},{8,10},{9,11},{10,... | collective-permute-start | bytes 1179656 | tf_op jit(solution)/shard_map/ppermute | solution.py:21
  41.2 0.8 collective-permute-start.11
  42.0 0.6 collective-permute-start.9
  42.6 14.8 %collective-permute-done.13 = bf16[4,512,256]{2,1,0:T(8,128)(2,1)S(1)} collective-permute-done((bf16[4,512,256]{2,1,0:T(8,128)(2,1)S(1)}, bf16[4,512,256]{2,1,0:T(8,128)(2,1)S(1)}, u32[]{:S(2)}, u32[]{:S(2)}) %collective-permute-start.13) | collective-permute-done | bytes 1048608 | tf_op jit(solution)/shard_map/ppermute | solution.py:21
  57.4 1.4 %collective-permute-start.14 = (bf16[4,512,256]{2,1,0:T(8,128)(2,1)S(1)}, bf16[4,512,256]{2,1,0:T(8,128)(2,1)S(1)}, u32[]{:S(2)}, u32[]{:S(2)}) collective-permute-start(bf16[4,512,256]{2,1,0:T(8,128)(2,1)S(1)} %collective-permute-done.13), channel_id=1, source_target_pairs={{0,4},{4,0},{1,5},{5,1},{2,6},{6,2},{3,7},{7,3},{8,12},{12,8},{9,1... | collective-permute-start | bytes 3145736 | tf_op jit(solution)/shard_map/ppermute | solution.py:25
  58.8 0.0 collective-permute-done.11.refs_3_
  58.8 0.6 collective-permute-done.9.refs_1_
  59.4 0.1 total.3._.refs_4_
  59.5 1.5 %own_kernel.1.refs_0_ = f32[768,512]{1,0:T(8,128)S(1)} custom-call(s32[4]{0:T(128)S(1)} %pad_add_fusion.place, bf16[4,8,2,32,256]{4,3,2,1,0:T(8,128)(2,1)S(1)} %bitcast.19, bf16[4,8,2,32,256]{4,3,2,1,0:T(8,128)(2,1)S(1)} %bitcast.17, bf16[4,8,2,32,256]{4,3,2,1,0:T(8,128)(2,1)S(1)} %bitcast.21, bf16[4,8,2,32,256]{4,3,2,1,0:T(8,128)(2,1)S(1)} %bitcast.28, ...), custom_call_target="tpu_custom_call" | custom-call | flops 1 | bytes 1 | tf_op jit(solution)/shard_map/own_kernel/pallas_call | solution.py:135
  61.0 0.1 collective-permute-done.14
  61.1 1.9 %late_kernel.1 = (f32[128,512]{1,0:T(8,128)S(1)}, f32[128,512]{1,0:T(8,128)S(1)}, f32[128,512]{1,0:T(8,128)S(1)}, f32[128,512]{1,0:T(8,128)S(1)}, f32[64,512]{1,...) custom-call(s32[4]{0:T(128)S(1)} %pad_add_fusion.place, ...), custom_call_target="tpu_custom_call" | custom-call | flops 1 | bytes 1 | tf_op jit(solution)/shard_map/late_kernel/pallas_call | solution.py:135
  63.0 2.8 %collective-permute-start.18 = (f32[128,512]{1,0:T(8,128)S(1)}, f32[128,512]{1,0:T(8,128)S(1)}, u32[]{:S(2)}, u32[]{:S(2)}) collective-permute-start(f32[128,512]{1,0:T(8,128)S(1)} %get-tuple-element.63), channel_id=1, source_target_pairs={{0,2},{1,3},{2,0},{3,1},{4,6},{5,7},{6,4},{7,5},{8,10},{9,11},{10,... | collective-permute-start | bytes 786440 | tf_op jit(solution)/shard_map/ppermute | solution.py:21
  65.8 0.9 collective-permute-start.19
  66.7 0.6 collective-permute-start.20
  67.3 1.2 collective-permute-start.12
  68.5 0.6 collective-permute-start.15
  69.1 3.6 %collective-permute-done.12.refs_4_.refs_5_ = f32[64,512]{1,0:T(8,128)S(1)} collective-permute-done((f32[64,512]{1,0:T(8,128)S(1)}, f32[64,512]{1,0:T(8,128)S(1)}, u32[]{:S(2)}, u32[]{:S(2)}) %collective-permute-start.12) | collective-permute-done | bytes 131104 | tf_op jit(solution)/shard_map/ppermute | solution.py:21
  72.7 2.1 %collective-permute-start.16 = (f32[64,512]{1,0:T(8,128)S(1)}, f32[64,512]{1,0:T(8,128)S(1)}, u32[]{:S(2)}, u32[]{:S(2)}) collective-permute-start(f32[64,512]{1,0:T(8,128)S(1)} %get-tuple-element.60), channel_id=1, source_target_pairs={{0,3},{1,0},{2,1},{3,2},{4,7},{5,4},{6,5},{7,6},{8,11},{9,8},{10,9... | collective-permute-start | bytes 393224 | tf_op jit(solution)/shard_map/ppermute | solution.py:21
  74.8 3.0 %collective-permute-done.19.refs_2_ = f32[128,512]{1,0:T(8,128)S(1)} collective-permute-done((f32[128,512]{1,0:T(8,128)S(1)}, f32[128,512]{1,0:T(8,128)S(1)}, u32[]{:S(2)}, u32[]{:S(2)}) %collective-permute-start.19) | collective-permute-done | bytes 262176 | tf_op jit(solution)/shard_map/ppermute | solution.py:21
  77.8 1.5 %collective-permute-done.20.refs_3_ = f32[128,512]{1,0:T(8,128)S(1)} collective-permute-done((f32[128,512]{1,0:T(8,128)S(1)}, f32[128,512]{1,0:T(8,128)S(1)}, u32[]{:S(2)}, u32[]{:S(2)}) %collective-permute-start.20) | collective-permute-done | bytes 262176 | tf_op jit(solution)/shard_map/ppermute | solution.py:21
  79.3 1.2 collective-permute-start.21
  80.5 1.6 %collective-permute-start.22 = (f32[64,512]{1,0:T(8,128)S(1)}, f32[64,512]{1,0:T(8,128)S(1)}, u32[]{:S(2)}, u32[]{:S(2)}) collective-permute-start(f32[64,512]{1,0:T(8,128)S(1)} %get-tuple-element.75), channel_id=1, source_target_pairs={{0,192},{64,0},{128,64},{192,128},{1,193},{65,1},{129,65},{193,129... | collective-permute-start | bytes 393224 | tf_op jit(solution)/shard_map/ppermute | solution.py:21
  82.1 0.0 collective-permute-done.15.refs_1_
  82.1 1.3 %collective-permute-done.16.refs_2_ = f32[64,512]{1,0:T(8,128)S(1)} collective-permute-done((f32[64,512]{1,0:T(8,128)S(1)}, f32[64,512]{1,0:T(8,128)S(1)}, u32[]{:S(2)}, u32[]{:S(2)}) %collective-permute-start.16) | collective-permute-done | bytes 131104 | tf_op jit(solution)/shard_map/ppermute | solution.py:21
  83.4 1.0 collective-permute-done.21.refs_7_
  84.4 1.0 pack.1
  85.4 5.7 %collective-permute-start.24 = (f32[8,8960]{1,0:T(8,128)S(1)}, f32[8,8960]{1,0:T(8,128)S(1)}, u32[]{:S(2)}, u32[]{:S(2)}) collective-permute-start(f32[8,8960]{1,0:T(8,128)S(1)} %get-tuple-element.68), channel_id=1, source_target_pairs={{0,56},{8,0},{16,8},{24,16},{32,24},{40,32},{48,40},{56,48},{1,57}... | collective-permute-start | bytes 860168 | tf_op jit(solution)/shard_map/ppermute | solution.py:21
  91.1 3.6 %collective-permute-done.24 = f32[8,8960]{1,0:T(8,128)S(1)} collective-permute-done((f32[8,8960]{1,0:T(8,128)S(1)}, f32[8,8960]{1,0:T(8,128)S(1)}, u32[]{:S(2)}, u32[]{:S(2)}) %collective-permute-start.24) | collective-permute-done | bytes 286752 | tf_op jit(solution)/shard_map/ppermute | solution.py:21
  94.7 3.1 %collective-permute-done.23 = f32[8,8960]{1,0:T(8,128)S(1)} collective-permute-done((f32[8,8960]{1,0:T(8,128)S(1)}, f32[8,8960]{1,0:T(8,128)S(1)}, u32[]{:S(2)}, u32[]{:S(2)}) %collective-permute-start.23) | collective-permute-done | bytes 286752 | tf_op jit(solution)/shard_map/ppermute | solution.py:21
  97.8 0.1 collective-permute-start.25
  98.0 4.5 %collective-permute-start.26 = (f32[8,3584]{1,0:T(8,128)S(1)}, f32[8,3584]{1,0:T(8,128)S(1)}, u32[]{:S(2)}, u32[]{:S(2)}) collective-permute-start(f32[8,3584]{1,0:T(8,128)S(1)} %pad_maximum_fusion.1), channel_id=1, source_target_pairs={{0,40},{8,48},{16,56},{24,0},{32,8},{40,16},{48,24},{56,32},{1,41}... | collective-permute-start | bytes 344072 | tf_op jit(solution)/shard_map/ppermute | solution.py:21
  102.5 3.2 %collective-permute-done.25 = f32[8,3584]{1,0:T(8,128)S(1)} collective-permute-done((f32[8,3584]{1,0:T(8,128)S(1)}, f32[8,3584]{1,0:T(8,128)S(1)}, u32[]{:S(2)}, u32[]{:S(2)}) %collective-permute-start.25) | collective-permute-done | bytes 114720 | tf_op jit(solution)/shard_map/ppermute | solution.py:21
  105.8 0.6 spread_kernel.1
  106.4 21.3 %all_to_all.5.pieces = f32[32,8,128]{2,1,0:T(8,128)S(1)} all-to-all(f32[32,8,128]{2,1,0:T(8,128)S(1)} %spread_kernel.1), channel_id=1, replica_groups=mesh['row'=4,'z'=8,'core'=2,'aux'=4] {'row','core','aux'}, dimensions={0} | all-to-all | bytes 262144 | tf_op jit(solution)/shard_map/all_to_all | solution.py:333
  127.8 1.4 %finish_kernel.1 = f32[8,2048]{1,0:T(8,128)} custom-call(s32[4]{0:T(128)S(1)} %pad_add_fusion.place, f32[8,3584]{1,0:T(8,128)S(1)} %fusion.1.rows, f32[32,8,128]{2,1,0:T(8,128)S(1)} %all_to_all.5.pieces), custom_call_target="tpu_custom_call" | custom-call | flops 1 | bytes 1 | tf_op jit(solution)/shard_map/finish_kernel/pallas_call | solution.py:176
  (24 shorter events, 0.3 us)
Async XLA Ops:
  0.0 7.4 %copy-start.1 = (s32[64,16]{0,1:T(8,128)S(1)}, s32[64,16]{0,1:T(8,128)}, u32[]{:S(2)}) copy-start(s32[64,16]{0,1:T(8,128)} %param.3) | copy-start | bytes 12292
  3.8 25.8 %collective-permute-start = (bf16[4,512,256]{2,1,0:T(8,128)(2,1)}, bf16[4,512,256]{2,1,0:T(8,128)(2,1)S(1)}, u32[]{:S(2)}, u32[]{:S(2)}) collective-permute-start(bf16[4,512,256]{2,1,0:T(8,128)(2,1)} %get-tuple-element.38), channel_id=1, source_target_pairs={{0,64},{64,128},{128,192},{192,0},{1,65},{65,129},{129,193},{193,1... | collective-permute-start | bytes 3145736 | tf_op jit(solution)/shard_map/ppermute | solution.py:21
  5.9 23.7 %collective-permute-start.1 = (bf16[4,512,256]{2,1,0:T(8,128)(2,1)S(1)}, bf16[4,512,256]{2,1,0:T(8,128)(2,1)S(1)}, u32[]{:S(2)}, u32[]{:S(2)}) collective-permute-start(bf16[4,512,256]{2,1,0:T(8,128)(2,1)S(1)} %get-tuple-element.39), channel_id=1, source_target_pairs={{0,192},{64,0},{128,64},{192,128},{1,193},{65,1},{129,65},{193,129... | collective-permute-start | bytes 3145736 | tf_op jit(solution)/shard_map/ppermute | solution.py:21
  7.5 2.2 %copy-start = (bf16[16,512,256]{2,1,0:T(8,128)(2,1)S(1)}, bf16[16,512,256]{2,1,0:T(8,128)(2,1)}, u32[]{:S(2)}) copy-start(bf16[16,512,256]{2,1,0:T(8,128)(2,1)} %slab) | copy-start | bytes 12582916
  14.4 4.5 %collective-permute-start.2 = (f32[256,512]{1,0:T(8,128)S(1)}, f32[256,512]{1,0:T(8,128)S(1)}, u32[]{:S(2)}, u32[]{:S(2)}) collective-permute-start(f32[256,512]{1,0:T(8,128)S(1)} %get-tuple-element.42), channel_id=1, source_target_pairs={{0,4},{4,0},{1,5},{5,1},{2,6},{6,2},{3,7},{7,3},{8,12},{12,8},{9,1... | collective-permute-start | bytes 1572872 | tf_op jit(solution)/shard_map/ppermute | solution.py:25
  19.6 6.7 %collective-permute-start.3 = (f32[64,512]{1,0:T(8,128)S(1)}, f32[64,512]{1,0:T(8,128)S(1)}, u32[]{:S(2)}, u32[]{:S(2)}) collective-permute-start(f32[64,512]{1,0:T(8,128)S(1)} %get-tuple-element.44), channel_id=1, source_target_pairs={{0,1},{1,2},{2,3},{3,0},{4,5},{5,6},{6,7},{7,4},{8,9},{9,10},{10,1... | collective-permute-start | bytes 393224 | tf_op jit(solution)/shard_map/ppermute | solution.py:21
  19.7 9.9 %collective-permute-start.4 = (f32[64,512]{1,0:T(8,128)S(1)}, f32[64,512]{1,0:T(8,128)S(1)}, u32[]{:S(2)}, u32[]{:S(2)}) collective-permute-start(f32[64,512]{1,0:T(8,128)S(1)} %get-tuple-element.45), channel_id=1, source_target_pairs={{0,2},{1,3},{2,0},{3,1},{4,6},{5,7},{6,4},{7,5},{8,10},{9,11},{10,... | collective-permute-start | bytes 393224 | tf_op jit(solution)/shard_map/ppermute | solution.py:21
  21.6 8.0 %collective-permute-start.5 = (f32[64,512]{1,0:T(8,128)S(1)}, f32[64,512]{1,0:T(8,128)S(1)}, u32[]{:S(2)}, u32[]{:S(2)}) collective-permute-start(f32[64,512]{1,0:T(8,128)S(1)} %get-tuple-element.46), channel_id=1, source_target_pairs={{0,3},{1,0},{2,1},{3,2},{4,7},{5,4},{6,5},{7,6},{8,11},{9,8},{10,9... | collective-permute-start | bytes 393224 | tf_op jit(solution)/shard_map/ppermute | solution.py:21
  26.3 7.8 %collective-permute-start.6 = (bf16[4,512,256]{2,1,0:T(8,128)(2,1)S(1)}, bf16[4,512,256]{2,1,0:T(8,128)(2,1)S(1)}, u32[]{:S(2)}, u32[]{:S(2)}) collective-permute-start(bf16[4,512,256]{2,1,0:T(8,128)(2,1)S(1)} %get-tuple-element.71), channel_id=1, source_target_pairs={{0,4},{4,0},{1,5},{5,1},{2,6},{6,2},{3,7},{7,3},{8,12},{12,8},{9,1... | collective-permute-start | bytes 3145736 | tf_op jit(solution)/shard_map/ppermute | solution.py:25
  29.6 4.5 %collective-permute-start.7 = (bf16[4,512,256]{2,1,0:T(8,128)(2,1)S(1)}, bf16[4,512,256]{2,1,0:T(8,128)(2,1)S(1)}, u32[]{:S(2)}, u32[]{:S(2)}) collective-permute-start(bf16[4,512,256]{2,1,0:T(8,128)(2,1)S(1)} %collective-permute-done.1), channel_id=1, source_target_pairs={{0,4},{4,0},{1,5},{5,1},{2,6},{6,2},{3,7},{7,3},{8,12},{12,8},{9,1... | collective-permute-start | bytes 3145736 | tf_op jit(solution)/shard_map/ppermute | solution.py:25
  31.7 3.8 %collective-permute-start.8 = (bf16[4,512,256]{2,1,0:T(8,128)(2,1)S(1)}, bf16[4,512,256]{2,1,0:T(8,128)(2,1)S(1)}, u32[]{:S(2)}, u32[]{:S(2)}) collective-permute-start(bf16[4,512,256]{2,1,0:T(8,128)(2,1)S(1)} %collective-permute-done), channel_id=1, source_target_pairs={{0,4},{4,0},{1,5},{5,1},{2,6},{6,2},{3,7},{7,3},{8,12},{12,8},{9,1... | collective-permute-start | bytes 3145736 | tf_op jit(solution)/shard_map/ppermute | solution.py:25
  31.7 25.7 %collective-permute-start.13 = (bf16[4,512,256]{2,1,0:T(8,128)(2,1)S(1)}, bf16[4,512,256]{2,1,0:T(8,128)(2,1)S(1)}, u32[]{:S(2)}, u32[]{:S(2)}) collective-permute-start(bf16[4,512,256]{2,1,0:T(8,128)(2,1)S(1)} %get-tuple-element.57), channel_id=1, source_target_pairs={{0,128},{64,192},{128,0},{192,64},{1,129},{65,193},{129,1},{193,65... | collective-permute-start | bytes 3145736 | tf_op jit(solution)/shard_map/ppermute | solution.py:21
  38.3 20.5 %collective-permute-start.10 = (f32[64,1536]{1,0:T(8,128)S(1)}, f32[64,1536]{1,0:T(8,128)S(1)}, u32[]{:S(2)}, u32[]{:S(2)}) collective-permute-start(f32[64,1536]{1,0:T(8,128)S(1)} %get-tuple-element.55), channel_id=1, source_target_pairs={{0,2},{1,3},{2,0},{3,1},{4,6},{5,7},{6,4},{7,5},{8,10},{9,11},{10,... | collective-permute-start | bytes 1179656 | tf_op jit(solution)/shard_map/ppermute | solution.py:21
  41.2 17.7 %collective-permute-start.11 = (f32[64,1536]{1,0:T(8,128)S(1)}, f32[64,1536]{1,0:T(8,128)S(1)}, u32[]{:S(2)}, u32[]{:S(2)}) collective-permute-start(f32[64,1536]{1,0:T(8,128)S(1)} %get-tuple-element.56), channel_id=1, source_target_pairs={{0,3},{1,0},{2,1},{3,2},{4,7},{5,4},{6,5},{7,6},{8,11},{9,8},{10,9... | collective-permute-start | bytes 1179656 | tf_op jit(solution)/shard_map/ppermute | solution.py:21
  42.0 17.4 %collective-permute-start.9 = (f32[64,1536]{1,0:T(8,128)S(1)}, f32[64,1536]{1,0:T(8,128)S(1)}, u32[]{:S(2)}, u32[]{:S(2)}) collective-permute-start(f32[64,1536]{1,0:T(8,128)S(1)} %get-tuple-element.54), channel_id=1, source_target_pairs={{0,1},{1,2},{2,3},{3,0},{4,5},{5,6},{6,7},{7,4},{8,9},{9,10},{10,1... | collective-permute-start | bytes 1179656 | tf_op jit(solution)/shard_map/ppermute | solution.py:21
  57.4 3.6 %collective-permute-start.14 = (bf16[4,512,256]{2,1,0:T(8,128)(2,1)S(1)}, bf16[4,512,256]{2,1,0:T(8,128)(2,1)S(1)}, u32[]{:S(2)}, u32[]{:S(2)}) collective-permute-start(bf16[4,512,256]{2,1,0:T(8,128)(2,1)S(1)} %collective-permute-done.13), channel_id=1, source_target_pairs={{0,4},{4,0},{1,5},{5,1},{2,6},{6,2},{3,7},{7,3},{8,12},{12,8},{9,1... | collective-permute-start | bytes 3145736 | tf_op jit(solution)/shard_map/ppermute | solution.py:25
  63.0 11.8 %collective-permute-start.18 = (f32[128,512]{1,0:T(8,128)S(1)}, f32[128,512]{1,0:T(8,128)S(1)}, u32[]{:S(2)}, u32[]{:S(2)}) collective-permute-start(f32[128,512]{1,0:T(8,128)S(1)} %get-tuple-element.63), channel_id=1, source_target_pairs={{0,2},{1,3},{2,0},{3,1},{4,6},{5,7},{6,4},{7,5},{8,10},{9,11},{10,... | collective-permute-start | bytes 786440 | tf_op jit(solution)/shard_map/ppermute | solution.py:21
  65.8 12.0 %collective-permute-start.19 = (f32[128,512]{1,0:T(8,128)S(1)}, f32[128,512]{1,0:T(8,128)S(1)}, u32[]{:S(2)}, u32[]{:S(2)}) collective-permute-start(f32[128,512]{1,0:T(8,128)S(1)} %get-tuple-element.64), channel_id=1, source_target_pairs={{0,3},{1,0},{2,1},{3,2},{4,7},{5,4},{6,5},{7,6},{8,11},{9,8},{10,9... | collective-permute-start | bytes 786440 | tf_op jit(solution)/shard_map/ppermute | solution.py:21
  66.7 12.6 %collective-permute-start.20 = (f32[128,512]{1,0:T(8,128)S(1)}, f32[128,512]{1,0:T(8,128)S(1)}, u32[]{:S(2)}, u32[]{:S(2)}) collective-permute-start(f32[128,512]{1,0:T(8,128)S(1)} %get-tuple-element.65), channel_id=1, source_target_pairs={{0,1},{1,2},{2,3},{3,0},{4,5},{5,6},{6,7},{7,4},{8,9},{9,10},{10,1... | collective-permute-start | bytes 786440 | tf_op jit(solution)/shard_map/ppermute | solution.py:21
  67.3 5.4 %collective-permute-start.12 = (f32[64,512]{1,0:T(8,128)S(1)}, f32[64,512]{1,0:T(8,128)S(1)}, u32[]{:S(2)}, u32[]{:S(2)}) collective-permute-start(f32[64,512]{1,0:T(8,128)S(1)} %slice.52), channel_id=1, source_target_pairs={{0,64},{64,128},{128,192},{192,0},{1,65},{65,129},{129,193},{193,1... | collective-permute-start | bytes 393224 | tf_op jit(solution)/shard_map/ppermute | solution.py:21
  68.5 13.6 %collective-permute-start.15 = (f32[64,512]{1,0:T(8,128)S(1)}, f32[64,512]{1,0:T(8,128)S(1)}, u32[]{:S(2)}, u32[]{:S(2)}) collective-permute-start(f32[64,512]{1,0:T(8,128)S(1)} %get-tuple-element.59), channel_id=1, source_target_pairs={{0,2},{1,3},{2,0},{3,1},{4,6},{5,7},{6,4},{7,5},{8,10},{9,11},{10,... | collective-permute-start | bytes 393224 | tf_op jit(solution)/shard_map/ppermute | solution.py:21
  72.7 10.7 %collective-permute-start.16 = (f32[64,512]{1,0:T(8,128)S(1)}, f32[64,512]{1,0:T(8,128)S(1)}, u32[]{:S(2)}, u32[]{:S(2)}) collective-permute-start(f32[64,512]{1,0:T(8,128)S(1)} %get-tuple-element.60), channel_id=1, source_target_pairs={{0,3},{1,0},{2,1},{3,2},{4,7},{5,4},{6,5},{7,6},{8,11},{9,8},{10,9... | collective-permute-start | bytes 393224 | tf_op jit(solution)/shard_map/ppermute | solution.py:21
  74.8 8.6 %collective-permute-start.17 = (f32[64,512]{1,0:T(8,128)S(1)}, f32[64,512]{1,0:T(8,128)S(1)}, u32[]{:S(2)}, u32[]{:S(2)}) collective-permute-start(f32[64,512]{1,0:T(8,128)S(1)} %get-tuple-element.61), channel_id=1, source_target_pairs={{0,1},{1,2},{2,3},{3,0},{4,5},{5,6},{6,7},{7,4},{8,9},{9,10},{10,1... | collective-permute-start | bytes 393224 | tf_op jit(solution)/shard_map/ppermute | solution.py:21
  79.3 5.1 %collective-permute-start.21 = (f32[64,512]{1,0:T(8,128)S(1)}, f32[64,512]{1,0:T(8,128)S(1)}, u32[]{:S(2)}, u32[]{:S(2)}) collective-permute-start(f32[64,512]{1,0:T(8,128)S(1)} %get-tuple-element.76), channel_id=1, source_target_pairs={{0,64},{64,128},{128,192},{192,0},{1,65},{65,129},{129,193},{193,1... | collective-permute-start | bytes 393224 | tf_op jit(solution)/shard_map/ppermute | solution.py:21
  80.5 3.9 %collective-permute-start.22 = (f32[64,512]{1,0:T(8,128)S(1)}, f32[64,512]{1,0:T(8,128)S(1)}, u32[]{:S(2)}, u32[]{:S(2)}) collective-permute-start(f32[64,512]{1,0:T(8,128)S(1)} %get-tuple-element.75), channel_id=1, source_target_pairs={{0,192},{64,0},{128,64},{192,128},{1,193},{65,1},{129,65},{193,129... | collective-permute-start | bytes 393224 | tf_op jit(solution)/shard_map/ppermute | solution.py:21
  85.4 9.3 %collective-permute-start.24 = (f32[8,8960]{1,0:T(8,128)S(1)}, f32[8,8960]{1,0:T(8,128)S(1)}, u32[]{:S(2)}, u32[]{:S(2)}) collective-permute-start(f32[8,8960]{1,0:T(8,128)S(1)} %get-tuple-element.68), channel_id=1, source_target_pairs={{0,56},{8,0},{16,8},{24,16},{32,24},{40,32},{48,40},{56,48},{1,57}... | collective-permute-start | bytes 860168 | tf_op jit(solution)/shard_map/ppermute | solution.py:21
  91.1 6.7 %collective-permute-start.23 = (f32[8,8960]{1,0:T(8,128)S(1)}, f32[8,8960]{1,0:T(8,128)S(1)}, u32[]{:S(2)}, u32[]{:S(2)}) collective-permute-start(f32[8,8960]{1,0:T(8,128)S(1)} %get-tuple-element.67), channel_id=1, source_target_pairs={{0,8},{8,16},{16,24},{24,32},{32,40},{40,48},{48,56},{56,0},{1,9},... | collective-permute-start | bytes 860168 | tf_op jit(solution)/shard_map/ppermute | solution.py:21
  97.8 7.9 %collective-permute-start.25 = (f32[8,3584]{1,0:T(8,128)S(1)}, f32[8,3584]{1,0:T(8,128)S(1)}, u32[]{:S(2)}, u32[]{:S(2)}) collective-permute-start(f32[8,3584]{1,0:T(8,128)S(1)} %pad_maximum_fusion), channel_id=1, source_target_pairs={{0,24},{8,32},{16,40},{24,48},{32,56},{40,0},{48,8},{56,16},{1,25}... | collective-permute-start | bytes 344072 | tf_op jit(solution)/shard_map/ppermute | solution.py:21
  98.0 7.8 %collective-permute-start.26 = (f32[8,3584]{1,0:T(8,128)S(1)}, f32[8,3584]{1,0:T(8,128)S(1)}, u32[]{:S(2)}, u32[]{:S(2)}) collective-permute-start(f32[8,3584]{1,0:T(8,128)S(1)} %pad_maximum_fusion.1), channel_id=1, source_target_pairs={{0,40},{8,48},{16,56},{24,0},{32,8},{40,16},{48,24},{56,32},{1,41}... | collective-permute-start | bytes 344072 | tf_op jit(solution)/shard_map/ppermute | solution.py:21

commit v7 on v5

--- a/solution.py
+++ b/solution.py
@@ -320,8 +320,8 @@
     (own,) = pairs(own_kernel, place, (below[0], mine, above[0], across_own), [(3 * n // 2, n)], (early,))
     shapes = [(2 * zs * 8, n)] * xs + [(zs * 8, n)] * xs
     late_parts = pairs(late_kernel, place, (below[1], mine2, above[1], across_sibling, own), shapes)
-    outer = total(over_aux(late_parts[:xs], xs), (third,))
-    middle = total(over_aux(late_parts[xs:], xs))
+    outer = total(over_aux(late_parts[:xs], xs))
+    middle = total(over_aux(late_parts[xs:], xs), (third,))
     up, down = shift(outer[zs * 8 :], "row", 1, ys), shift(outer[: zs * 8], "row", -1, ys)
     rows = first_z(pack(place, *diag, early, third, middle, up, down))
     here, forward, backward = second_z(*rows)

time: 129 us -> 130 us (level)
  starting transfers between devices: 42.5 us -> 46.3 us
  waiting for transfers between devices: 43.8 us -> 40.8 us
    ppermute x22, starting transfers between devices: 33.9 us -> 37.7 us  [shift(): lax.ppermute(value, axis, [(i, (i + step) % size) for i in range(size)])]
    ppermute x22, waiting for transfers between devices: 40.9 us -> 37.9 us  [shift(): lax.ppermute(value, axis, [(i, (i + step) % size) for i in range(size)])]
where the time goes in v7:
time: 130 us
  starting transfers between devices  46.3 us (36%)
  waiting for transfers between devices  40.8 us (31%)
  blocking collectives  21.1 us (16%)
  Pallas kernels  14.8 us (11%)
  other arithmetic  4.43 us (3%)
  local copies, waits for them, and re-layouts  2.52 us (2%)
    ppermute x22, waiting for transfers between devices, shift(): lax.ppermute(value, axis, [(i, (i + step) % size) for i in range(size)])  37.9 us
    ppermute x22, starting transfers between devices, shift(): lax.ppermute(value, axis, [(i, (i + step) % size) for i in range(size)])  37.7 us
    all_to_all x1, blocking collectives, body(): pieces = lax.all_to_all(pieces, ('row', 'core', 'aux'), 0, 0, tiled=True)  21.1 us
    ppermute x5, starting transfers between devices, sibling(): return lax.ppermute(value, 'core', [(0, 1), (1, 0)])  8.59 us
    pallas_call x4, Pallas kernels, pairs(): pl.pallas_call(kernel, in_specs=[SCALARS] + [ANYWHERE] * len(operands) +...  6.95 us
    pallas_call x1, Pallas kernels, diagonal(): pl.pallas_call(diagonal_kernel, grid=(depth // group,), in_specs=[SCALARS...  4.62 us
    mul x2, other arithmetic, slab(): part * lax.dynamic_slice(keep, (first, 0), (quarter, mrows))[:, :, None]  3.41 us
    ppermute x5, waiting for transfers between devices, sibling(): return lax.ppermute(value, 'core', [(0, 1), (1, 0)])  2.89 us
  transfers between devices with their start and end apart: 27, of which 15 were waited for; matrix products, arithmetic and copies ran while one was open for 1% of the time, Pallas kernels for 8%

profile of v7, /device:TPU:1, one launch (start us, length us, event | category | flops | bytes accessed | tf_op | source)
XLA Modules:
  0.0 130.2 jit_solution(11245818584933732013)
XLA Ops:
  0.0 0.8 dynamic-slice_convert_fusion
  0.8 0.1 copy.3
  0.9 0.1 broadcast_in_dim.2
  1.1 2.7 %dynamic-slice_multiply_fusion.2 = (bf16[4,512,256]{2,1,0:T(8,128)(2,1)S(1)}, bf16[4,512,256]{2,1,0:T(8,128)(2,1)}) fusion(bf16[16,512,256]{2,1,0:T(8,128)(2,1)} %slab, s32[]{:T(128)S(6)} %select_n.25, bf16[4,512]{1,0:T(4,128)(2,1)S(1)} %get-tuple-element.83, bf16[4,512]{1,0:T(4,128)(2,1)S(1)} %get-tuple-element.84, s32[]{:T(128)S(6)} %select_n.22), kind=kLoop, calls=%fused_computation.2 | loop fusion | flops 1048576 | bytes 4202504 | tf_op jit(solution)/shard_map/mul | solution.py:296
  3.8 2.1 %collective-permute-start = (bf16[4,512,256]{2,1,0:T(8,128)(2,1)}, bf16[4,512,256]{2,1,0:T(8,128)(2,1)S(1)}, u32[]{:S(2)}, u32[]{:S(2)}) collective-permute-start(bf16[4,512,256]{2,1,0:T(8,128)(2,1)} %get-tuple-element.38), channel_id=1, source_target_pairs={{0,64},{64,128},{128,192},{192,0},{1,65},{65,129},{129,193},{193,1... | collective-permute-start | bytes 3145736 | tf_op jit(solution)/shard_map/ppermute | solution.py:21
  5.9 1.4 %collective-permute-start.1 = (bf16[4,512,256]{2,1,0:T(8,128)(2,1)S(1)}, bf16[4,512,256]{2,1,0:T(8,128)(2,1)S(1)}, u32[]{:S(2)}, u32[]{:S(2)}) collective-permute-start(bf16[4,512,256]{2,1,0:T(8,128)(2,1)S(1)} %get-tuple-element.39), channel_id=1, source_target_pairs={{0,192},{64,0},{128,64},{192,128},{1,193},{65,1},{129,65},{193,129... | collective-permute-start | bytes 3145736 | tf_op jit(solution)/shard_map/ppermute | solution.py:21
  7.4 0.1 copy.4.screen
  7.5 0.1 pad_add_fusion.place
  7.5 2.2 %copy-done = bf16[16,512,256]{2,1,0:T(8,128)(2,1)S(1)} copy-done((bf16[16,512,256]{2,1,0:T(8,128)(2,1)S(1)}, bf16[16,512,256]{2,1,0:T(8,128)(2,1)}, u32[]{:S(2)}) %copy-start) | copy-done | bytes 4194328
  9.7 4.6 %diagonal.1 = (f32[256,512]{1,0:T(8,128)S(1)}, f32[256,512]{1,0:T(8,128)S(1)}) custom-call(s32[4]{0:T(128)S(1)} %pad_add_fusion.place, s32[64,16]{1,0:T(8,128)S(1)} %copy.4.screen, bf16[16,512,256]{2,1,0:T(8,128)(2,1)S(1)} %copy-done), custom_call_target="tpu_custom_call" | custom-call | flops 1 | bytes 1 | tf_op jit(solution)/shard_map/diagonal/pallas_call | solution.py:68
  14.4 3.0 %collective-permute-start.2 = (f32[256,512]{1,0:T(8,128)S(1)}, f32[256,512]{1,0:T(8,128)S(1)}, u32[]{:S(2)}, u32[]{:S(2)}) collective-permute-start(f32[256,512]{1,0:T(8,128)S(1)} %get-tuple-element.42), channel_id=1, source_target_pairs={{0,4},{4,0},{1,5},{5,1},{2,6},{6,2},{3,7},{7,3},{8,12},{12,8},{9,1... | collective-permute-start | bytes 1572872 | tf_op jit(solution)/shard_map/ppermute | solution.py:25
  17.4 1.5 %collective-permute-done.2.got = f32[256,512]{1,0:T(8,128)S(1)} collective-permute-done((f32[256,512]{1,0:T(8,128)S(1)}, f32[256,512]{1,0:T(8,128)S(1)}, u32[]{:S(2)}, u32[]{:S(2)}) %collective-permute-start.2) | collective-permute-done | bytes 524320 | tf_op jit(solution)/shard_map/ppermute | solution.py:25
  18.9 0.7 split_kernel.1
  19.6 1.1 collective-permute-start.3
  20.7 0.9 collective-permute-start.4
  21.5 0.6 collective-permute-start.5
  22.2 0.7 dynamic-slice_multiply_fusion
  22.9 3.0 %collective-permute-done.3.refs_1_ = f32[64,512]{1,0:T(8,128)S(1)} collective-permute-done((f32[64,512]{1,0:T(8,128)S(1)}, f32[64,512]{1,0:T(8,128)S(1)}, u32[]{:S(2)}, u32[]{:S(2)}) %collective-permute-start.3) | collective-permute-done | bytes 131104 | tf_op jit(solution)/shard_map/ppermute | solution.py:21
  25.9 2.0 %collective-permute-start.6 = (bf16[4,512,256]{2,1,0:T(8,128)(2,1)S(1)}, bf16[4,512,256]{2,1,0:T(8,128)(2,1)S(1)}, u32[]{:S(2)}, u32[]{:S(2)}) collective-permute-start(bf16[4,512,256]{2,1,0:T(8,128)(2,1)S(1)} %get-tuple-element.71), channel_id=1, source_target_pairs={{0,4},{4,0},{1,5},{5,1},{2,6},{6,2},{3,7},{7,3},{8,12},{12,8},{9,1... | collective-permute-start | bytes 3145736 | tf_op jit(solution)/shard_map/ppermute | solution.py:25
  27.9 0.0 collective-permute-done.4.refs_2_
  27.9 1.1 collective-permute-done.5.refs_3_
  29.0 0.0 collective-permute-done
  29.0 0.5 collective-permute-done.1
  29.5 2.2 %collective-permute-start.7 = (bf16[4,512,256]{2,1,0:T(8,128)(2,1)S(1)}, bf16[4,512,256]{2,1,0:T(8,128)(2,1)S(1)}, u32[]{:S(2)}, u32[]{:S(2)}) collective-permute-start(bf16[4,512,256]{2,1,0:T(8,128)(2,1)S(1)} %collective-permute-done.1), channel_id=1, source_target_pairs={{0,4},{4,0},{1,5},{5,1},{2,6},{6,2},{3,7},{7,3},{8,12},{12,8},{9,1... | collective-permute-start | bytes 3145736 | tf_op jit(solution)/shard_map/ppermute | solution.py:25
  31.7 0.0 collective-permute-start.8
  31.7 2.4 %collective-permute-start.13 = (bf16[4,512,256]{2,1,0:T(8,128)(2,1)S(1)}, bf16[4,512,256]{2,1,0:T(8,128)(2,1)S(1)}, u32[]{:S(2)}, u32[]{:S(2)}) collective-permute-start(bf16[4,512,256]{2,1,0:T(8,128)(2,1)S(1)} %get-tuple-element.57), channel_id=1, source_target_pairs={{0,128},{64,192},{128,0},{192,64},{1,129},{65,193},{129,1},{193,65... | collective-permute-start | bytes 3145736 | tf_op jit(solution)/shard_map/ppermute | solution.py:21
  34.1 0.0 collective-permute-done.6
  34.1 1.3 %collective-permute-done.8 = bf16[4,512,256]{2,1,0:T(8,128)(2,1)S(1)} collective-permute-done((bf16[4,512,256]{2,1,0:T(8,128)(2,1)S(1)}, bf16[4,512,256]{2,1,0:T(8,128)(2,1)S(1)}, u32[]{:S(2)}, u32[]{:S(2)}) %collective-permute-start.8) | collective-permute-done | bytes 1048608 | tf_op jit(solution)/shard_map/ppermute | solution.py:25
  35.5 2.8 %early_kernel.1 = (f32[64,1536]{1,0:T(8,128)S(1)}, f32[64,1536]{1,0:T(8,128)S(1)}, f32[64,1536]{1,0:T(8,128)S(1)}, f32[64,1536]{1,0:T(8,128)S(1)}) custom-call(s32[4]{0:T(128)S(1)} %pad_add_fusion.place, bf16[4,8,2,32,256]{4,3,2,1,0:T(8,128)(2,1)S(1)} %bitcast.16, bf16[4,8,2,32,256]{4,3,2,1,0:T(8,128)(2,1)S(1)} %bitcast.22, ...), custom_call_target="tpu_custom_call" | custom-call | flops 1 | bytes 1 | tf_op jit(solution)/shard_map/early_kernel/pallas_call | solution.py:135
  38.3 2.6 %collective-permute-start.10 = (f32[64,1536]{1,0:T(8,128)S(1)}, f32[64,1536]{1,0:T(8,128)S(1)}, u32[]{:S(2)}, u32[]{:S(2)}) collective-permute-start(f32[64,1536]{1,0:T(8,128)S(1)} %get-tuple-element.55), channel_id=1, source_target_pairs={{0,3},{1,0},{2,1},{3,2},{4,7},{5,4},{6,5},{7,6},{8,11},{9,8},{10,9... | collective-permute-start | bytes 1179656 | tf_op jit(solution)/shard_map/ppermute | solution.py:21
  40.9 0.0 collective-permute-start.11
  40.9 1.7 %collective-permute-start.9 = (f32[64,1536]{1,0:T(8,128)S(1)}, f32[64,1536]{1,0:T(8,128)S(1)}, u32[]{:S(2)}, u32[]{:S(2)}) collective-permute-start(f32[64,1536]{1,0:T(8,128)S(1)} %get-tuple-element.54), channel_id=1, source_target_pairs={{0,2},{1,3},{2,0},{3,1},{4,6},{5,7},{6,4},{7,5},{8,10},{9,11},{10,... | collective-permute-start | bytes 1179656 | tf_op jit(solution)/shard_map/ppermute | solution.py:21
  42.6 14.8 %collective-permute-done.13 = bf16[4,512,256]{2,1,0:T(8,128)(2,1)S(1)} collective-permute-done((bf16[4,512,256]{2,1,0:T(8,128)(2,1)S(1)}, bf16[4,512,256]{2,1,0:T(8,128)(2,1)S(1)}, u32[]{:S(2)}, u32[]{:S(2)}) %collective-permute-start.13) | collective-permute-done | bytes 1048608 | tf_op jit(solution)/shard_map/ppermute | solution.py:21
  57.4 1.4 %collective-permute-start.14 = (bf16[4,512,256]{2,1,0:T(8,128)(2,1)S(1)}, bf16[4,512,256]{2,1,0:T(8,128)(2,1)S(1)}, u32[]{:S(2)}, u32[]{:S(2)}) collective-permute-start(bf16[4,512,256]{2,1,0:T(8,128)(2,1)S(1)} %collective-permute-done.13), channel_id=1, source_target_pairs={{0,4},{4,0},{1,5},{5,1},{2,6},{6,2},{3,7},{7,3},{8,12},{12,8},{9,1... | collective-permute-start | bytes 3145736 | tf_op jit(solution)/shard_map/ppermute | solution.py:25
  58.8 0.8 collective-permute-done.9.refs_1_
  59.6 0.1 total.3._.refs_4_
  59.7 1.5 %own_kernel.1.refs_0_ = f32[768,512]{1,0:T(8,128)S(1)} custom-call(s32[4]{0:T(128)S(1)} %pad_add_fusion.place, bf16[4,8,2,32,256]{4,3,2,1,0:T(8,128)(2,1)S(1)} %bitcast.19, bf16[4,8,2,32,256]{4,3,2,1,0:T(8,128)(2,1)S(1)} %bitcast.17, bf16[4,8,2,32,256]{4,3,2,1,0:T(8,128)(2,1)S(1)} %bitcast.21, bf16[4,8,2,32,256]{4,3,2,1,0:T(8,128)(2,1)S(1)} %bitcast.28, ...), custom_call_target="tpu_custom_call" | custom-call | flops 1 | bytes 1 | tf_op jit(solution)/shard_map/own_kernel/pallas_call | solution.py:135
  61.3 0.0 collective-permute-done.14
  61.3 1.9 %late_kernel.1 = (f32[128,512]{1,0:T(8,128)S(1)}, f32[128,512]{1,0:T(8,128)S(1)}, f32[128,512]{1,0:T(8,128)S(1)}, f32[128,512]{1,0:T(8,128)S(1)}, f32[64,512]{1,...) custom-call(s32[4]{0:T(128)S(1)} %pad_add_fusion.place, ...), custom_call_target="tpu_custom_call" | custom-call | flops 1 | bytes 1 | tf_op jit(solution)/shard_map/late_kernel/pallas_call | solution.py:135
  63.2 2.6 %collective-permute-start.18 = (f32[128,512]{1,0:T(8,128)S(1)}, f32[128,512]{1,0:T(8,128)S(1)}, u32[]{:S(2)}, u32[]{:S(2)}) collective-permute-start(f32[128,512]{1,0:T(8,128)S(1)} %get-tuple-element.63), channel_id=1, source_target_pairs={{0,2},{1,3},{2,0},{3,1},{4,6},{5,7},{6,4},{7,5},{8,10},{9,11},{10,... | collective-permute-start | bytes 786440 | tf_op jit(solution)/shard_map/ppermute | solution.py:21
  65.8 0.9 collective-permute-start.19
  66.7 0.6 collective-permute-start.20
  67.3 1.2 collective-permute-start.12
  68.5 0.6 collective-permute-start.15
  69.1 2.1 %collective-permute-done.18.refs_1_ = f32[128,512]{1,0:T(8,128)S(1)} collective-permute-done((f32[128,512]{1,0:T(8,128)S(1)}, f32[128,512]{1,0:T(8,128)S(1)}, u32[]{:S(2)}, u32[]{:S(2)}) %collective-permute-start.18) | collective-permute-done | bytes 262176 | tf_op jit(solution)/shard_map/ppermute | solution.py:21
  71.2 3.4 %collective-permute-start.16 = (f32[64,512]{1,0:T(8,128)S(1)}, f32[64,512]{1,0:T(8,128)S(1)}, u32[]{:S(2)}, u32[]{:S(2)}) collective-permute-start(f32[64,512]{1,0:T(8,128)S(1)} %get-tuple-element.60), channel_id=1, source_target_pairs={{0,3},{1,0},{2,1},{3,2},{4,7},{5,4},{6,5},{7,6},{8,11},{9,8},{10,9... | collective-permute-start | bytes 393224 | tf_op jit(solution)/shard_map/ppermute | solution.py:21
  74.6 3.2 %collective-permute-done.19.refs_2_ = f32[128,512]{1,0:T(8,128)S(1)} collective-permute-done((f32[128,512]{1,0:T(8,128)S(1)}, f32[128,512]{1,0:T(8,128)S(1)}, u32[]{:S(2)}, u32[]{:S(2)}) %collective-permute-start.19) | collective-permute-done | bytes 262176 | tf_op jit(solution)/shard_map/ppermute | solution.py:21
  77.8 2.5 %collective-permute-start.17 = (f32[64,512]{1,0:T(8,128)S(1)}, f32[64,512]{1,0:T(8,128)S(1)}, u32[]{:S(2)}, u32[]{:S(2)}) collective-permute-start(f32[64,512]{1,0:T(8,128)S(1)} %get-tuple-element.61), channel_id=1, source_target_pairs={{0,1},{1,2},{2,3},{3,0},{4,5},{5,6},{6,7},{7,4},{8,9},{9,10},{10,1... | collective-permute-start | bytes 393224 | tf_op jit(solution)/shard_map/ppermute | solution.py:21
  80.4 1.2 collective-permute-start.21
  81.6 1.6 %collective-permute-start.22 = (f32[64,512]{1,0:T(8,128)S(1)}, f32[64,512]{1,0:T(8,128)S(1)}, u32[]{:S(2)}, u32[]{:S(2)}) collective-permute-start(f32[64,512]{1,0:T(8,128)S(1)} %get-tuple-element.75), channel_id=1, source_target_pairs={{0,192},{64,0},{128,64},{192,128},{1,193},{65,1},{129,65},{193,129... | collective-permute-start | bytes 393224 | tf_op jit(solution)/shard_map/ppermute | solution.py:21
  83.1 0.0 collective-permute-done.15.refs_1_
  83.1 0.4 collective-permute-done.16.refs_2_
  83.5 0.4 collective-permute-done.17.refs_3_
  83.9 1.7 %collective-permute-done.21.refs_7_ = f32[64,512]{1,0:T(8,128)S(1)} collective-permute-done((f32[64,512]{1,0:T(8,128)S(1)}, f32[64,512]{1,0:T(8,128)S(1)}, u32[]{:S(2)}, u32[]{:S(2)}) %collective-permute-start.21) | collective-permute-done | bytes 131104 | tf_op jit(solution)/shard_map/ppermute | solution.py:21
  85.6 1.0 pack.1
  86.6 5.6 %collective-permute-start.24 = (f32[8,8960]{1,0:T(8,128)S(1)}, f32[8,8960]{1,0:T(8,128)S(1)}, u32[]{:S(2)}, u32[]{:S(2)}) collective-permute-start(f32[8,8960]{1,0:T(8,128)S(1)} %get-tuple-element.68), channel_id=1, source_target_pairs={{0,56},{8,0},{16,8},{24,16},{32,24},{40,32},{48,40},{56,48},{1,57}... | collective-permute-start | bytes 860168 | tf_op jit(solution)/shard_map/ppermute | solution.py:21
  92.3 3.6 %collective-permute-done.24 = f32[8,8960]{1,0:T(8,128)S(1)} collective-permute-done((f32[8,8960]{1,0:T(8,128)S(1)}, f32[8,8960]{1,0:T(8,128)S(1)}, u32[]{:S(2)}, u32[]{:S(2)}) %collective-permute-start.24) | collective-permute-done | bytes 286752 | tf_op jit(solution)/shard_map/ppermute | solution.py:21
  95.9 3.1 %collective-permute-done.23 = f32[8,8960]{1,0:T(8,128)S(1)} collective-permute-done((f32[8,8960]{1,0:T(8,128)S(1)}, f32[8,8960]{1,0:T(8,128)S(1)}, u32[]{:S(2)}, u32[]{:S(2)}) %collective-permute-start.23) | collective-permute-done | bytes 286752 | tf_op jit(solution)/shard_map/ppermute | solution.py:21
  99.0 0.1 collective-permute-start.25
  99.2 4.5 %collective-permute-start.26 = (f32[8,3584]{1,0:T(8,128)S(1)}, f32[8,3584]{1,0:T(8,128)S(1)}, u32[]{:S(2)}, u32[]{:S(2)}) collective-permute-start(f32[8,3584]{1,0:T(8,128)S(1)} %pad_maximum_fusion.1), channel_id=1, source_target_pairs={{0,40},{8,48},{16,56},{24,0},{32,8},{40,16},{48,24},{56,32},{1,41}... | collective-permute-start | bytes 344072 | tf_op jit(solution)/shard_map/ppermute | solution.py:21
  103.7 3.2 %collective-permute-done.25 = f32[8,3584]{1,0:T(8,128)S(1)} collective-permute-done((f32[8,3584]{1,0:T(8,128)S(1)}, f32[8,3584]{1,0:T(8,128)S(1)}, u32[]{:S(2)}, u32[]{:S(2)}) %collective-permute-start.25) | collective-permute-done | bytes 114720 | tf_op jit(solution)/shard_map/ppermute | solution.py:21
  107.0 0.6 spread_kernel.1
  107.6 21.1 %all_to_all.5.pieces = f32[32,8,128]{2,1,0:T(8,128)S(1)} all-to-all(f32[32,8,128]{2,1,0:T(8,128)S(1)} %spread_kernel.1), channel_id=1, replica_groups=mesh['row'=4,'z'=8,'core'=2,'aux'=4] {'row','core','aux'}, dimensions={0} | all-to-all | bytes 262144 | tf_op jit(solution)/shard_map/all_to_all | solution.py:331
  128.8 1.4 %finish_kernel.1 = f32[8,2048]{1,0:T(8,128)} custom-call(s32[4]{0:T(128)S(1)} %pad_add_fusion.place, f32[8,3584]{1,0:T(8,128)S(1)} %fusion.1.rows, f32[32,8,128]{2,1,0:T(8,128)S(1)} %all_to_all.5.pieces), custom_call_target="tpu_custom_call" | custom-call | flops 1 | bytes 1 | tf_op jit(solution)/shard_map/finish_kernel/pallas_call | solution.py:174
  (24 shorter events, 0.3 us)
Async XLA Ops:
  0.0 7.4 %copy-start.1 = (s32[64,16]{0,1:T(8,128)S(1)}, s32[64,16]{0,1:T(8,128)}, u32[]{:S(2)}) copy-start(s32[64,16]{0,1:T(8,128)} %param.3) | copy-start | bytes 12292
  3.8 25.2 %collective-permute-start = (bf16[4,512,256]{2,1,0:T(8,128)(2,1)}, bf16[4,512,256]{2,1,0:T(8,128)(2,1)S(1)}, u32[]{:S(2)}, u32[]{:S(2)}) collective-permute-start(bf16[4,512,256]{2,1,0:T(8,128)(2,1)} %get-tuple-element.38), channel_id=1, source_target_pairs={{0,64},{64,128},{128,192},{192,0},{1,65},{65,129},{129,193},{193,1... | collective-permute-start | bytes 3145736 | tf_op jit(solution)/shard_map/ppermute | solution.py:21
  5.9 23.5 %collective-permute-start.1 = (bf16[4,512,256]{2,1,0:T(8,128)(2,1)S(1)}, bf16[4,512,256]{2,1,0:T(8,128)(2,1)S(1)}, u32[]{:S(2)}, u32[]{:S(2)}) collective-permute-start(bf16[4,512,256]{2,1,0:T(8,128)(2,1)S(1)} %get-tuple-element.39), channel_id=1, source_target_pairs={{0,192},{64,0},{128,64},{192,128},{1,193},{65,1},{129,65},{193,129... | collective-permute-start | bytes 3145736 | tf_op jit(solution)/shard_map/ppermute | solution.py:21
  7.5 2.2 %copy-start = (bf16[16,512,256]{2,1,0:T(8,128)(2,1)S(1)}, bf16[16,512,256]{2,1,0:T(8,128)(2,1)}, u32[]{:S(2)}) copy-start(bf16[16,512,256]{2,1,0:T(8,128)(2,1)} %slab) | copy-start | bytes 12582916
  14.4 4.5 %collective-permute-start.2 = (f32[256,512]{1,0:T(8,128)S(1)}, f32[256,512]{1,0:T(8,128)S(1)}, u32[]{:S(2)}, u32[]{:S(2)}) collective-permute-start(f32[256,512]{1,0:T(8,128)S(1)} %get-tuple-element.42), channel_id=1, source_target_pairs={{0,4},{4,0},{1,5},{5,1},{2,6},{6,2},{3,7},{7,3},{8,12},{12,8},{9,1... | collective-permute-start | bytes 1572872 | tf_op jit(solution)/shard_map/ppermute | solution.py:25
  19.6 6.3 %collective-permute-start.3 = (f32[64,512]{1,0:T(8,128)S(1)}, f32[64,512]{1,0:T(8,128)S(1)}, u32[]{:S(2)}, u32[]{:S(2)}) collective-permute-start(f32[64,512]{1,0:T(8,128)S(1)} %get-tuple-element.44), channel_id=1, source_target_pairs={{0,2},{1,3},{2,0},{3,1},{4,6},{5,7},{6,4},{7,5},{8,10},{9,11},{10,... | collective-permute-start | bytes 393224 | tf_op jit(solution)/shard_map/ppermute | solution.py:21
  20.7 7.2 %collective-permute-start.4 = (f32[64,512]{1,0:T(8,128)S(1)}, f32[64,512]{1,0:T(8,128)S(1)}, u32[]{:S(2)}, u32[]{:S(2)}) collective-permute-start(f32[64,512]{1,0:T(8,128)S(1)} %get-tuple-element.45), channel_id=1, source_target_pairs={{0,3},{1,0},{2,1},{3,2},{4,7},{5,4},{6,5},{7,6},{8,11},{9,8},{10,9... | collective-permute-start | bytes 393224 | tf_op jit(solution)/shard_map/ppermute | solution.py:21
  21.5 7.4 %collective-permute-start.5 = (f32[64,512]{1,0:T(8,128)S(1)}, f32[64,512]{1,0:T(8,128)S(1)}, u32[]{:S(2)}, u32[]{:S(2)}) collective-permute-start(f32[64,512]{1,0:T(8,128)S(1)} %get-tuple-element.46), channel_id=1, source_target_pairs={{0,1},{1,2},{2,3},{3,0},{4,5},{5,6},{6,7},{7,4},{8,9},{9,10},{10,1... | collective-permute-start | bytes 393224 | tf_op jit(solution)/shard_map/ppermute | solution.py:21
  25.9 8.2 %collective-permute-start.6 = (bf16[4,512,256]{2,1,0:T(8,128)(2,1)S(1)}, bf16[4,512,256]{2,1,0:T(8,128)(2,1)S(1)}, u32[]{:S(2)}, u32[]{:S(2)}) collective-permute-start(bf16[4,512,256]{2,1,0:T(8,128)(2,1)S(1)} %get-tuple-element.71), channel_id=1, source_target_pairs={{0,4},{4,0},{1,5},{5,1},{2,6},{6,2},{3,7},{7,3},{8,12},{12,8},{9,1... | collective-permute-start | bytes 3145736 | tf_op jit(solution)/shard_map/ppermute | solution.py:25
  29.5 4.7 %collective-permute-start.7 = (bf16[4,512,256]{2,1,0:T(8,128)(2,1)S(1)}, bf16[4,512,256]{2,1,0:T(8,128)(2,1)S(1)}, u32[]{:S(2)}, u32[]{:S(2)}) collective-permute-start(bf16[4,512,256]{2,1,0:T(8,128)(2,1)S(1)} %collective-permute-done.1), channel_id=1, source_target_pairs={{0,4},{4,0},{1,5},{5,1},{2,6},{6,2},{3,7},{7,3},{8,12},{12,8},{9,1... | collective-permute-start | bytes 3145736 | tf_op jit(solution)/shard_map/ppermute | solution.py:25
  31.7 3.8 %collective-permute-start.8 = (bf16[4,512,256]{2,1,0:T(8,128)(2,1)S(1)}, bf16[4,512,256]{2,1,0:T(8,128)(2,1)S(1)}, u32[]{:S(2)}, u32[]{:S(2)}) collective-permute-start(bf16[4,512,256]{2,1,0:T(8,128)(2,1)S(1)} %collective-permute-done), channel_id=1, source_target_pairs={{0,4},{4,0},{1,5},{5,1},{2,6},{6,2},{3,7},{7,3},{8,12},{12,8},{9,1... | collective-permute-start | bytes 3145736 | tf_op jit(solution)/shard_map/ppermute | solution.py:25
  31.7 25.7 %collective-permute-start.13 = (bf16[4,512,256]{2,1,0:T(8,128)(2,1)S(1)}, bf16[4,512,256]{2,1,0:T(8,128)(2,1)S(1)}, u32[]{:S(2)}, u32[]{:S(2)}) collective-permute-start(bf16[4,512,256]{2,1,0:T(8,128)(2,1)S(1)} %get-tuple-element.57), channel_id=1, source_target_pairs={{0,128},{64,192},{128,0},{192,64},{1,129},{65,193},{129,1},{193,65... | collective-permute-start | bytes 3145736 | tf_op jit(solution)/shard_map/ppermute | solution.py:21
  38.3 20.5 %collective-permute-start.10 = (f32[64,1536]{1,0:T(8,128)S(1)}, f32[64,1536]{1,0:T(8,128)S(1)}, u32[]{:S(2)}, u32[]{:S(2)}) collective-permute-start(f32[64,1536]{1,0:T(8,128)S(1)} %get-tuple-element.55), channel_id=1, source_target_pairs={{0,3},{1,0},{2,1},{3,2},{4,7},{5,4},{6,5},{7,6},{8,11},{9,8},{10,9... | collective-permute-start | bytes 1179656 | tf_op jit(solution)/shard_map/ppermute | solution.py:21
  40.9 17.9 %collective-permute-start.11 = (f32[64,1536]{1,0:T(8,128)S(1)}, f32[64,1536]{1,0:T(8,128)S(1)}, u32[]{:S(2)}, u32[]{:S(2)}) collective-permute-start(f32[64,1536]{1,0:T(8,128)S(1)} %get-tuple-element.56), channel_id=1, source_target_pairs={{0,1},{1,2},{2,3},{3,0},{4,5},{5,6},{6,7},{7,4},{8,9},{9,10},{10,1... | collective-permute-start | bytes 1179656 | tf_op jit(solution)/shard_map/ppermute | solution.py:21
  40.9 18.7 %collective-permute-start.9 = (f32[64,1536]{1,0:T(8,128)S(1)}, f32[64,1536]{1,0:T(8,128)S(1)}, u32[]{:S(2)}, u32[]{:S(2)}) collective-permute-start(f32[64,1536]{1,0:T(8,128)S(1)} %get-tuple-element.54), channel_id=1, source_target_pairs={{0,2},{1,3},{2,0},{3,1},{4,6},{5,7},{6,4},{7,5},{8,10},{9,11},{10,... | collective-permute-start | bytes 1179656 | tf_op jit(solution)/shard_map/ppermute | solution.py:21
  57.4 3.8 %collective-permute-start.14 = (bf16[4,512,256]{2,1,0:T(8,128)(2,1)S(1)}, bf16[4,512,256]{2,1,0:T(8,128)(2,1)S(1)}, u32[]{:S(2)}, u32[]{:S(2)}) collective-permute-start(bf16[4,512,256]{2,1,0:T(8,128)(2,1)S(1)} %collective-permute-done.13), channel_id=1, source_target_pairs={{0,4},{4,0},{1,5},{5,1},{2,6},{6,2},{3,7},{7,3},{8,12},{12,8},{9,1... | collective-permute-start | bytes 3145736 | tf_op jit(solution)/shard_map/ppermute | solution.py:25
  63.2 8.0 %collective-permute-start.18 = (f32[128,512]{1,0:T(8,128)S(1)}, f32[128,512]{1,0:T(8,128)S(1)}, u32[]{:S(2)}, u32[]{:S(2)}) collective-permute-start(f32[128,512]{1,0:T(8,128)S(1)} %get-tuple-element.63), channel_id=1, source_target_pairs={{0,2},{1,3},{2,0},{3,1},{4,6},{5,7},{6,4},{7,5},{8,10},{9,11},{10,... | collective-permute-start | bytes 786440 | tf_op jit(solution)/shard_map/ppermute | solution.py:21
  65.8 12.0 %collective-permute-start.19 = (f32[128,512]{1,0:T(8,128)S(1)}, f32[128,512]{1,0:T(8,128)S(1)}, u32[]{:S(2)}, u32[]{:S(2)}) collective-permute-start(f32[128,512]{1,0:T(8,128)S(1)} %get-tuple-element.64), channel_id=1, source_target_pairs={{0,3},{1,0},{2,1},{3,2},{4,7},{5,4},{6,5},{7,6},{8,11},{9,8},{10,9... | collective-permute-start | bytes 786440 | tf_op jit(solution)/shard_map/ppermute | solution.py:21
  66.7 13.6 %collective-permute-start.20 = (f32[128,512]{1,0:T(8,128)S(1)}, f32[128,512]{1,0:T(8,128)S(1)}, u32[]{:S(2)}, u32[]{:S(2)}) collective-permute-start(f32[128,512]{1,0:T(8,128)S(1)} %get-tuple-element.65), channel_id=1, source_target_pairs={{0,1},{1,2},{2,3},{3,0},{4,5},{5,6},{6,7},{7,4},{8,9},{9,10},{10,1... | collective-permute-start | bytes 786440 | tf_op jit(solution)/shard_map/ppermute | solution.py:21
  67.3 14.3 %collective-permute-start.12 = (f32[64,512]{1,0:T(8,128)S(1)}, f32[64,512]{1,0:T(8,128)S(1)}, u32[]{:S(2)}, u32[]{:S(2)}) collective-permute-start(f32[64,512]{1,0:T(8,128)S(1)} %slice.52), channel_id=1, source_target_pairs={{0,64},{64,128},{128,192},{192,0},{1,65},{65,129},{129,193},{193,1... | collective-permute-start | bytes 393224 | tf_op jit(solution)/shard_map/ppermute | solution.py:21
  68.5 14.7 %collective-permute-start.15 = (f32[64,512]{1,0:T(8,128)S(1)}, f32[64,512]{1,0:T(8,128)S(1)}, u32[]{:S(2)}, u32[]{:S(2)}) collective-permute-start(f32[64,512]{1,0:T(8,128)S(1)} %get-tuple-element.59), channel_id=1, source_target_pairs={{0,2},{1,3},{2,0},{3,1},{4,6},{5,7},{6,4},{7,5},{8,10},{9,11},{10,... | collective-permute-start | bytes 393224 | tf_op jit(solution)/shard_map/ppermute | solution.py:21
  71.2 12.3 %collective-permute-start.16 = (f32[64,512]{1,0:T(8,128)S(1)}, f32[64,512]{1,0:T(8,128)S(1)}, u32[]{:S(2)}, u32[]{:S(2)}) collective-permute-start(f32[64,512]{1,0:T(8,128)S(1)} %get-tuple-element.60), channel_id=1, source_target_pairs={{0,3},{1,0},{2,1},{3,2},{4,7},{5,4},{6,5},{7,6},{8,11},{9,8},{10,9... | collective-permute-start | bytes 393224 | tf_op jit(solution)/shard_map/ppermute | solution.py:21
  77.8 6.1 %collective-permute-start.17 = (f32[64,512]{1,0:T(8,128)S(1)}, f32[64,512]{1,0:T(8,128)S(1)}, u32[]{:S(2)}, u32[]{:S(2)}) collective-permute-start(f32[64,512]{1,0:T(8,128)S(1)} %get-tuple-element.61), channel_id=1, source_target_pairs={{0,1},{1,2},{2,3},{3,0},{4,5},{5,6},{6,7},{7,4},{8,9},{9,10},{10,1... | collective-permute-start | bytes 393224 | tf_op jit(solution)/shard_map/ppermute | solution.py:21
  80.4 5.3 %collective-permute-start.21 = (f32[64,512]{1,0:T(8,128)S(1)}, f32[64,512]{1,0:T(8,128)S(1)}, u32[]{:S(2)}, u32[]{:S(2)}) collective-permute-start(f32[64,512]{1,0:T(8,128)S(1)} %get-tuple-element.76), channel_id=1, source_target_pairs={{0,64},{64,128},{128,192},{192,0},{1,65},{65,129},{129,193},{193,1... | collective-permute-start | bytes 393224 | tf_op jit(solution)/shard_map/ppermute | solution.py:21
  81.6 4.1 %collective-permute-start.22 = (f32[64,512]{1,0:T(8,128)S(1)}, f32[64,512]{1,0:T(8,128)S(1)}, u32[]{:S(2)}, u32[]{:S(2)}) collective-permute-start(f32[64,512]{1,0:T(8,128)S(1)} %get-tuple-element.75), channel_id=1, source_target_pairs={{0,192},{64,0},{128,64},{192,128},{1,193},{65,1},{129,65},{193,129... | collective-permute-start | bytes 393224 | tf_op jit(solution)/shard_map/ppermute | solution.py:21
  86.6 9.2 %collective-permute-start.24 = (f32[8,8960]{1,0:T(8,128)S(1)}, f32[8,8960]{1,0:T(8,128)S(1)}, u32[]{:S(2)}, u32[]{:S(2)}) collective-permute-start(f32[8,8960]{1,0:T(8,128)S(1)} %get-tuple-element.68), channel_id=1, source_target_pairs={{0,56},{8,0},{16,8},{24,16},{32,24},{40,32},{48,40},{56,48},{1,57}... | collective-permute-start | bytes 860168 | tf_op jit(solution)/shard_map/ppermute | solution.py:21
  92.3 6.7 %collective-permute-start.23 = (f32[8,8960]{1,0:T(8,128)S(1)}, f32[8,8960]{1,0:T(8,128)S(1)}, u32[]{:S(2)}, u32[]{:S(2)}) collective-permute-start(f32[8,8960]{1,0:T(8,128)S(1)} %get-tuple-element.67), channel_id=1, source_target_pairs={{0,8},{8,16},{16,24},{24,32},{32,40},{40,48},{48,56},{56,0},{1,9},... | collective-permute-start | bytes 860168 | tf_op jit(solution)/shard_map/ppermute | solution.py:21
  99.0 7.9 %collective-permute-start.25 = (f32[8,3584]{1,0:T(8,128)S(1)}, f32[8,3584]{1,0:T(8,128)S(1)}, u32[]{:S(2)}, u32[]{:S(2)}) collective-permute-start(f32[8,3584]{1,0:T(8,128)S(1)} %pad_maximum_fusion), channel_id=1, source_target_pairs={{0,24},{8,32},{16,40},{24,48},{32,56},{40,0},{48,8},{56,16},{1,25}... | collective-permute-start | bytes 344072 | tf_op jit(solution)/shard_map/ppermute | solution.py:21
  99.2 7.8 %collective-permute-start.26 = (f32[8,3584]{1,0:T(8,128)S(1)}, f32[8,3584]{1,0:T(8,128)S(1)}, u32[]{:S(2)}, u32[]{:S(2)}) collective-permute-start(f32[8,3584]{1,0:T(8,128)S(1)} %pad_maximum_fusion.1), channel_id=1, source_target_pairs={{0,40},{8,48},{16,56},{24,0},{32,8},{40,16},{48,24},{56,32},{1,41}... | collective-permute-start | bytes 344072 | tf_op jit(solution)/shard_map/ppermute | solution.py:21
